TPU v7x, 512 devices: a whole 4x8x8 slice. The times are simulated.
512 devices in a mesh: members: 8 (over y), bands: 64 (over z, x, core).
Axes of the slice: x: 4, y: 8, z: 8, core: 2. Of those that a mesh axis runs over, the one named last changes fastest.
Arguments:
- ensemble: float32 [128, 1024, 128], P('members', 'bands'), may hold values from -6 to 6
- neighbours: int32 [1024, 4], P('bands'), may hold values from 0 to 1023, as said below
- regime: int32 [1024], P('bands'), may hold values from 0 to 3
- norm_gain: float32 [128], replicated, may hold values from 0.25 to 1.75
- up_weight: bfloat16 [4, 128, 512], replicated, may hold values from -0.5 to 0.5
- down_weight: bfloat16 [4, 512, 128], replicated, may hold values from -0.25 to 0.25
- vertical_modes: float32 [4, 128], replicated, may hold values from -3 to 3
- obs_col: int32 [16384], P('bands'), may hold values from 0 to 1023, as said below
- obs_lev: int32 [16384], P('bands'), may hold values from 0 to 127
- obs_val: float32 [16384], P('bands'), may hold values from -9 to 9
- obs_err: float32 [16384], P('bands'), may hold values from 0.3 to 1
Outputs:
- analysis: float32 [128, 1024, 128], P('members', 'bands')
Inputs may be any that keep to these rules, and one draw needn't show every extreme that they name: `neighbours`: every neighbour of column c lies within 8 columns of c. `obs_col`: the observations at positions b * 256 to (b + 1) * 256 - 1 lie in columns b * 16 to (b + 1) * 16 - 1.
All inputs are finite; a program needn't handle non-finite values.
Results may differ from a plain program's by a relative error of at most 0.0034.
Values sent between devices are 32-bit elements; how exact they have to be, the bound alone decides.
No kernel may reach another device: no remote copies, remote signals or barrier semaphores. Data moves between devices by JAX's collectives and lax.ppermute only.
A program may use at most 64 MiB of HBM per device.

v0:
```python
import math

import jax
import jax.numpy as jnp
from jax import lax
from jax.sharding import PartitionSpec as P

E = 4
L = 4
NB = 4
HALO = 8
NS_ITERS = 4


highest = lax.Precision.HIGHEST


def extended(block, sides, width):
    for axis, dim in sides:
        count = lax.axis_size(axis)
        forward = [(i, i + 1) for i in range(count - 1)]
        backward = [(target, source) for source, target in forward]
        low = lax.ppermute(
            lax.slice_in_dim(block, block.shape[dim] - width, None, axis=dim), axis, forward
        )
        high = lax.ppermute(lax.slice_in_dim(block, 0, width, axis=dim), axis, backward)
        block = jnp.concatenate([low, block, high], axis=dim)
    return block


def analysis_coefficients(gram_matrix, cross_terms, drive_terms):
    order_k = gram_matrix.shape[0]
    identity = jnp.eye(order_k, dtype=jnp.float32)
    system = identity + gram_matrix
    norm_scale = jnp.sqrt(jnp.sum(system * system))
    iterate = system / norm_scale
    inverse = identity
    for sweep_index in range(NS_ITERS):
        if sweep_index == 0:
            product = iterate
        else:
            product = jnp.dot(inverse, iterate, precision=highest)
        factor = 1.5 * identity - 0.5 * product
        if sweep_index + 1 < NS_ITERS:
            iterate = jnp.dot(iterate, factor, precision=highest)
        if sweep_index == 0:
            inverse = factor
        else:
            inverse = jnp.dot(factor, inverse, precision=highest)
    root_factor = inverse / jnp.sqrt(norm_scale)
    weights_matrix = jnp.dot(root_factor, root_factor, precision=highest)
    mean_weights = jnp.dot(weights_matrix, drive_terms, precision=highest)
    return mean_weights[:, None] - 0.5 * jnp.dot(weights_matrix, cross_terms, precision=highest)


def per_device(
    ensemble,
    neighbours,
    regime,
    norm_gain,
    up_weight,
    down_weight,
    vertical_modes,
    obs_col,
    obs_lev,
    obs_val,
    obs_err,
):
    member_deviation, column_deviation, level_count = ensemble.shape
    band_index = lax.axis_index("bands")
    group_index = lax.axis_index("members")
    widened = extended(ensemble, (("bands", 1),), HALO)
    local_nb = neighbours - band_index * column_deviation + HALO
    summed_nb = jnp.zeros_like(ensemble)
    for which in range(NB):
        summed_nb = summed_nb + widened[:, local_nb[:, which], :]
    filtered_profile = ensemble + 0.5 * (0.25 * summed_nb - ensemble)
    flat = filtered_profile.reshape(member_deviation * column_deviation, level_count)
    inv_rms = lax.rsqrt(jnp.mean(flat * flat, axis=1, keepdims=True) + 1e-05)
    normed = (flat * inv_rms * norm_gain).astype(jnp.bfloat16)
    hidden = jax.nn.silu(
        jnp.einsum("rl,elf->erf", normed, up_weight, preferred_element_type=jnp.float32)
    ).astype(jnp.bfloat16)
    expert_out = jnp.einsum("erf,efl->erl", hidden, down_weight, preferred_element_type=jnp.float32)
    selected = regime[None, :] == jnp.arange(E, dtype=jnp.int32)[:, None]
    selected = jnp.tile(selected, (1, member_deviation))
    time_derivative = jnp.sum(jnp.where(selected[:, :, None], expert_out, 0.0), axis=0)
    predicted_vector = filtered_profile + time_derivative.reshape(
        member_deviation, column_deviation, level_count
    )
    vertical_lattice = lax.all_to_all(
        predicted_vector, "members", split_axis=1, concat_axis=0, tiled=True
    )
    share_cols = vertical_lattice.shape[1]
    average_sample_vector = jnp.mean(vertical_lattice, axis=0)
    sample_anomaly = vertical_lattice - average_sample_vector
    local_col = obs_col - band_index * column_deviation - group_index * share_cols
    inside = (local_col >= 0) & (local_col < share_cols)
    clipped = jnp.clip(local_col, 0, share_cols - 1)
    sampled = sample_anomaly[:, clipped, obs_lev]
    obs_pert = jnp.where(inside[None, :], sampled / obs_err, 0.0).T
    innovation = jnp.where(
        inside, (obs_val - average_sample_vector[clipped, obs_lev]) / obs_err, 0.0
    )
    members_all = obs_pert.shape[1]
    order_k = L * members_all
    obs_rows = obs_pert.shape[0]
    modulated = (vertical_modes[:, obs_lev].T[:, :, None] * obs_pert[:, None, :]).reshape(
        obs_rows, order_k
    ) / math.sqrt(order_k - 1)
    cross_part = jnp.dot(modulated.T, obs_pert, precision=highest)
    drive_part = jnp.dot(modulated.T, innovation, precision=highest)
    gram_part = jnp.dot(modulated.T, modulated, precision=highest)
    gram_matrix, cross_terms, drive_terms = lax.psum(
        (gram_part, cross_part, drive_part), ("members", "bands")
    )
    coefficients = analysis_coefficients(gram_matrix, cross_terms, drive_terms)
    coeff_modes = coefficients.reshape(L, members_all, members_all)
    update_correction = jnp.zeros_like(vertical_lattice)
    for layer in range(L):
        mixed = jnp.einsum("acv,ab->bcv", sample_anomaly, coeff_modes[layer], precision=highest)
        update_correction = update_correction + vertical_modes[layer][None, None, :] * mixed
    analysed = vertical_lattice + update_correction / math.sqrt(order_k - 1)
    return lax.all_to_all(analysed, "members", split_axis=0, concat_axis=1, tiled=True)


def solution(mesh):
    in_specs = (
        P("members", "bands", None),
        P("bands", None),
        P("bands"),
        P(),
        P(),
        P(),
        P(),
        P("bands"),
        P("bands"),
        P("bands"),
        P("bands"),
    )
    out_specs = P("members", "bands", None)
    return jax.shard_map(
        per_device, mesh=mesh, in_specs=in_specs, out_specs=out_specs, check_vma=False
    )
```

profile of v0, /device:TPU:1, one launch (start us, length us, event | category | flops | bytes accessed | tf_op | source)
XLA Modules:
  0.0 368.0 jit_solution(5785162211855150360)
XLA Ops:
  7.5 4.6 %collective-permute-start = (f32[16,8,128]{2,0,1:T(8,128)S(1)}, f32[16,8,128]{2,0,1:T(8,128)S(1)}, u32[]{:S(2)}, u32[]{:S(2)}) collective-permute-start(f32[16,8,128]{2,0,1:T(8,128)S(1)} %copy.107), channel_id=1, source_target_pairs={{0,1},{1,2},{2,3},{3,4},{4,5},{5,6},{6,7},{7,8},{8,9},{9,10},{10,1... | collective-permute-start | bytes 196616 | tf_op jit(solution)/shard_map/ppermute | solution.py:23
  12.2 5.6 %collective-permute-start.1 = (f32[16,8,128]{2,0,1:T(8,128)S(1)}, f32[16,8,128]{2,0,1:T(8,128)S(1)}, u32[]{:S(2)}, u32[]{:S(2)}) collective-permute-start(f32[16,8,128]{2,0,1:T(8,128)S(1)} %copy.108), channel_id=1, source_target_pairs={{1,0},{2,1},{3,2},{4,3},{5,4},{6,5},{7,6},{8,7},{9,8},{10,9},{11,1... | collective-permute-start | bytes 196616 | tf_op jit(solution)/shard_map/ppermute | solution.py:26
  23.9 1.0 fusion.6
  25.6 3.5 all-to-all-start
  30.0 8.1 %all-to-all-done = f32[16,16,128]{2,0,1:T(8,128)S(1)} async-done(((f32[16,16,128]{2,0,1:T(8,128)}), f32[16,16,128]{2,0,1:T(8,128)S(1)}, u32[]{:S(2)}, u32[]{:S(2)}) %all-to-all-start) | async-done | bytes 131104 | tf_op jit(solution)/shard_map/all_to_all | solution.py:91
  38.2 2.4 gather_fusion.6
  40.7 1.9 gather_fusion.5
  43.2 1.7 fusion.17
  44.9 2.1 fusion.19
  48.0 105.4 %psum.22 = f32[512]{0:T(512)S(1)} all-reduce(f32[512]{0:T(512)S(1)} %bitcast.136), channel_id=1, replica_groups=mesh['members'=8,'bands'=64] {'members','bands'}, use_global_device_ids=true, to_apply=%region_5.6 | all-reduce | flops 512 | bytes 4096 | tf_op jit(solution)/shard_map/psum | solution.py:114
  153.4 168.5 %all-reduce.3.cloned.1.call-done = (f32[512,512]{1,0:T(8,128)}, f32[512,128]{1,0:T(8,128)}) async-done(((f32[512,512]{1,0:T(8,128)}, f32[512,128]{1,0:T(8,128)}), (f32[512,512]{1,0:T(8,128)}, f32[512,128]{1,0:T(8,128)})) %all-reduce.3.cloned.1.call-update) | async-done | bytes 1310736 | tf_op jit(solution)/shard_map/psum | solution.py:114
  322.0 2.2 multiply_reduce_fusion
  324.9 2.0 fusion.14
  326.9 2.0 select_subtract_fusion.2
  328.9 2.0 fusion.13
  330.9 1.8 fusion.63
  332.7 1.9 select_subtract_fusion.1
  334.6 1.8 fusion.64
  336.4 2.1 fusion.65
  338.5 1.8 select_subtract_fusion
  340.4 1.8 convolution_divide_fusion
  342.2 1.8 fusion.66
  345.1 1.0 fusion.7
  347.5 13.0 %all_to_all.36 = f32[128,2,128]{2,1,0:T(2,128)S(1)} all-to-all(f32[128,2,128]{2,1,0:T(2,128)S(1)} %copy.79), channel_id=1, replica_groups=mesh['members'=8,'bands'=64] {'members'}, dimensions={0} | all-to-all | bytes 262144 | tf_op jit(solution)/shard_map/all_to_all | solution.py:124
  (72 shorter events, 13.2 us)
Async XLA Ops:
  6.5 17.3 %copy-start = (bf16[4,512,128]{2,1,0:T(8,128)(2,1)S(1)}, bf16[4,512,128]{2,1,0:T(8,128)(2,1)}, u32[]{:S(2)}) copy-start(bf16[4,512,128]{2,1,0:T(8,128)(2,1)} %param.16) | copy-start | bytes 1572868
  7.5 15.9 %copy-start.1 = (f32[16,16,128]{2,1,0:T(8,128)S(1)}, f32[16,16,128]{2,1,0:T(8,128)}, u32[]{:S(2)}) copy-start(f32[16,16,128]{2,1,0:T(8,128)} %param.11) | copy-start | bytes 393220
  7.5 12.5 %collective-permute-start = (f32[16,8,128]{2,0,1:T(8,128)S(1)}, f32[16,8,128]{2,0,1:T(8,128)S(1)}, u32[]{:S(2)}, u32[]{:S(2)}) collective-permute-start(f32[16,8,128]{2,0,1:T(8,128)S(1)} %copy.107), channel_id=1, source_target_pairs={{0,1},{1,2},{2,3},{3,4},{4,5},{5,6},{6,7},{7,8},{8,9},{9,10},{10,1... | collective-permute-start | bytes 196616 | tf_op jit(solution)/shard_map/ppermute | solution.py:23
  12.2 8.8 %collective-permute-start.1 = (f32[16,8,128]{2,0,1:T(8,128)S(1)}, f32[16,8,128]{2,0,1:T(8,128)S(1)}, u32[]{:S(2)}, u32[]{:S(2)}) collective-permute-start(f32[16,8,128]{2,0,1:T(8,128)S(1)} %copy.108), channel_id=1, source_target_pairs={{1,0},{2,1},{3,2},{4,3},{5,4},{6,5},{7,6},{8,7},{9,8},{10,9},{11,1... | collective-permute-start | bytes 196616 | tf_op jit(solution)/shard_map/ppermute | solution.py:26
  21.0 2.7 copy-start.9
  21.6 2.2 copy-start.10
  23.9 5.3 %copy-start.6 = (s32[256]{0:T(256)S(1)}, s32[256]{0:T(256)}, u32[]{:S(2)}) copy-start(s32[256]{0:T(256)} %param.18) | copy-start | bytes 3076
  23.9 5.3 %copy-start.7 = (s32[256]{0:T(256)S(1)}, s32[256]{0:T(256)}, u32[]{:S(2)}) copy-start(s32[256]{0:T(256)} %param.19) | copy-start | bytes 3076
  25.6 12.5 %all-to-all-start = ((f32[16,16,128]{2,0,1:T(8,128)}), f32[16,16,128]{2,0,1:T(8,128)S(1)}, u32[]{:S(2)}, u32[]{:S(2)}) async-start(f32[16,16,128]{2,0,1:T(8,128)} %copy_add_fusion), calls=%async_computation | async-start | bytes 262144 | tf_op jit(solution)/shard_map/all_to_all | solution.py:91
  29.2 292.8 %all-reduce.3.cloned.1.call-start = ((), (), s32[]{:S(2)}) async-start(), calls=%async_computation.2 | async-start | bytes 2621440 | tf_op jit(solution)/shard_map/psum | solution.py:114
  40.6 2.1 copy-start.5
  40.6 2.1 copy-start.8
  46.9 0.7 copy-start.4
  322.0 2.9 copy-start.2
  344.1 1.0 copy-start.3
Sparse Core Ops, SparseCore 0:
  47.1 274.8 all-reduce.2
where the time goes:
time: 369 us; the launch traced here: 368 us
  waiting for transfers between devices  177 us (48%)
  blocking collectives  118 us (32%)
  matrix products  27.5 us (7%)
  between operations  14.6 us (4%)
  starting transfers between devices  13.8 us (4%)
  local copies, waits for them, and re-layouts  11.9 us (3%)
  other arithmetic  5.08 us (1%)
    psum x1, waiting for transfers between devices, per_device(): lax.psum((gram_part, cross_part, drive_part), ('members', 'bands'))  169 us
    psum x1, blocking collectives, per_device(): lax.psum((gram_part, cross_part, drive_part), ('members', 'bands'))  105 us
    all_to_all x1, blocking collectives, per_device(): lax.all_to_all(analysed, 'members', split_axis=0, concat_axis=1, tiled=True)  13 us
    all_to_all x1, waiting for transfers between devices, per_device(): lax.all_to_all(predicted_vector, 'members', split_axis=1, concat_axis=0,...  8.1 us
  transfers between devices with their start and end apart: 4, of which 2 were waited for; matrix products, arithmetic and copies ran while one was open for 1% of the time, Pallas kernels for 0%

commit v1 on v0

v1 whole, which is shorter than its diff:
```python
import functools
import math

import jax
import jax.numpy as jnp
from jax import lax
from jax.experimental import pallas as pl
from jax.experimental.pallas import tpu as pltpu
from jax.sharding import Mesh, PartitionSpec as P

E = 4
L = 4
NB = 4
HALO = 8
M = 128
LEV = 128
FF = 512
C = 16
MD = 16
OBS = 256
GROUPS = 8
PACKS = 7
PAIRS = [(a, b) for a in range(L) for b in range(a, L)]
ROOT = math.sqrt(L * M - 1)
BF = jnp.bfloat16
F32 = jnp.float32
VMEM_LIMIT = 48 * 1024 * 1024
BANDS = ("z", "x", "core")


def dot(a, b):
    return jnp.dot(a, b, preferred_element_type=F32)


def dot_nt(a, b):
    return lax.dot_general(a, b, (((1,), (1,)), ((), ())), preferred_element_type=F32)


def split2(a):
    high = a.astype(BF)
    return high, (a - high.astype(F32)).astype(BF)


def split3(a):
    high = a.astype(BF)
    rest = a - high.astype(F32)
    middle = rest.astype(BF)
    return high, middle, (rest - middle.astype(F32)).astype(BF)


def forecast_kernel(
    nb, regime, ens, low, high, gain, up, down, lev, col, err, modes,
    f_out, v_out, w_out, wide, regs,
):
    band = (lax.axis_index("z") * 4 + lax.axis_index("x")) * 2 + lax.axis_index("core")
    for c in range(C):
        wide[HALO + c] = ens[:, c, :]
        regs[c * MD:(c + 1) * MD, :] = jnp.full((MD, LEV), regime[c], jnp.int32)
    for c in range(HALO):
        wide[c] = low[:, c, :]
        wide[HALO + C + c] = high[:, c, :]
    start = band * C - HALO
    rows = []
    for c in range(C):
        total = wide[nb[c, 0] - start]
        for k in range(1, NB):
            total = total + wide[nb[c, k] - start]
        own = wide[HALO + c]
        rows.append(own + 0.5 * (0.25 * total - own))
    flat = jnp.concatenate(rows, axis=0)
    inv_rms = lax.rsqrt(jnp.mean(flat * flat, axis=1, keepdims=True) + 1e-05)
    normed = (flat * inv_rms * gain[...]).astype(BF)
    which = regs[...]
    which4 = jnp.concatenate([which] * (FF // LEV), axis=1)
    pre = dot(normed, up[0])
    for e in range(1, E):
        pre = jnp.where(which4 == e, dot(normed, up[e]), pre)
    hidden = pre / (1.0 + jnp.exp(-pre))
    out = flat
    tendency = None
    for e in range(E):
        part = dot(jnp.where(which4 == e, hidden, 0.0).astype(BF), down[e])
        tendency = part if tendency is None else tendency + part
    out = flat + tendency
    f_out[...] = out.reshape(C, MD, LEV)

    one_hot = (lax.broadcasted_iota(jnp.int32, (LEV, OBS), 0) == lev[...]).astype(F32).astype(BF)
    picked = None
    for part in split3(out):
        got = dot(part, one_hot)
        picked = got if picked is None else picked + got
    place = col[...] - band * C
    sampled = jnp.zeros((MD, OBS), F32)
    for c in range(C):
        sampled = sampled + jnp.where(place == c, picked[c * MD:(c + 1) * MD, :], 0.0)
    sampled = sampled / err[...]
    for g in range(GROUPS):
        v_out[g] = sampled
    at_obs = None
    for part in split3(modes[...]):
        got = dot(part, one_hot)
        at_obs = got if at_obs is None else at_obs + got
    w_out[...] = at_obs


def gram_kernel(values, at_obs, val, err, packed, centred):
    group = lax.axis_index("members")
    raw = values[...].reshape(M, OBS)
    mean = jnp.sum(raw, axis=0, keepdims=True) * (1.0 / M)
    pert = raw - mean
    again = jnp.sum(pert, axis=0, keepdims=True) * (1.0 / M)
    pert = pert - again
    centred[...] = pert
    innovation = val[...] / err[...] - (mean + again)
    own = centred[pl.ds(pl.multiple_of(group * MD, MD), MD), :]
    w = at_obs[...]
    weights = [w[a:a + 1] * w[b:b + 1] * (1.0 / (L * M - 1)) for a, b in PAIRS]
    weights += [w[a:a + 1] * (1.0 / ROOT) for a in range(L)]
    left = jnp.concatenate([own * f for f in weights], axis=0)
    right = jnp.concatenate(
        [pert, jnp.broadcast_to(innovation, (M, OBS))], axis=0
    )
    lh, ll = split2(left)
    rh, rl = split2(right)
    s = dot_nt(lh, rh) + (dot_nt(lh, rl) + dot_nt(ll, rh))
    row = lax.broadcasted_iota(jnp.int32, (MD, M), 0) + group * MD
    column = lax.broadcasted_iota(jnp.int32, (MD, M), 1)
    for t in range(PACKS):
        first = s[(2 * t) * MD:(2 * t + 1) * MD, :M]
        second = s[(2 * t + 1) * MD:(2 * t + 2) * MD, :M]
        if t < L:
            k = len(PAIRS) + t
            middle = s[k * MD:(k + 1) * MD, M:]
        else:
            middle = jnp.zeros((MD, M), F32)
        p = jnp.where(column > row, first, jnp.where(column < row, second, middle))
        for h in range(2):
            for x in range(4):
                packed[2 * x + h, t] = p[8 * h:8 * h + 8]


def analysis_kernel(
    mine, other, forecasts, own_forecast, modes, out,
    packed, crosses, zf, zh, zl, fh, fl,
):
    group = lax.axis_index("members")
    core = lax.axis_index("core")
    for g in range(GROUPS):
        for t in range(PACKS):
            at = pl.multiple_of(g * MD + core * 8, 8)
            packed[t, pl.ds(at, 8), :] = mine[g, t]
            at = pl.multiple_of(g * MD + 8 - core * 8, 8)
            packed[t, pl.ds(at, 8), :] = other[g, t]
    i = lax.broadcasted_iota(jnp.int32, (M, M), 0)
    j = lax.broadcasted_iota(jnp.int32, (M, M), 1)
    diagonal = i == j
    drives = []
    square = None
    for t in range(PACKS):
        p = packed[t]
        q = p.T
        if t < L:
            drives.append(jnp.sum(jnp.where(diagonal, p, 0.0), axis=0, keepdims=True))
        for side in range(2):
            keep = (i < j) if side == 0 else (i > j)
            s = jnp.where(diagonal, 0.0, jnp.where(keep, p, q))
            s = s - jnp.where(diagonal, jnp.sum(s, axis=0, keepdims=True), 0.0)
            k = 2 * t + side
            if k >= len(PAIRS):
                crosses[k - len(PAIRS)] = s
                continue
            a, b = PAIRS[k]
            if a == b:
                s = s + jnp.where(diagonal, 1.0, 0.0)
            zf[a * M:(a + 1) * M, b * M:(b + 1) * M] = s
            if a != b:
                zf[b * M:(b + 1) * M, a * M:(a + 1) * M] = s
            part = jnp.sum(s * s, axis=0, keepdims=True) * (1.0 if a == b else 2.0)
            square = part if square is None else square + part
    norm = jnp.sqrt(jnp.sum(square, axis=1, keepdims=True))
    inverse_norm = 1.0 / norm
    own_rows = pl.ds(pl.multiple_of(group * MD, MD), MD)
    v = jnp.concatenate(
        [drives[a] - 0.5 * crosses[a, own_rows, :] for a in range(L)], axis=1
    )
    z = zf[...] * inverse_norm
    size = L * M
    for step in range(3):
        high, low = split2(z)
        zf[...] = z
        zh[0:size] = high
        zl[0:size] = low
        vh, vl = split2(v)
        zh[size:size + MD] = vh
        zl[size:size + MD] = vl
        a, b = zh[0:size], zl[0:size]
        q = dot(a, a) + (dot(a, b) + dot(b, a))
        identity = (
            lax.broadcasted_iota(jnp.int32, (size, size), 0)
            == lax.broadcasted_iota(jnp.int32, (size, size), 1)
        )
        f = jnp.where(identity, 2.25, 0.0) - 1.5 * zf[...] + 0.25 * q
        high, low = split2(f)
        fh[...] = high
        fl[...] = low
        a, b = zh[...], zl[...]
        new = dot(a, fh[...]) + (dot(a, fl[...]) + dot(b, fh[...]))
        z = new[0:size]
        v = new[size:size + MD]
    high, low = split2(z)
    fh[...] = high
    fl[...] = low
    for step in range(2):
        vh, vl = split2(v)
        v = 1.5 * v - 0.5 * (dot(vh, fh[...]) + (dot(vh, fl[...]) + dot(vl, fh[...])))
    v = v * inverse_norm
    blocks = []
    for a in range(L):
        block = v[:, a * M:(a + 1) * M]
        blocks.append(block - jnp.mean(block, axis=1, keepdims=True))
    coeff = jnp.concatenate(blocks, axis=0)
    ch, cl = split2(coeff)
    both = jnp.concatenate([ch, cl], axis=0)
    scaled = modes[...] * (1.0 / ROOT)
    for c in range(0, C, 2):
        block = jnp.concatenate(
            [forecasts[:, c + k].reshape(M, LEV) for k in range(2)], axis=1
        )
        bh, bl = split2(block)
        r = dot(both, bh)
        r = r[:L * MD] + (r[L * MD:] + dot(ch, bl))
        for k in range(2):
            total = own_forecast[c + k]
            for a in range(L):
                total = total + scaled[a:a + 1] * r[a * MD:(a + 1) * MD, k * LEV:(k + 1) * LEV]
            out[:, c + k, :] = total


def call(kernel, outs, scratch, smem=0, total=0, name=None, flops=0):
    specs = [
        pl.BlockSpec(memory_space=pltpu.SMEM if n < smem else pltpu.VMEM)
        for n in range(total)
    ]
    return pl.pallas_call(
        kernel,
        out_shape=outs,
        in_specs=specs,
        out_specs=jax.tree.map(lambda _: pl.BlockSpec(memory_space=pltpu.VMEM), outs),
        scratch_shapes=scratch,
        compiler_params=pltpu.CompilerParams(vmem_limit_bytes=VMEM_LIMIT),
        name=name,
    )


def swap(x, axes):
    return lax.all_to_all(x, axes, split_axis=0, concat_axis=0, tiled=True)


def summed_copies(x, copies):
    total = jnp.sum(x, axis=0)
    return jnp.broadcast_to(total[None], (copies,) + total.shape)


def per_device(
    ensemble, neighbours, regime, norm_gain, up_weight, down_weight, vertical_modes,
    obs_col, obs_lev, obs_val, obs_err,
):
    shape = jax.ShapeDtypeStruct
    forward = [(n, n + 1) for n in range(63)]
    backward = [(b, a) for a, b in forward]
    low = lax.ppermute(ensemble[:, C - HALO:, :], BANDS, forward)
    high = lax.ppermute(ensemble[:, :HALO, :], BANDS, backward)
    lev = obs_lev.reshape(1, OBS)
    col = obs_col.reshape(1, OBS)
    val = obs_val.reshape(1, OBS)
    err = obs_err.reshape(1, OBS)
    forecast, values, at_obs = call(
        forecast_kernel,
        [shape((C, MD, LEV), F32), shape((GROUPS, MD, OBS), F32), shape((L, OBS), F32)],
        [pltpu.VMEM((C + 2 * HALO, MD, LEV), F32), pltpu.VMEM((C * MD, LEV), jnp.int32)],
        smem=2, total=12, name="forecast",
    )(
        neighbours, regime, ensemble, low, high, norm_gain.reshape(1, LEV), up_weight, down_weight,
        lev, col, err, vertical_modes,
    )
    values = swap(values, "members")
    gathered = lax.all_gather(forecast, "members")
    packed = call(
        gram_kernel,
        shape((8, PACKS, 8, M), F32),
        [pltpu.VMEM((M, OBS), F32)],
        total=4, name="gram",
    )(values, at_obs, val, err)
    packed = swap(packed, ("x", "core"))
    packed = swap(summed_copies(packed, 8), "z")
    mine = swap(summed_copies(packed, GROUPS), "members")
    other = lax.ppermute(mine, "core", [(0, 1), (1, 0)])
    size = L * M
    return call(
        analysis_kernel,
        shape((MD, C, LEV), F32),
        [
            pltpu.VMEM((PACKS, M, M), F32),
            pltpu.VMEM((L, M, M), F32),
            pltpu.VMEM((size, size), F32),
            pltpu.VMEM((size + MD, size), BF),
            pltpu.VMEM((size + MD, size), BF),
            pltpu.VMEM((size, size), BF),
            pltpu.VMEM((size, size), BF),
        ],
        total=5, name="analysis",
    )(mine, other, gathered, forecast, vertical_modes)


def solution(mesh):
    fine = Mesh(mesh.devices.reshape(8, 8, 4, 2), ("members",) + BANDS)
    in_specs = (
        P("members", BANDS, None),
        P(BANDS, None),
        P(BANDS),
        P(),
        P(),
        P(),
        P(),
        P(BANDS),
        P(BANDS),
        P(BANDS),
        P(BANDS),
    )
    out_specs = P("members", BANDS, None)
    return jax.shard_map(
        per_device, mesh=fine, in_specs=in_specs, out_specs=out_specs, check_vma=False
    )
```

time: 369 us -> 107 us (0.29)
  waiting for transfers between devices: 177 us -> 2.31 us
  blocking collectives: 118 us -> 56.8 us
  matrix products: 27.5 us -> 0 us
  Pallas kernels: 0 us -> 11.5 us
  local copies, waits for them, and re-layouts: 11.9 us -> 5.74 us
  other arithmetic: 5.08 us -> 0.03 us
    psum x1 -> x0, waiting for transfers between devices: 169 us -> none  [per_device(): lax.psum((gram_part, cross_part, drive_part), ('members', 'bands'))]
    psum x1 -> x0, blocking collectives: 105 us -> none  [per_device(): lax.psum((gram_part, cross_part, drive_part), ('members', 'bands'))]
    all_to_all x1 -> x4, blocking collectives: 13 us -> 56.8 us  [swap(): return lax.all_to_all(x, axes, split_axis=0, concat_axis=0, tiled=True)]
    dot_general x20 -> x0, matrix products: 27.5 us -> none  [the longest x3 5.94 us: analysis_coefficients(): iterate = jnp.dot(iterate, factor, precision=highest)]
    pallas_call x0 -> x3, Pallas kernels: none -> 11.5 us  [the longest x1 8.59 us: per_device(): call(analysis_kernel, shape((MD, C, LEV), F32), [pltpu.VMEM((PACKS, M, M)...]
    all_to_all x1 -> x0, waiting for transfers between devices: 8.1 us -> none  [per_device(): lax.all_to_all(predicted_vector, 'members', split_axis=1, concat_axis=0,...]
    gather x7 -> x0, local copies, waits for them, and re-layouts: 7.3 us -> none  [the longest x1 2.4 us: per_device(): average_sample_vector[clipped, obs_lev]]
    ppermute x2 -> x3, starting transfers between devices: 10.2 us -> 16.4 us  [the longest x1 8.79 us: per_device(): high = lax.ppermute(ensemble[:, :HALO, :], BANDS, backward)]
  transfers between devices with their start and end apart: 4 -> 4, of which waited for: 2 -> 2; matrix products, arithmetic and copies ran while one was open for 1% -> 0% of each run, Pallas kernels for 0% -> 0%
where the time goes in v1:
time: 107 us; the launch traced here: 106 us
  blocking collectives  56.8 us (53%)
  starting transfers between devices  16.4 us (15%)
  between operations  13.5 us (13%)
  Pallas kernels  11.5 us (11%)
  local copies, waits for them, and re-layouts  5.74 us (5%)
  waiting for transfers between devices  2.31 us (2%)
    all_to_all x4, blocking collectives, swap(): return lax.all_to_all(x, axes, split_axis=0, concat_axis=0, tiled=True)  56.8 us
    ppermute x1, starting transfers between devices, per_device(): high = lax.ppermute(ensemble[:, :HALO, :], BANDS, backward)  8.79 us
    pallas_call x1, Pallas kernels, per_device(): call(analysis_kernel, shape((MD, C, LEV), F32), [pltpu.VMEM((PACKS, M, M)...  8.59 us
    ppermute x1, starting transfers between devices, per_device(): other = lax.ppermute(mine, 'core', [(0, 1), (1, 0)])  5.72 us
    unnamed x25, local copies, waits for them, and re-layouts  4.79 us
    pallas_call x1, Pallas kernels, per_device(): call(forecast_kernel, [shape((C, MD, LEV), F32), shape((GROUPS, MD, OBS),...  2.57 us
  transfers between devices with their start and end apart: 4, of which 2 were waited for; matrix products, arithmetic and copies ran while one was open for 0% of the time, Pallas kernels for 0%

profile of v1, /device:TPU:1, one launch (start us, length us, event | category | flops | bytes accessed | tf_op | source)
XLA Modules:
  0.0 106.3 jit_solution(3010116031306212676)
XLA Ops:
  6.5 0.9 fusion
  7.5 0.0 copy-start.11
  7.5 8.8 %collective-permute-start.1 = (f32[16,8,128]{2,1,0:T(8,128)S(1)}, f32[16,8,128]{2,1,0:T(8,128)S(1)}, u32[]{:S(2)}, u32[]{:S(2)}) collective-permute-start(f32[16,8,128]{2,1,0:T(8,128)S(1)} %get-tuple-element.11), channel_id=1, source_target_pairs={{1,0},{2,1},{3,2},{4,3},{5,4},{6,5},{7,6},{8,7},{9,8},{10,9},{11,1... | collective-permute-start | bytes 196616 | tf_op jit(solution)/shard_map/ppermute | solution.py:272
  16.3 1.9 %collective-permute-start = (f32[16,8,128]{2,1,0:T(8,128)S(1)}, f32[16,8,128]{2,1,0:T(8,128)S(1)}, u32[]{:S(2)}, u32[]{:S(2)}) collective-permute-start(f32[16,8,128]{2,1,0:T(8,128)S(1)} %get-tuple-element.12), channel_id=1, source_target_pairs={{0,1},{1,2},{2,3},{3,4},{4,5},{5,6},{6,7},{7,8},{8,9},{9,10},{10,1... | collective-permute-start | bytes 196616 | tf_op jit(solution)/shard_map/ppermute | solution.py:271
  18.2 0.1 copy.14.nb
  18.3 1.2 %collective-permute-done.low = f32[16,8,128]{2,1,0:T(8,128)S(1)} collective-permute-done((f32[16,8,128]{2,1,0:T(8,128)S(1)}, f32[16,8,128]{2,1,0:T(8,128)S(1)}, u32[]{:S(2)}, u32[]{:S(2)}) %collective-permute-start) | collective-permute-done | bytes 65568 | tf_op jit(solution)/shard_map/ppermute | solution.py:271
  19.5 0.6 copy-done.7
  20.2 0.0 copy-done.8
  20.2 0.0 copy-done.4
  20.2 0.0 copy-done.5
  20.2 1.0 copy-done.1
  21.3 1.0 copy-done.2
  22.3 2.6 %forecast.1 = (f32[16,16,128]{2,1,0:T(8,128)}, f32[8,16,256]{2,1,0:T(8,128)S(1)}, f32[4,256]{1,0:T(4,128)S(1)}) custom-call(s32[16,4]{1,0:T(8,128)S(1)} %copy.14.nb, s32[16]{0:T(128)S(1)} %copy-done.9, f32[16,16,128]{2,1,0:T(8,128)S(1)} %copy-done.3, f32[16,8,128]{2,1,0:T(8,128)S(1)} %collective-permute-done.low, ...), custom_call_target="tpu_custom_call" | custom-call | tf_op jit(solution)/shard_map/forecast/pallas_call | solution.py:277
  24.9 0.0 all-gather.3.cloned.1.call-update
  24.9 11.3 %all_to_all.20.values = f32[8,16,256]{2,1,0:T(8,128)S(1)} all-to-all(f32[8,16,256]{2,1,0:T(8,128)S(1)} %get-tuple-element.8), channel_id=1, replica_groups=mesh['members'=8,'z'=8,'x'=4,'core'=2] {'members'}, dimensions={0} | all-to-all | bytes 262144 | tf_op jit(solution)/shard_map/all_to_all | solution.py:256
  36.2 0.7 copy-done.6
  36.9 0.4 gram.1
  37.3 13.2 %all_to_all.21 = f32[8,7,8,128]{3,2,1,0:T(8,128)S(1)} all-to-all(f32[8,7,8,128]{3,2,1,0:T(8,128)S(1)} %gram.1), channel_id=1, replica_groups=mesh['members'=8,'z'=8,'x'=4,'core'=2] {'x','core'}, dimensions={0} | all-to-all | bytes 458752 | tf_op jit(solution)/shard_map/all_to_all | solution.py:256
  50.5 20.9 %all_to_all.22 = f32[8,7,8,128]{3,2,1,0:T(8,128)S(1)} all-to-all(f32[8,7,8,128]{3,2,1,0:T(8,128)S(1)} %broadcast_in_dim.4), channel_id=1, replica_groups=mesh['members'=8,'z'=8,'x'=4,'core'=2] {'z'}, dimensions={0} | all-to-all | bytes 458752 | tf_op jit(solution)/shard_map/all_to_all | solution.py:256
  71.4 11.4 %all_to_all.23.mine = f32[8,7,8,128]{3,2,1,0:T(8,128)S(1)} all-to-all(f32[8,7,8,128]{3,2,1,0:T(8,128)S(1)} %broadcast_in_dim.5), channel_id=1, replica_groups=mesh['members'=8,'z'=8,'x'=4,'core'=2] {'members'}, dimensions={0} | all-to-all | bytes 458752 | tf_op jit(solution)/shard_map/all_to_all | solution.py:256
  82.8 5.7 %collective-permute-start.2 = (f32[8,7,8,128]{3,2,1,0:T(8,128)S(1)}, f32[8,7,8,128]{3,2,1,0:T(8,128)S(1)}, u32[]{:S(2)}, u32[]{:S(2)}) collective-permute-start(f32[8,7,8,128]{3,2,1,0:T(8,128)S(1)} %all_to_all.23.mine), channel_id=1, source_target_pairs={{0,1},{1,0},{2,3},{3,2},{4,5},{5,4},{6,7},{7,6},{8,9},{9,8},{10,11... | collective-permute-start | bytes 688136 | tf_op jit(solution)/shard_map/ppermute | solution.py:297
  88.6 1.1 %collective-permute-done.2.other = f32[8,7,8,128]{3,2,1,0:T(8,128)S(1)} collective-permute-done((f32[8,7,8,128]{3,2,1,0:T(8,128)S(1)}, f32[8,7,8,128]{3,2,1,0:T(8,128)S(1)}, u32[]{:S(2)}, u32[]{:S(2)}) %collective-permute-start.2) | collective-permute-done | bytes 229408 | tf_op jit(solution)/shard_map/ppermute | solution.py:297
  89.7 1.2 %copy-done = f32[128,16,128]{2,1,0:T(8,128)S(1)} copy-done((f32[128,16,128]{2,1,0:T(8,128)S(1)}, f32[128,16,128]{2,1,0:T(8,128)}, u32[]{:S(2)}) %copy-start) | copy-done | bytes 1048600
  90.9 8.6 %analysis.1 = f32[16,16,128]{2,1,0:T(8,128)} custom-call(f32[8,7,8,128]{3,2,1,0:T(8,128)S(1)} %all_to_all.23.mine, f32[8,7,8,128]{3,2,1,0:T(8,128)S(1)} %collective-permute-done.2.other, f32[8,16,16,128]{3,2,1,0:T(8,128)S(1)} %bitcast.6, f32[16,16,128]{2,1,0:T(8,128)} %get-tuple-element.10.own_forecast, f32[4,128]{1,0:T(4,128)S(1)} %copy-done.4), custom_call_target="tpu_custom_call" | custom-call | tf_op jit(solution)/shard_map/analysis/pallas_call | solution.py:299
  (22 shorter events, 0.1 us)
Async XLA Ops:
  6.5 13.0 %copy-start.3 = (f32[16,16,128]{2,1,0:T(8,128)S(1)}, f32[16,16,128]{2,1,0:T(8,128)}, u32[]{:S(2)}) copy-start(f32[16,16,128]{2,1,0:T(8,128)} %ens.1) | copy-start | bytes 393220
  6.5 83.1 %all-gather.3.cloned.1.call-start = ((), (), s32[]{:S(2)}) async-start(), calls=%async_computation.4 | async-start | bytes 1179648 | tf_op jit(solution)/shard_map/all_gather | solution.py:287
  7.5 10.7 %copy-start.11 = (s32[16,4]{0,1:T(4,128)S(1)}, s32[16,4]{0,1:T(4,128)}, u32[]{:S(2)}) copy-start(s32[16,4]{0,1:T(4,128)} %param.12) | copy-start | bytes 772
  7.5 10.8 %collective-permute-start.1 = (f32[16,8,128]{2,1,0:T(8,128)S(1)}, f32[16,8,128]{2,1,0:T(8,128)S(1)}, u32[]{:S(2)}, u32[]{:S(2)}) collective-permute-start(f32[16,8,128]{2,1,0:T(8,128)S(1)} %get-tuple-element.11), channel_id=1, source_target_pairs={{1,0},{2,1},{3,2},{4,3},{5,4},{6,5},{7,6},{8,7},{9,8},{10,9},{11,1... | collective-permute-start | bytes 196616 | tf_op jit(solution)/shard_map/ppermute | solution.py:272
  16.3 3.2 %collective-permute-start = (f32[16,8,128]{2,1,0:T(8,128)S(1)}, f32[16,8,128]{2,1,0:T(8,128)S(1)}, u32[]{:S(2)}, u32[]{:S(2)}) collective-permute-start(f32[16,8,128]{2,1,0:T(8,128)S(1)} %get-tuple-element.12), channel_id=1, source_target_pairs={{0,1},{1,2},{2,3},{3,4},{4,5},{5,6},{6,7},{7,8},{8,9},{9,10},{10,1... | collective-permute-start | bytes 196616 | tf_op jit(solution)/shard_map/ppermute | solution.py:271
  18.2 1.3 %copy-start.10 = (f32[128]{0:T(128)S(1)}, f32[128]{0:T(128)}, u32[]{:S(2)}) copy-start(f32[128]{0:T(128)} %param.14) | copy-start | bytes 1540
  19.5 0.7 copy-start.7
  19.5 0.7 copy-start.8
  19.5 0.7 copy-start.4
  19.5 0.7 copy-start.5
  19.5 0.7 copy-start.9
  20.2 1.0 copy-start.1
  21.3 1.0 copy-start.2
  36.2 0.7 copy-start.6
  82.8 6.8 %collective-permute-start.2 = (f32[8,7,8,128]{3,2,1,0:T(8,128)S(1)}, f32[8,7,8,128]{3,2,1,0:T(8,128)S(1)}, u32[]{:S(2)}, u32[]{:S(2)}) collective-permute-start(f32[8,7,8,128]{3,2,1,0:T(8,128)S(1)} %all_to_all.23.mine), channel_id=1, source_target_pairs={{0,1},{1,0},{2,3},{3,2},{4,5},{5,4},{6,7},{7,6},{8,9},{9,8},{10,11... | collective-permute-start | bytes 688136 | tf_op jit(solution)/shard_map/ppermute | solution.py:297
  89.7 1.2 %copy-start = (f32[128,16,128]{2,1,0:T(8,128)S(1)}, f32[128,16,128]{2,1,0:T(8,128)}, u32[]{:S(2)}) copy-start(f32[128,16,128]{2,1,0:T(8,128)} %all-gather.3.cloned.1.call-done) | copy-start | bytes 3145732
Sparse Core Ops, SparseCore 0:
  25.0 39.3 all-gather.2

commit v2 on v1

--- a/solution.py
+++ b/solution.py
@@ -24,7 +24,8 @@
 ROOT = math.sqrt(L * M - 1)
 BF = jnp.bfloat16
 F32 = jnp.float32
-VMEM_LIMIT = 48 * 1024 * 1024
+VMEM_LIMIT = 40 * 1024 * 1024
+FULL_LIMIT = 53 * 1024 * 1024
 BANDS = ("z", "x", "core")
 
 
@@ -48,14 +49,35 @@
     return high, middle, (rest - middle.astype(F32)).astype(BF)
 
 
-def forecast_kernel(
-    nb, regime, ens, low, high, gain, up, down, lev, col, err, modes,
-    f_out, v_out, w_out, wide, regs,
+def prepare_kernel(
+    regime, ens, up, down, col, lev, val, err, modes, gain,
+    own_out, up_out, down_out, hot_out, regs_out, w_out, place_out,
 ):
     band = (lax.axis_index("z") * 4 + lax.axis_index("x")) * 2 + lax.axis_index("core")
+    place_out[...] = col[...] - band * C
     for c in range(C):
-        wide[HALO + c] = ens[:, c, :]
-        regs[c * MD:(c + 1) * MD, :] = jnp.full((MD, LEV), regime[c], jnp.int32)
+        own_out[c] = ens[:, c, :]
+        regs_out[c * MD:(c + 1) * MD, :] = jnp.full((MD, LEV), regime[c], jnp.int32)
+    up_out[...] = up[...]
+    down_out[...] = down[...]
+    one_hot = (lax.broadcasted_iota(jnp.int32, (LEV, OBS), 0) == lev[...]).astype(F32).astype(BF)
+    hot_out[...] = one_hot
+    at_obs = None
+    for part in split3(modes[...]):
+        got = dot(part, one_hot)
+        at_obs = got if at_obs is None else at_obs + got
+    w_out[0:L, :] = at_obs
+    w_out[L:L + 1, :] = val[...] / err[...]
+    w_out[L + 1:L + 2, :] = err[...]
+    w_out[L + 2:L + 3, 0:LEV] = gain[...]
+
+
+def forecast_kernel(
+    nb, own_columns, low, high, up, down, one_hot, which_ref, rows_in, place_in,
+    f_out, v_out, wide,
+):
+    band = (lax.axis_index("z") * 4 + lax.axis_index("x")) * 2 + lax.axis_index("core")
+    wide[HALO:HALO + C] = own_columns[...]
     for c in range(HALO):
         wide[c] = low[:, c, :]
         wide[HALO + C + c] = high[:, c, :]
@@ -65,18 +87,17 @@
         total = wide[nb[c, 0] - start]
         for k in range(1, NB):
             total = total + wide[nb[c, k] - start]
-        own = wide[HALO + c]
+        own = own_columns[c]
         rows.append(own + 0.5 * (0.25 * total - own))
     flat = jnp.concatenate(rows, axis=0)
     inv_rms = lax.rsqrt(jnp.mean(flat * flat, axis=1, keepdims=True) + 1e-05)
-    normed = (flat * inv_rms * gain[...]).astype(BF)
-    which = regs[...]
+    normed = (flat * inv_rms * rows_in[L + 2:L + 3, 0:LEV]).astype(BF)
+    which = which_ref[...]
     which4 = jnp.concatenate([which] * (FF // LEV), axis=1)
     pre = dot(normed, up[0])
     for e in range(1, E):
         pre = jnp.where(which4 == e, dot(normed, up[e]), pre)
     hidden = pre / (1.0 + jnp.exp(-pre))
-    out = flat
     tendency = None
     for e in range(E):
         part = dot(jnp.where(which4 == e, hidden, 0.0).astype(BF), down[e])
@@ -84,26 +105,20 @@
     out = flat + tendency
     f_out[...] = out.reshape(C, MD, LEV)
 
-    one_hot = (lax.broadcasted_iota(jnp.int32, (LEV, OBS), 0) == lev[...]).astype(F32).astype(BF)
     picked = None
     for part in split3(out):
-        got = dot(part, one_hot)
+        got = dot(part, one_hot[...])
         picked = got if picked is None else picked + got
-    place = col[...] - band * C
+    place = place_in[...]
     sampled = jnp.zeros((MD, OBS), F32)
     for c in range(C):
         sampled = sampled + jnp.where(place == c, picked[c * MD:(c + 1) * MD, :], 0.0)
-    sampled = sampled / err[...]
+    sampled = sampled / rows_in[L + 1:L + 2, :]
     for g in range(GROUPS):
         v_out[g] = sampled
-    at_obs = None
-    for part in split3(modes[...]):
-        got = dot(part, one_hot)
-        at_obs = got if at_obs is None else at_obs + got
-    w_out[...] = at_obs
-
-
-def gram_kernel(values, at_obs, val, err, packed, centred):
+
+
+def gram_kernel(values, at_obs, packed, centred):
     group = lax.axis_index("members")
     raw = values[...].reshape(M, OBS)
     mean = jnp.sum(raw, axis=0, keepdims=True) * (1.0 / M)
@@ -111,7 +126,7 @@
     again = jnp.sum(pert, axis=0, keepdims=True) * (1.0 / M)
     pert = pert - again
     centred[...] = pert
-    innovation = val[...] / err[...] - (mean + again)
+    innovation = at_obs[L:L + 1, :] - (mean + again)
     own = centred[pl.ds(pl.multiple_of(group * MD, MD), MD), :]
     w = at_obs[...]
     weights = [w[a:a + 1] * w[b:b + 1] * (1.0 / (L * M - 1)) for a, b in PAIRS]
@@ -140,9 +155,11 @@
 
 
 def analysis_kernel(
-    mine, other, forecasts, own_forecast, modes, out,
-    packed, crosses, zf, zh, zl, fh, fl,
+    mine, other, forecasts, modes, out,
+    packed, crosses, zf, zh, fh, held, arrival,
 ):
+    fetch = pltpu.make_async_copy(forecasts, held, arrival)
+    fetch.start()
     group = lax.axis_index("members")
     core = lax.axis_index("core")
     for g in range(GROUPS):
@@ -183,36 +200,30 @@
     v = jnp.concatenate(
         [drives[a] - 0.5 * crosses[a, own_rows, :] for a in range(L)], axis=1
     )
+    size = L * M
     z = zf[...] * inverse_norm
-    size = L * M
     for step in range(3):
         high, low = split2(z)
-        zf[...] = z
+        zf[0:size] = z
         zh[0:size] = high
-        zl[0:size] = low
+        zh[size:2 * size] = low
         vh, vl = split2(v)
-        zh[size:size + MD] = vh
-        zl[size:size + MD] = vl
-        a, b = zh[0:size], zl[0:size]
-        q = dot(a, a) + (dot(a, b) + dot(b, a))
-        identity = (
-            lax.broadcasted_iota(jnp.int32, (size, size), 0)
-            == lax.broadcasted_iota(jnp.int32, (size, size), 1)
-        )
-        f = jnp.where(identity, 2.25, 0.0) - 1.5 * zf[...] + 0.25 * q
-        high, low = split2(f)
-        fh[...] = high
-        fl[...] = low
-        a, b = zh[...], zl[...]
-        new = dot(a, fh[...]) + (dot(a, fl[...]) + dot(b, fh[...]))
-        z = new[0:size]
-        v = new[size:size + MD]
+        zh[2 * size:2 * size + MD] = vh
+        zh[2 * size + MD:] = vl
+        q = dot(zh[0:size], zh[0:size])
+        fh[...] = (0.25 * q - 1.5 * zf[...]).astype(BF)
+        new = dot(zh[...], fh[...])
+        z = 2.25 * zf[...] + (new[0:size] + new[size:2 * size])
+        v = 2.25 * v + (new[2 * size:2 * size + MD] + new[2 * size + MD:])
     high, low = split2(z)
     fh[...] = high
-    fl[...] = low
+    zh[0:size] = low
     for step in range(2):
         vh, vl = split2(v)
-        v = 1.5 * v - 0.5 * (dot(vh, fh[...]) + (dot(vh, fl[...]) + dot(vl, fh[...])))
+        both = jnp.concatenate([vh, vl], axis=0)
+        got = dot(both, fh[...])
+        got = got[:MD] + (got[MD:] + dot(vh, zh[0:size]))
+        v = 1.5 * v - 0.5 * got
     v = v * inverse_norm
     blocks = []
     for a in range(L):
@@ -222,32 +233,30 @@
     ch, cl = split2(coeff)
     both = jnp.concatenate([ch, cl], axis=0)
     scaled = modes[...] * (1.0 / ROOT)
+    fetch.wait()
     for c in range(0, C, 2):
         block = jnp.concatenate(
-            [forecasts[:, c + k].reshape(M, LEV) for k in range(2)], axis=1
+            [held[:, c + k].reshape(M, LEV) for k in range(2)], axis=1
         )
         bh, bl = split2(block)
         r = dot(both, bh)
         r = r[:L * MD] + (r[L * MD:] + dot(ch, bl))
         for k in range(2):
-            total = own_forecast[c + k]
+            total = held[group, c + k]
             for a in range(L):
                 total = total + scaled[a:a + 1] * r[a * MD:(a + 1) * MD, k * LEV:(k + 1) * LEV]
             out[:, c + k, :] = total
 
 
-def call(kernel, outs, scratch, smem=0, total=0, name=None, flops=0):
-    specs = [
-        pl.BlockSpec(memory_space=pltpu.SMEM if n < smem else pltpu.VMEM)
-        for n in range(total)
-    ]
+def call(kernel, outs, scratch, total, smem=0, remain=None, name=None):
+    spaces = [pltpu.SMEM if n < smem else pltpu.HBM if n == remain else pltpu.VMEM for n in range(total)]
     return pl.pallas_call(
         kernel,
         out_shape=outs,
-        in_specs=specs,
+        in_specs=[pl.BlockSpec(memory_space=s) for s in spaces],
         out_specs=jax.tree.map(lambda _: pl.BlockSpec(memory_space=pltpu.VMEM), outs),
         scratch_shapes=scratch,
-        compiler_params=pltpu.CompilerParams(vmem_limit_bytes=VMEM_LIMIT),
+        compiler_params=pltpu.CompilerParams(vmem_limit_bytes=VMEM_LIMIT if remain is None else FULL_LIMIT),
         name=name,
     )
 
@@ -274,23 +283,32 @@
     col = obs_col.reshape(1, OBS)
     val = obs_val.reshape(1, OBS)
     err = obs_err.reshape(1, OBS)
-    forecast, values, at_obs = call(
+    own, up, down, one_hot, which, at_obs, place = call(
+        prepare_kernel,
+        [
+            shape((C, MD, LEV), F32), shape((E, LEV, FF), BF), shape((E, FF, LEV), BF),
+            shape((LEV, OBS), BF), shape((C * MD, LEV), jnp.int32), shape((8, OBS), F32),
+            shape((1, OBS), jnp.int32),
+        ],
+        [], 10, smem=1, name="prepare",
+    )(
+        regime, ensemble, up_weight, down_weight, col, lev, val, err, vertical_modes,
+        norm_gain.reshape(1, LEV),
+    )
+    forecast, values = call(
         forecast_kernel,
-        [shape((C, MD, LEV), F32), shape((GROUPS, MD, OBS), F32), shape((L, OBS), F32)],
-        [pltpu.VMEM((C + 2 * HALO, MD, LEV), F32), pltpu.VMEM((C * MD, LEV), jnp.int32)],
-        smem=2, total=12, name="forecast",
-    )(
-        neighbours, regime, ensemble, low, high, norm_gain.reshape(1, LEV), up_weight, down_weight,
-        lev, col, err, vertical_modes,
-    )
+        [shape((C, MD, LEV), F32), shape((GROUPS, MD, OBS), F32)],
+        [pltpu.VMEM((C + 2 * HALO, MD, LEV), F32)],
+        10, smem=1, name="forecast",
+    )(neighbours, own, low, high, up, down, one_hot, which, at_obs, place)
     values = swap(values, "members")
     gathered = lax.all_gather(forecast, "members")
     packed = call(
         gram_kernel,
         shape((8, PACKS, 8, M), F32),
         [pltpu.VMEM((M, OBS), F32)],
-        total=4, name="gram",
-    )(values, at_obs, val, err)
+        2, name="gram",
+    )(values, at_obs)
     packed = swap(packed, ("x", "core"))
     packed = swap(summed_copies(packed, 8), "z")
     mine = swap(summed_copies(packed, GROUPS), "members")
@@ -303,13 +321,13 @@
             pltpu.VMEM((PACKS, M, M), F32),
             pltpu.VMEM((L, M, M), F32),
             pltpu.VMEM((size, size), F32),
-            pltpu.VMEM((size + MD, size), BF),
-            pltpu.VMEM((size + MD, size), BF),
+            pltpu.VMEM((2 * size + 2 * MD, size), BF),
             pltpu.VMEM((size, size), BF),
-            pltpu.VMEM((size, size), BF),
+            pltpu.VMEM((GROUPS, C, MD, LEV), F32),
+            pltpu.SemaphoreType.DMA,
         ],
-        total=5, name="analysis",
-    )(mine, other, gathered, forecast, vertical_modes)
+        4, remain=2, name="analysis",
+    )(mine, other, gathered, vertical_modes)
 
 
 def solution(mesh):

time: 107 us -> 98.5 us (0.921)
  Pallas kernels: 11.5 us -> 8.73 us
  blocking collectives: 56.8 us -> 54.4 us
  local copies, waits for them, and re-layouts: 5.74 us -> 3.85 us
  waiting for transfers between devices: 2.31 us -> 1.12 us
    pallas_call x1, Pallas kernels: 8.59 us -> 5.11 us  [per_device(): call(analysis_kernel, shape((MD, C, LEV), F32), [pltpu.VMEM((PACKS, M, M)...]
    all_to_all x4, blocking collectives: 56.8 us -> 54.4 us  [swap(): return lax.all_to_all(x, axes, split_axis=0, concat_axis=0, tiled=True)]
    unnamed x25 -> x23, local copies, waits for them, and re-layouts: 4.79 us -> 2.9 us
    ppermute x1, waiting for transfers between devices: 1.2 us -> 0.01 us  [per_device(): low = lax.ppermute(ensemble[:, C - HALO:, :], BANDS, forward)]
  transfers between devices with their start and end apart: 4 -> 4, of which waited for: 2 -> 1; matrix products, arithmetic and copies ran while one was open for 0% -> 0% of each run, Pallas kernels for 0% -> 1%
where the time goes in v2:
time: 98.5 us; the launch traced here: 98.1 us
  blocking collectives  54.4 us (55%)
  starting transfers between devices  16.4 us (17%)
  between operations  13.5 us (14%)
  Pallas kernels  8.73 us (9%)
  local copies, waits for them, and re-layouts  3.85 us (4%)
  waiting for transfers between devices  1.12 us (1%)
    all_to_all x4, blocking collectives, swap(): return lax.all_to_all(x, axes, split_axis=0, concat_axis=0, tiled=True)  54.4 us
    ppermute x1, starting transfers between devices, per_device(): high = lax.ppermute(ensemble[:, :HALO, :], BANDS, backward)  8.79 us
    ppermute x1, starting transfers between devices, per_device(): other = lax.ppermute(mine, 'core', [(0, 1), (1, 0)])  5.74 us
    pallas_call x1, Pallas kernels, per_device(): call(analysis_kernel, shape((MD, C, LEV), F32), [pltpu.VMEM((PACKS, M, M)...  5.11 us
    unnamed x23, local copies, waits for them, and re-layouts  2.9 us
    pallas_call x1, Pallas kernels, per_device(): call(forecast_kernel, [shape((C, MD, LEV), F32), shape((GROUPS, MD, OBS),...  2.43 us
  transfers between devices with their start and end apart: 4, of which 1 were waited for; matrix products, arithmetic and copies ran while one was open for 0% of the time, Pallas kernels for 1%

profile of v2, /device:TPU:1, one launch (start us, length us, event | category | flops | bytes accessed | tf_op | source)
XLA Modules:
  0.0 98.1 jit_solution(8026402871625642439)
XLA Ops:
  6.5 0.9 fusion
  7.5 8.8 %collective-permute-start.1 = (f32[16,8,128]{2,1,0:T(8,128)S(1)}, f32[16,8,128]{2,1,0:T(8,128)S(1)}, u32[]{:S(2)}, u32[]{:S(2)}) collective-permute-start(f32[16,8,128]{2,1,0:T(8,128)S(1)} %get-tuple-element.23), channel_id=1, source_target_pairs={{1,0},{2,1},{3,2},{4,3},{5,4},{6,5},{7,6},{8,7},{9,8},{10,9},{11,1... | collective-permute-start | bytes 196616 | tf_op jit(solution)/shard_map/ppermute | solution.py:281
  16.3 1.9 %collective-permute-start = (f32[16,8,128]{2,1,0:T(8,128)S(1)}, f32[16,8,128]{2,1,0:T(8,128)S(1)}, u32[]{:S(2)}, u32[]{:S(2)}) collective-permute-start(f32[16,8,128]{2,1,0:T(8,128)S(1)} %get-tuple-element.24), channel_id=1, source_target_pairs={{0,1},{1,2},{2,3},{3,4},{4,5},{5,6},{6,7},{7,8},{8,9},{9,10},{10,1... | collective-permute-start | bytes 196616 | tf_op jit(solution)/shard_map/ppermute | solution.py:280
  18.2 0.1 copy.14.nb
  18.3 0.0 copy-start.4
  18.3 0.6 copy-done.7
  19.0 0.0 copy-done.5
  19.0 0.0 copy-done.6
  19.0 0.0 copy-done.3
  19.0 0.0 copy-done.4
  19.1 1.0 %copy-done = bf16[4,128,512]{2,1,0:T(8,128)(2,1)S(1)} copy-done((bf16[4,128,512]{2,1,0:T(8,128)(2,1)S(1)}, bf16[4,128,512]{2,1,0:T(8,128)(2,1)}, u32[]{:S(2)}) %copy-start) | copy-done | bytes 524312
  20.1 1.0 %copy-done.1 = bf16[4,512,128]{2,1,0:T(8,128)(2,1)S(1)} copy-done((bf16[4,512,128]{2,1,0:T(8,128)(2,1)S(1)}, bf16[4,512,128]{2,1,0:T(8,128)(2,1)}, u32[]{:S(2)}) %copy-start.1) | copy-done | bytes 524312
  21.1 0.8 prepare.1
  22.0 0.0 collective-permute-done.low
  22.0 2.4 %forecast.1 = (f32[16,16,128]{2,1,0:T(8,128)}, f32[8,16,256]{2,1,0:T(8,128)S(1)}) custom-call(s32[16,4]{1,0:T(8,128)S(1)} %copy.14.nb, f32[16,16,128]{2,1,0:T(8,128)S(1)} %get-tuple-element.14.own_columns, f32[16,8,128]{2,1,0:T(8,128)S(1)} %collective-permute-done.low, f32[16,8,128]{2,1,0:T(8,128)S(1)} %collective-permute-done.1.high, ...), custom_call_target="tpu_custom_call" | custom-call | tf_op jit(solution)/shard_map/forecast/pallas_call | solution.py:298
  24.4 0.0 all-gather.3.cloned.1.call-update
  24.4 10.5 %all_to_all.20.values = f32[8,16,256]{2,1,0:T(8,128)S(1)} all-to-all(f32[8,16,256]{2,1,0:T(8,128)S(1)} %get-tuple-element.21), channel_id=1, replica_groups=mesh['members'=8,'z'=8,'x'=4,'core'=2] {'members'}, dimensions={0} | all-to-all | bytes 262144 | tf_op jit(solution)/shard_map/all_to_all | solution.py:265
  35.0 0.4 gram.1
  35.3 12.1 %all_to_all.21 = f32[8,7,8,128]{3,2,1,0:T(8,128)S(1)} all-to-all(f32[8,7,8,128]{3,2,1,0:T(8,128)S(1)} %gram.1), channel_id=1, replica_groups=mesh['members'=8,'z'=8,'x'=4,'core'=2] {'x','core'}, dimensions={0} | all-to-all | bytes 458752 | tf_op jit(solution)/shard_map/all_to_all | solution.py:265
  47.5 20.3 %all_to_all.22 = f32[8,7,8,128]{3,2,1,0:T(8,128)S(1)} all-to-all(f32[8,7,8,128]{3,2,1,0:T(8,128)S(1)} %broadcast_in_dim.4), channel_id=1, replica_groups=mesh['members'=8,'z'=8,'x'=4,'core'=2] {'z'}, dimensions={0} | all-to-all | bytes 458752 | tf_op jit(solution)/shard_map/all_to_all | solution.py:265
  67.8 11.4 %all_to_all.23.mine = f32[8,7,8,128]{3,2,1,0:T(8,128)S(1)} all-to-all(f32[8,7,8,128]{3,2,1,0:T(8,128)S(1)} %broadcast_in_dim.5), channel_id=1, replica_groups=mesh['members'=8,'z'=8,'x'=4,'core'=2] {'members'}, dimensions={0} | all-to-all | bytes 458752 | tf_op jit(solution)/shard_map/all_to_all | solution.py:265
  79.3 5.7 %collective-permute-start.2 = (f32[8,7,8,128]{3,2,1,0:T(8,128)S(1)}, f32[8,7,8,128]{3,2,1,0:T(8,128)S(1)}, u32[]{:S(2)}, u32[]{:S(2)}) collective-permute-start(f32[8,7,8,128]{3,2,1,0:T(8,128)S(1)} %all_to_all.23.mine), channel_id=1, source_target_pairs={{0,1},{1,0},{2,3},{3,2},{4,5},{5,4},{6,7},{7,6},{8,9},{9,8},{10,11... | collective-permute-start | bytes 688136 | tf_op jit(solution)/shard_map/ppermute | solution.py:315
  85.0 1.1 %collective-permute-done.2.other = f32[8,7,8,128]{3,2,1,0:T(8,128)S(1)} collective-permute-done((f32[8,7,8,128]{3,2,1,0:T(8,128)S(1)}, f32[8,7,8,128]{3,2,1,0:T(8,128)S(1)}, u32[]{:S(2)}, u32[]{:S(2)}) %collective-permute-start.2) | collective-permute-done | bytes 229408 | tf_op jit(solution)/shard_map/ppermute | solution.py:315
  86.1 5.1 %analysis.1 = f32[16,16,128]{2,1,0:T(8,128)} custom-call(f32[8,7,8,128]{3,2,1,0:T(8,128)S(1)} %all_to_all.23.mine, f32[8,7,8,128]{3,2,1,0:T(8,128)S(1)} %collective-permute-done.2.other, f32[8,16,16,128]{3,2,1,0:T(8,128)} %bitcast.11, f32[4,128]{1,0:T(4,128)S(1)} %copy-done.3), custom_call_target="tpu_custom_call" | custom-call | tf_op jit(solution)/shard_map/analysis/pallas_call | solution.py:317
  (21 shorter events, 0.1 us)
Async XLA Ops:
  6.5 11.8 %copy-start.2 = (f32[16,16,128]{2,1,0:T(8,128)S(1)}, f32[16,16,128]{2,1,0:T(8,128)}, u32[]{:S(2)}) copy-start(f32[16,16,128]{2,1,0:T(8,128)} %ens.1) | copy-start | bytes 393220
  6.5 79.6 %all-gather.3.cloned.1.call-start = ((), (), s32[]{:S(2)}) async-start(), calls=%async_computation.4 | async-start | bytes 1179648 | tf_op jit(solution)/shard_map/all_gather | solution.py:305
  7.5 10.7 %copy-start.10 = (s32[16,4]{0,1:T(4,128)S(1)}, s32[16,4]{0,1:T(4,128)}, u32[]{:S(2)}) copy-start(s32[16,4]{0,1:T(4,128)} %param.12) | copy-start | bytes 772
  7.5 14.5 %collective-permute-start.1 = (f32[16,8,128]{2,1,0:T(8,128)S(1)}, f32[16,8,128]{2,1,0:T(8,128)S(1)}, u32[]{:S(2)}, u32[]{:S(2)}) collective-permute-start(f32[16,8,128]{2,1,0:T(8,128)S(1)} %get-tuple-element.23), channel_id=1, source_target_pairs={{1,0},{2,1},{3,2},{4,3},{5,4},{6,5},{7,6},{8,7},{9,8},{10,9},{11,1... | collective-permute-start | bytes 196616 | tf_op jit(solution)/shard_map/ppermute | solution.py:281
  16.3 5.7 %collective-permute-start = (f32[16,8,128]{2,1,0:T(8,128)S(1)}, f32[16,8,128]{2,1,0:T(8,128)S(1)}, u32[]{:S(2)}, u32[]{:S(2)}) collective-permute-start(f32[16,8,128]{2,1,0:T(8,128)S(1)} %get-tuple-element.24), channel_id=1, source_target_pairs={{0,1},{1,2},{2,3},{3,4},{4,5},{5,6},{6,7},{7,8},{8,9},{9,10},{10,1... | collective-permute-start | bytes 196616 | tf_op jit(solution)/shard_map/ppermute | solution.py:280
  18.3 0.7 copy-start.7
  18.3 0.7 copy-start.9
  18.3 0.7 copy-start.5
  18.3 0.7 copy-start.6
  18.3 0.7 copy-start.3
  18.3 0.7 copy-start.4
  18.3 0.7 copy-start.8
  19.1 1.0 %copy-start = (bf16[4,128,512]{2,1,0:T(8,128)(2,1)S(1)}, bf16[4,128,512]{2,1,0:T(8,128)(2,1)}, u32[]{:S(2)}) copy-start(bf16[4,128,512]{2,1,0:T(8,128)(2,1)} %up.1) | copy-start | bytes 1572868
  20.1 1.0 %copy-start.1 = (bf16[4,512,128]{2,1,0:T(8,128)(2,1)S(1)}, bf16[4,512,128]{2,1,0:T(8,128)(2,1)}, u32[]{:S(2)}) copy-start(bf16[4,512,128]{2,1,0:T(8,128)(2,1)} %down.1) | copy-start | bytes 1572868
  79.3 6.8 %collective-permute-start.2 = (f32[8,7,8,128]{3,2,1,0:T(8,128)S(1)}, f32[8,7,8,128]{3,2,1,0:T(8,128)S(1)}, u32[]{:S(2)}, u32[]{:S(2)}) collective-permute-start(f32[8,7,8,128]{3,2,1,0:T(8,128)S(1)} %all_to_all.23.mine), channel_id=1, source_target_pairs={{0,1},{1,0},{2,3},{3,2},{4,5},{5,4},{6,7},{7,6},{8,9},{9,8},{10,11... | collective-permute-start | bytes 688136 | tf_op jit(solution)/shard_map/ppermute | solution.py:315
Sparse Core Ops, SparseCore 0:
  24.6 38.4 all-gather.2

commit v3 on v2

--- a/solution.py
+++ b/solution.py
@@ -25,7 +25,6 @@
 BF = jnp.bfloat16
 F32 = jnp.float32
 VMEM_LIMIT = 40 * 1024 * 1024
-FULL_LIMIT = 53 * 1024 * 1024
 BANDS = ("z", "x", "core")
 
 
@@ -118,7 +117,9 @@
         v_out[g] = sampled
 
 
-def gram_kernel(values, at_obs, packed, centred):
+def gram_kernel(values, at_obs, own_forecast, far_forecast, packed, pair, centred):
+    pair[0] = own_forecast[...]
+    pair[1] = far_forecast[...]
     group = lax.axis_index("members")
     raw = values[...].reshape(M, OBS)
     mean = jnp.sum(raw, axis=0, keepdims=True) * (1.0 / M)
@@ -154,14 +155,25 @@
                 packed[2 * x + h, t] = p[8 * h:8 * h + 8]
 
 
+def middle_kernel(parts, pair, far_pair, copies, quad):
+    total = parts[0]
+    for n in range(1, parts.shape[0]):
+        total = total + parts[n]
+    for n in range(copies.shape[0]):
+        copies[n] = total
+    quad[0:2] = pair[...]
+    quad[2:4] = far_pair[...]
+
+
 def analysis_kernel(
-    mine, other, forecasts, modes, out,
-    packed, crosses, zf, zh, fh, held, arrival,
+    mine, other, quad, far_quad, modes, out,
+    packed, crosses, zf, zh, fh, held,
 ):
-    fetch = pltpu.make_async_copy(forecasts, held, arrival)
-    fetch.start()
     group = lax.axis_index("members")
     core = lax.axis_index("core")
+    for n, offset in enumerate((0, 4, 2, 6)):
+        held[group ^ offset] = quad[n]
+        held[group ^ (offset + 1)] = far_quad[n]
     for g in range(GROUPS):
         for t in range(PACKS):
             at = pl.multiple_of(g * MD + core * 8, 8)
@@ -233,7 +245,6 @@
     ch, cl = split2(coeff)
     both = jnp.concatenate([ch, cl], axis=0)
     scaled = modes[...] * (1.0 / ROOT)
-    fetch.wait()
     for c in range(0, C, 2):
         block = jnp.concatenate(
             [held[:, c + k].reshape(M, LEV) for k in range(2)], axis=1
@@ -248,21 +259,25 @@
             out[:, c + k, :] = total
 
 
-def call(kernel, outs, scratch, total, smem=0, remain=None, name=None):
-    spaces = [pltpu.SMEM if n < smem else pltpu.HBM if n == remain else pltpu.VMEM for n in range(total)]
+def call(kernel, outs, scratch, total, smem=0, name=None):
+    spaces = [pltpu.SMEM if n < smem else pltpu.VMEM for n in range(total)]
     return pl.pallas_call(
         kernel,
         out_shape=outs,
         in_specs=[pl.BlockSpec(memory_space=s) for s in spaces],
         out_specs=jax.tree.map(lambda _: pl.BlockSpec(memory_space=pltpu.VMEM), outs),
         scratch_shapes=scratch,
-        compiler_params=pltpu.CompilerParams(vmem_limit_bytes=VMEM_LIMIT if remain is None else FULL_LIMIT),
+        compiler_params=pltpu.CompilerParams(vmem_limit_bytes=VMEM_LIMIT),
         name=name,
     )
 
 
 def swap(x, axes):
     return lax.all_to_all(x, axes, split_axis=0, concat_axis=0, tiled=True)
+
+
+def partner(x, distance):
+    return lax.ppermute(x, "members", [(n, n ^ distance) for n in range(GROUPS)])
 
 
 def summed_copies(x, copies):
@@ -301,16 +316,24 @@
         [pltpu.VMEM((C + 2 * HALO, MD, LEV), F32)],
         10, smem=1, name="forecast",
     )(neighbours, own, low, high, up, down, one_hot, which, at_obs, place)
+    far = partner(forecast, 4)
     values = swap(values, "members")
-    gathered = lax.all_gather(forecast, "members")
-    packed = call(
+    packed, pair = call(
         gram_kernel,
-        shape((8, PACKS, 8, M), F32),
+        [shape((8, PACKS, 8, M), F32), shape((2, C, MD, LEV), F32)],
         [pltpu.VMEM((M, OBS), F32)],
-        2, name="gram",
-    )(values, at_obs)
+        4, name="gram",
+    )(values, at_obs, forecast, far)
+    far_pair = partner(pair, 2)
     packed = swap(packed, ("x", "core"))
-    packed = swap(summed_copies(packed, 8), "z")
+    packed, quad = call(
+        middle_kernel,
+        [shape((8, PACKS, 8, M), F32), shape((4, C, MD, LEV), F32)],
+        [], 3, name="middle",
+    )(packed, pair, far_pair)
+    far_quad = partner(quad, 1)
+    packed = swap(packed, "z")
+    packed, far_quad = lax.optimization_barrier((packed, far_quad))
     mine = swap(summed_copies(packed, GROUPS), "members")
     other = lax.ppermute(mine, "core", [(0, 1), (1, 0)])
     size = L * M
@@ -324,10 +347,9 @@
             pltpu.VMEM((2 * size + 2 * MD, size), BF),
             pltpu.VMEM((size, size), BF),
             pltpu.VMEM((GROUPS, C, MD, LEV), F32),
-            pltpu.SemaphoreType.DMA,
         ],
-        4, remain=2, name="analysis",
-    )(mine, other, gathered, vertical_modes)
+        5, name="analysis",
+    )(mine, other, quad, far_quad, vertical_modes)
 
 
 def solution(mesh):

time: 98.5 us -> 101 us (1.025)
  the two profiles are of different devices: /device:TPU:1 before, /device:TPU:3 now
where the time goes in v3:
time: 101 us; the launch traced here: 99.9 us
  blocking collectives  45 us (45%)
  starting transfers between devices  30.4 us (30%)
  waiting for transfers between devices  11.5 us (11%)
  Pallas kernels  9 us (9%)
  local copies, waits for them, and re-layouts  3.84 us (4%)
    all_to_all x3, blocking collectives, swap(): return lax.all_to_all(x, axes, split_axis=0, concat_axis=0, tiled=True)  45 us
    ppermute x3, starting transfers between devices, partner(): lax.ppermute(x, 'members', [(n, n ^ distance) for n in range(GROUPS)])  12.3 us
    ppermute x3, waiting for transfers between devices, partner(): lax.ppermute(x, 'members', [(n, n ^ distance) for n in range(GROUPS)])  10.4 us
    all_to_all x1, starting transfers between devices, swap(): return lax.all_to_all(x, axes, split_axis=0, concat_axis=0, tiled=True)  6.82 us
    ppermute x1, starting transfers between devices, per_device(): other = lax.ppermute(mine, 'core', [(0, 1), (1, 0)])  5.68 us
    pallas_call x1, Pallas kernels, per_device(): call(analysis_kernel, shape((MD, C, LEV), F32), [pltpu.VMEM((PACKS, M, M)...  5.09 us
    ppermute x1, starting transfers between devices, per_device(): low = lax.ppermute(ensemble[:, C - HALO:, :], BANDS, forward)  3.02 us
    unnamed x23, local copies, waits for them, and re-layouts  2.9 us
  transfers between devices with their start and end apart: 7, of which 3 were waited for; matrix products, arithmetic and copies ran while one was open for 0% of the time, Pallas kernels for 1%

profile of v3, /device:TPU:3, one launch (start us, length us, event | category | flops | bytes accessed | tf_op | source)
XLA Modules:
  0.0 99.9 jit_solution(6322091161624794134)
XLA Ops:
  0.0 0.9 fusion
  0.9 2.6 %collective-permute-start.1 = (f32[16,8,128]{2,1,0:T(8,128)S(1)}, f32[16,8,128]{2,1,0:T(8,128)S(1)}, u32[]{:S(2)}, u32[]{:S(2)}) collective-permute-start(f32[16,8,128]{2,1,0:T(8,128)S(1)} %get-tuple-element.35), channel_id=1, source_target_pairs={{1,0},{2,1},{3,2},{4,3},{5,4},{6,5},{7,6},{8,7},{9,8},{10,9},{11,1... | collective-permute-start | bytes 196616 | tf_op jit(solution)/shard_map/ppermute | solution.py:296
  3.5 3.0 %collective-permute-start = (f32[16,8,128]{2,1,0:T(8,128)S(1)}, f32[16,8,128]{2,1,0:T(8,128)S(1)}, u32[]{:S(2)}, u32[]{:S(2)}) collective-permute-start(f32[16,8,128]{2,1,0:T(8,128)S(1)} %get-tuple-element.36), channel_id=1, source_target_pairs={{0,1},{1,2},{2,3},{3,4},{4,5},{5,6},{6,7},{7,8},{8,9},{9,10},{10,1... | collective-permute-start | bytes 196616 | tf_op jit(solution)/shard_map/ppermute | solution.py:295
  6.6 0.1 copy.12.nb
  6.7 0.6 copy-done.7
  7.3 0.0 copy-done.5
  7.4 1.0 %copy-done = bf16[4,128,512]{2,1,0:T(8,128)(2,1)S(1)} copy-done((bf16[4,128,512]{2,1,0:T(8,128)(2,1)S(1)}, bf16[4,128,512]{2,1,0:T(8,128)(2,1)}, u32[]{:S(2)}) %copy-start) | copy-done | bytes 524312
  8.5 1.0 %copy-done.1 = bf16[4,512,128]{2,1,0:T(8,128)(2,1)S(1)} copy-done((bf16[4,512,128]{2,1,0:T(8,128)(2,1)S(1)}, bf16[4,512,128]{2,1,0:T(8,128)(2,1)}, u32[]{:S(2)}) %copy-start.1) | copy-done | bytes 524312
  9.5 0.8 prepare.1
  10.3 2.7 %forecast.1 = (f32[16,16,128]{2,1,0:T(8,128)S(1)}, f32[8,16,256]{2,1,0:T(8,128)}) custom-call(s32[16,4]{1,0:T(8,128)S(1)} %copy.12.nb, f32[16,16,128]{2,1,0:T(8,128)S(1)} %get-tuple-element.20.own_columns, f32[16,8,128]{2,1,0:T(8,128)S(1)} %collective-permute-done.low, f32[16,8,128]{2,1,0:T(8,128)S(1)} %collective-permute-done.1.high, ...), custom_call_target="tpu_custom_call" | custom-call | tf_op jit(solution)/shard_map/forecast/pallas_call | solution.py:313
  13.0 6.8 %all-to-all-start = ((f32[8,16,256]{2,1,0:T(8,128)}), f32[8,16,256]{2,1,0:T(8,128)S(1)}, u32[]{:S(2)}, u32[]{:S(2)}) async-start(f32[8,16,256]{2,1,0:T(8,128)} %get-tuple-element.27), calls=%async_computation | async-start | bytes 262144 | tf_op jit(solution)/shard_map/all_to_all | solution.py:276
  19.8 7.3 %collective-permute-start.2 = (f32[16,16,128]{2,1,0:T(8,128)S(1)}, f32[16,16,128]{2,1,0:T(8,128)S(1)}, u32[]{:S(2)}, u32[]{:S(2)}) collective-permute-start(f32[16,16,128]{2,1,0:T(8,128)S(1)} %get-tuple-element.28.own_forecast), channel_id=1, source_target_pairs={{0,256},{64,320},{128,384},{192,448},{256,0},{320,64},{384,128},{4... | collective-permute-start | bytes 393224 | tf_op jit(solution)/shard_map/ppermute | solution.py:280
  27.1 7.6 %collective-permute-done.2.far_forecast = f32[16,16,128]{2,1,0:T(8,128)S(1)} collective-permute-done((f32[16,16,128]{2,1,0:T(8,128)S(1)}, f32[16,16,128]{2,1,0:T(8,128)S(1)}, u32[]{:S(2)}, u32[]{:S(2)}) %collective-permute-start.2) | collective-permute-done | bytes 131104 | tf_op jit(solution)/shard_map/ppermute | solution.py:280
  34.7 0.4 gram.1
  35.0 3.1 %collective-permute-start.3 = (f32[2,16,16,128]{3,2,1,0:T(8,128)S(1)}, f32[2,16,16,128]{3,2,1,0:T(8,128)S(1)}, u32[]{:S(2)}, u32[]{:S(2)}) collective-permute-start(f32[2,16,16,128]{3,2,1,0:T(8,128)S(1)} %get-tuple-element.30.pair), channel_id=1, source_target_pairs={{0,128},{64,192},{128,0},{192,64},{256,384},{320,448},{384,256},{4... | collective-permute-start | bytes 786440 | tf_op jit(solution)/shard_map/ppermute | solution.py:280
  38.1 10.7 %all_to_all.20.parts = f32[8,7,8,128]{3,2,1,0:T(8,128)S(1)} all-to-all(f32[8,7,8,128]{3,2,1,0:T(8,128)S(1)} %get-tuple-element.29), channel_id=1, replica_groups=mesh['members'=8,'z'=8,'x'=4,'core'=2] {'x','core'}, dimensions={0} | all-to-all | bytes 458752 | tf_op jit(solution)/shard_map/all_to_all | solution.py:276
  48.8 2.9 %collective-permute-done.3.far_pair = f32[2,16,16,128]{3,2,1,0:T(8,128)S(1)} collective-permute-done((f32[2,16,16,128]{3,2,1,0:T(8,128)S(1)}, f32[2,16,16,128]{3,2,1,0:T(8,128)S(1)}, u32[]{:S(2)}, u32[]{:S(2)}) %collective-permute-start.3) | collective-permute-done | bytes 262176 | tf_op jit(solution)/shard_map/ppermute | solution.py:280
  51.7 0.1 middle.1
  51.7 1.9 %collective-permute-start.4 = (f32[4,16,16,128]{3,2,1,0:T(8,128)S(1)}, f32[4,16,16,128]{3,2,1,0:T(8,128)S(1)}, u32[]{:S(2)}, u32[]{:S(2)}) collective-permute-start(f32[4,16,16,128]{3,2,1,0:T(8,128)S(1)} %get-tuple-element.32.quad), channel_id=1, source_target_pairs={{0,64},{64,0},{128,192},{192,128},{256,320},{320,256},{384,448},{4... | collective-permute-start | bytes 1572872 | tf_op jit(solution)/shard_map/ppermute | solution.py:280
  53.7 19.8 %all_to_all.21 = f32[8,7,8,128]{3,2,1,0:T(8,128)S(1)} all-to-all(f32[8,7,8,128]{3,2,1,0:T(8,128)S(1)} %get-tuple-element.31), channel_id=1, replica_groups=mesh['members'=8,'z'=8,'x'=4,'core'=2] {'z'}, dimensions={0} | all-to-all | bytes 458752 | tf_op jit(solution)/shard_map/all_to_all | solution.py:276
  73.5 14.5 %all_to_all.22.mine = f32[8,7,8,128]{3,2,1,0:T(8,128)S(1)} all-to-all(f32[8,7,8,128]{3,2,1,0:T(8,128)S(1)} %broadcast_in_dim.2), channel_id=1, replica_groups=mesh['members'=8,'z'=8,'x'=4,'core'=2] {'members'}, dimensions={0} | all-to-all | bytes 458752 | tf_op jit(solution)/shard_map/all_to_all | solution.py:276
  88.1 5.7 %collective-permute-start.5 = (f32[8,7,8,128]{3,2,1,0:T(8,128)S(1)}, f32[8,7,8,128]{3,2,1,0:T(8,128)S(1)}, u32[]{:S(2)}, u32[]{:S(2)}) collective-permute-start(f32[8,7,8,128]{3,2,1,0:T(8,128)S(1)} %all_to_all.22.mine), channel_id=1, source_target_pairs={{0,1},{1,0},{2,3},{3,2},{4,5},{5,4},{6,7},{7,6},{8,9},{9,8},{10,11... | collective-permute-start | bytes 688136 | tf_op jit(solution)/shard_map/ppermute | solution.py:338
  93.7 1.1 %collective-permute-done.5.other = f32[8,7,8,128]{3,2,1,0:T(8,128)S(1)} collective-permute-done((f32[8,7,8,128]{3,2,1,0:T(8,128)S(1)}, f32[8,7,8,128]{3,2,1,0:T(8,128)S(1)}, u32[]{:S(2)}, u32[]{:S(2)}) %collective-permute-start.5) | collective-permute-done | bytes 229408 | tf_op jit(solution)/shard_map/ppermute | solution.py:338
  94.8 5.1 %analysis.1 = f32[16,16,128]{2,1,0:T(8,128)} custom-call(f32[8,7,8,128]{3,2,1,0:T(8,128)S(1)} %all_to_all.22.mine, f32[8,7,8,128]{3,2,1,0:T(8,128)S(1)} %collective-permute-done.5.other, f32[4,16,16,128]{3,2,1,0:T(8,128)S(1)} %get-tuple-element.32.quad, f32[4,16,16,128]{3,2,1,0:T(8,128)S(1)} %collective-permute-done.4.far_quad, f32[4,128]{1,0:T(4,128)S(1)} %copy-done.3), custom_call_target="tpu_custom_call" | custom-call | tf_op jit(solution)/shard_map/analysis/pallas_call | solution.py:340
  (24 shorter events, 0.1 us)
Async XLA Ops:
  0.0 6.7 %copy-start.2 = (f32[16,16,128]{2,1,0:T(8,128)S(1)}, f32[16,16,128]{2,1,0:T(8,128)}, u32[]{:S(2)}) copy-start(f32[16,16,128]{2,1,0:T(8,128)} %ens.1) | copy-start | bytes 393220
  0.9 5.6 %copy-start.10 = (s32[16,4]{0,1:T(4,128)S(1)}, s32[16,4]{0,1:T(4,128)}, u32[]{:S(2)}) copy-start(s32[16,4]{0,1:T(4,128)} %param.12) | copy-start | bytes 772
  0.9 9.4 %collective-permute-start.1 = (f32[16,8,128]{2,1,0:T(8,128)S(1)}, f32[16,8,128]{2,1,0:T(8,128)S(1)}, u32[]{:S(2)}, u32[]{:S(2)}) collective-permute-start(f32[16,8,128]{2,1,0:T(8,128)S(1)} %get-tuple-element.35), channel_id=1, source_target_pairs={{1,0},{2,1},{3,2},{4,3},{5,4},{6,5},{7,6},{8,7},{9,8},{10,9},{11,1... | collective-permute-start | bytes 196616 | tf_op jit(solution)/shard_map/ppermute | solution.py:296
  3.5 6.8 %collective-permute-start = (f32[16,8,128]{2,1,0:T(8,128)S(1)}, f32[16,8,128]{2,1,0:T(8,128)S(1)}, u32[]{:S(2)}, u32[]{:S(2)}) collective-permute-start(f32[16,8,128]{2,1,0:T(8,128)S(1)} %get-tuple-element.36), channel_id=1, source_target_pairs={{0,1},{1,2},{2,3},{3,4},{4,5},{5,6},{6,7},{7,8},{8,9},{9,10},{10,1... | collective-permute-start | bytes 196616 | tf_op jit(solution)/shard_map/ppermute | solution.py:295
  6.7 0.7 copy-start.7
  6.7 0.7 copy-start.9
  6.7 0.7 copy-start.5
  6.7 0.7 copy-start.6
  6.7 0.7 copy-start.3
  6.7 0.7 copy-start.4
  6.7 0.7 copy-start.8
  7.4 1.0 %copy-start = (bf16[4,128,512]{2,1,0:T(8,128)(2,1)S(1)}, bf16[4,128,512]{2,1,0:T(8,128)(2,1)}, u32[]{:S(2)}) copy-start(bf16[4,128,512]{2,1,0:T(8,128)(2,1)} %up.1) | copy-start | bytes 1572868
  8.5 1.0 %copy-start.1 = (bf16[4,512,128]{2,1,0:T(8,128)(2,1)S(1)}, bf16[4,512,128]{2,1,0:T(8,128)(2,1)}, u32[]{:S(2)}) copy-start(bf16[4,512,128]{2,1,0:T(8,128)(2,1)} %down.1) | copy-start | bytes 1572868
  13.0 21.7 %all-to-all-start = ((f32[8,16,256]{2,1,0:T(8,128)}), f32[8,16,256]{2,1,0:T(8,128)S(1)}, u32[]{:S(2)}, u32[]{:S(2)}) async-start(f32[8,16,256]{2,1,0:T(8,128)} %get-tuple-element.27), calls=%async_computation | async-start | bytes 262144 | tf_op jit(solution)/shard_map/all_to_all | solution.py:276
  19.8 14.8 %collective-permute-start.2 = (f32[16,16,128]{2,1,0:T(8,128)S(1)}, f32[16,16,128]{2,1,0:T(8,128)S(1)}, u32[]{:S(2)}, u32[]{:S(2)}) collective-permute-start(f32[16,16,128]{2,1,0:T(8,128)S(1)} %get-tuple-element.28.own_forecast), channel_id=1, source_target_pairs={{0,256},{64,320},{128,384},{192,448},{256,0},{320,64},{384,128},{4... | collective-permute-start | bytes 393224 | tf_op jit(solution)/shard_map/ppermute | solution.py:280
  35.0 16.6 %collective-permute-start.3 = (f32[2,16,16,128]{3,2,1,0:T(8,128)S(1)}, f32[2,16,16,128]{3,2,1,0:T(8,128)S(1)}, u32[]{:S(2)}, u32[]{:S(2)}) collective-permute-start(f32[2,16,16,128]{3,2,1,0:T(8,128)S(1)} %get-tuple-element.30.pair), channel_id=1, source_target_pairs={{0,128},{64,192},{128,0},{192,64},{256,384},{320,448},{384,256},{4... | collective-permute-start | bytes 786440 | tf_op jit(solution)/shard_map/ppermute | solution.py:280
  51.7 21.8 %collective-permute-start.4 = (f32[4,16,16,128]{3,2,1,0:T(8,128)S(1)}, f32[4,16,16,128]{3,2,1,0:T(8,128)S(1)}, u32[]{:S(2)}, u32[]{:S(2)}) collective-permute-start(f32[4,16,16,128]{3,2,1,0:T(8,128)S(1)} %get-tuple-element.32.quad), channel_id=1, source_target_pairs={{0,64},{64,0},{128,192},{192,128},{256,320},{320,256},{384,448},{4... | collective-permute-start | bytes 1572872 | tf_op jit(solution)/shard_map/ppermute | solution.py:280
  88.1 6.8 %collective-permute-start.5 = (f32[8,7,8,128]{3,2,1,0:T(8,128)S(1)}, f32[8,7,8,128]{3,2,1,0:T(8,128)S(1)}, u32[]{:S(2)}, u32[]{:S(2)}) collective-permute-start(f32[8,7,8,128]{3,2,1,0:T(8,128)S(1)} %all_to_all.22.mine), channel_id=1, source_target_pairs={{0,1},{1,0},{2,3},{3,2},{4,5},{5,4},{6,7},{7,6},{8,9},{9,8},{10,11... | collective-permute-start | bytes 688136 | tf_op jit(solution)/shard_map/ppermute | solution.py:338

commit v4 on v3

--- a/solution.py
+++ b/solution.py
@@ -117,9 +117,7 @@
         v_out[g] = sampled
 
 
-def gram_kernel(values, at_obs, own_forecast, far_forecast, packed, pair, centred):
-    pair[0] = own_forecast[...]
-    pair[1] = far_forecast[...]
+def gram_kernel(values, at_obs, packed, centred):
     group = lax.axis_index("members")
     raw = values[...].reshape(M, OBS)
     mean = jnp.sum(raw, axis=0, keepdims=True) * (1.0 / M)
@@ -155,14 +153,14 @@
                 packed[2 * x + h, t] = p[8 * h:8 * h + 8]
 
 
-def middle_kernel(parts, pair, far_pair, copies, quad):
+def middle_kernel(parts, own, far2, far4, far6, copies, quad):
     total = parts[0]
     for n in range(1, parts.shape[0]):
         total = total + parts[n]
     for n in range(copies.shape[0]):
         copies[n] = total
-    quad[0:2] = pair[...]
-    quad[2:4] = far_pair[...]
+    for n, block in enumerate((own, far2, far4, far6)):
+        quad[n] = block[...]
 
 
 def analysis_kernel(
@@ -171,7 +169,7 @@
 ):
     group = lax.axis_index("members")
     core = lax.axis_index("core")
-    for n, offset in enumerate((0, 4, 2, 6)):
+    for n, offset in enumerate((0, 2, 4, 6)):
         held[group ^ offset] = quad[n]
         held[group ^ (offset + 1)] = far_quad[n]
     for g in range(GROUPS):
@@ -316,21 +314,21 @@
         [pltpu.VMEM((C + 2 * HALO, MD, LEV), F32)],
         10, smem=1, name="forecast",
     )(neighbours, own, low, high, up, down, one_hot, which, at_obs, place)
-    far = partner(forecast, 4)
     values = swap(values, "members")
-    packed, pair = call(
+    packed = call(
         gram_kernel,
-        [shape((8, PACKS, 8, M), F32), shape((2, C, MD, LEV), F32)],
+        shape((8, PACKS, 8, M), F32),
         [pltpu.VMEM((M, OBS), F32)],
-        4, name="gram",
-    )(values, at_obs, forecast, far)
-    far_pair = partner(pair, 2)
+        2, name="gram",
+    )(values, at_obs)
+    packed, forecast = lax.optimization_barrier((packed, forecast))
+    far = [partner(forecast, distance) for distance in (2, 4, 6)]
     packed = swap(packed, ("x", "core"))
     packed, quad = call(
         middle_kernel,
         [shape((8, PACKS, 8, M), F32), shape((4, C, MD, LEV), F32)],
-        [], 3, name="middle",
-    )(packed, pair, far_pair)
+        [], 5, name="middle",
+    )(packed, forecast, *far)
     far_quad = partner(quad, 1)
     packed = swap(packed, "z")
     packed, far_quad = lax.optimization_barrier((packed, far_quad))

time: 101 us -> 106 us (1.050)
  the two profiles are of different devices: /device:TPU:3 before, /device:TPU:1 now
where the time goes in v4:
time: 106 us; the launch traced here: 105 us
  blocking collectives  44.4 us (42%)
  starting transfers between devices  35.8 us (34%)
  waiting for transfers between devices  12 us (11%)
  Pallas kernels  9.02 us (9%)
  local copies, waits for them, and re-layouts  3.84 us (4%)
    all_to_all x3, blocking collectives, swap(): return lax.all_to_all(x, axes, split_axis=0, concat_axis=0, tiled=True)  44.4 us
    ppermute x4, starting transfers between devices, partner(): lax.ppermute(x, 'members', [(n, n ^ distance) for n in range(GROUPS)])  13.3 us
    ppermute x4, waiting for transfers between devices, partner(): lax.ppermute(x, 'members', [(n, n ^ distance) for n in range(GROUPS)])  10.9 us
    ppermute x1, starting transfers between devices, per_device(): high = lax.ppermute(ensemble[:, :HALO, :], BANDS, backward)  8.79 us
    all_to_all x1, starting transfers between devices, swap(): return lax.all_to_all(x, axes, split_axis=0, concat_axis=0, tiled=True)  6.05 us
    ppermute x1, starting transfers between devices, per_device(): other = lax.ppermute(mine, 'core', [(0, 1), (1, 0)])  5.71 us
    pallas_call x1, Pallas kernels, per_device(): call(analysis_kernel, shape((MD, C, LEV), F32), [pltpu.VMEM((PACKS, M, M)...  5.09 us
    unnamed x23, local copies, waits for them, and re-layouts  2.9 us
  transfers between devices with their start and end apart: 8, of which 3 were waited for; matrix products, arithmetic and copies ran while one was open for 0% of the time, Pallas kernels for 1%

profile of v4, /device:TPU:1, one launch (start us, length us, event | category | flops | bytes accessed | tf_op | source)
XLA Modules:
  0.0 105.2 jit_solution(4757192586139092903)
XLA Ops:
  0.0 0.9 fusion
  0.9 8.8 %collective-permute-start.1 = (f32[16,8,128]{2,1,0:T(8,128)S(1)}, f32[16,8,128]{2,1,0:T(8,128)S(1)}, u32[]{:S(2)}, u32[]{:S(2)}) collective-permute-start(f32[16,8,128]{2,1,0:T(8,128)S(1)} %get-tuple-element.35), channel_id=1, source_target_pairs={{1,0},{2,1},{3,2},{4,3},{5,4},{6,5},{7,6},{8,7},{9,8},{10,9},{11,1... | collective-permute-start | bytes 196616 | tf_op jit(solution)/shard_map/ppermute | solution.py:294
  9.7 1.9 %collective-permute-start = (f32[16,8,128]{2,1,0:T(8,128)S(1)}, f32[16,8,128]{2,1,0:T(8,128)S(1)}, u32[]{:S(2)}, u32[]{:S(2)}) collective-permute-start(f32[16,8,128]{2,1,0:T(8,128)S(1)} %get-tuple-element.36), channel_id=1, source_target_pairs={{0,1},{1,2},{2,3},{3,4},{4,5},{5,6},{6,7},{7,8},{8,9},{9,10},{10,1... | collective-permute-start | bytes 196616 | tf_op jit(solution)/shard_map/ppermute | solution.py:293
  11.7 0.1 copy.12.nb
  11.8 0.6 copy-done.7
  12.5 1.0 copy-done
  13.6 1.0 copy-done.1
  14.6 0.8 prepare.1
  15.4 2.0 %forecast.1 = (f32[16,16,128]{2,1,0:T(8,128)S(1)}, f32[8,16,256]{2,1,0:T(8,128)S(1)}) custom-call(s32[16,4]{1,0:T(8,128)S(1)} %copy.12.nb, f32[16,16,128]{2,1,0:T(8,128)S(1)} %get-tuple-element.20.own_columns, f32[16,8,128]{2,1,0:T(8,128)S(1)} %collective-permute-done.low, f32[16,8,128]{2,1,0:T(8,128)S(1)} %collective-permute-done.1.high, ...), custom_call_target="tpu_custom_call" | custom-call | tf_op jit(solution)/shard_map/forecast/pallas_call | solution.py:311
  17.5 10.6 %all_to_all.20.values = f32[8,16,256]{2,1,0:T(8,128)S(1)} all-to-all(f32[8,16,256]{2,1,0:T(8,128)S(1)} %get-tuple-element.27), channel_id=1, replica_groups=mesh['members'=8,'z'=8,'x'=4,'core'=2] {'members'}, dimensions={0} | all-to-all | bytes 262144 | tf_op jit(solution)/shard_map/all_to_all | solution.py:274
  28.0 1.0 gram.1
  29.1 6.1 %all-to-all-start.1 = ((f32[8,7,8,128]{3,2,1,0:T(8,128)}), f32[8,7,8,128]{3,2,1,0:T(8,128)S(1)}, u32[]{:S(2)}, u32[]{:S(2)}) async-start(f32[8,7,8,128]{3,2,1,0:T(8,128)} %gram.1), calls=%async_computation.1 | async-start | bytes 458752 | tf_op jit(solution)/shard_map/all_to_all | solution.py:274
  35.1 1.9 %collective-permute-start.4 = (f32[16,16,128]{2,1,0:T(8,128)S(1)}, f32[16,16,128]{2,1,0:T(8,128)S(1)}, u32[]{:S(2)}, u32[]{:S(2)}) collective-permute-start(f32[16,16,128]{2,1,0:T(8,128)S(1)} %get-tuple-element.30.own), channel_id=1, source_target_pairs={{0,384},{64,448},{128,256},{192,320},{256,128},{320,192},{384,0},{... | collective-permute-start | bytes 393224 | tf_op jit(solution)/shard_map/ppermute | solution.py:278
  37.0 4.9 %collective-permute-start.3 = (f32[16,16,128]{2,1,0:T(8,128)S(1)}, f32[16,16,128]{2,1,0:T(8,128)S(1)}, u32[]{:S(2)}, u32[]{:S(2)}) collective-permute-start(f32[16,16,128]{2,1,0:T(8,128)S(1)} %get-tuple-element.30.own), channel_id=1, source_target_pairs={{0,256},{64,320},{128,384},{192,448},{256,0},{320,64},{384,128},{4... | collective-permute-start | bytes 393224 | tf_op jit(solution)/shard_map/ppermute | solution.py:278
  42.0 4.5 %collective-permute-start.2 = (f32[16,16,128]{2,1,0:T(8,128)S(1)}, f32[16,16,128]{2,1,0:T(8,128)S(1)}, u32[]{:S(2)}, u32[]{:S(2)}) collective-permute-start(f32[16,16,128]{2,1,0:T(8,128)S(1)} %get-tuple-element.30.own), channel_id=1, source_target_pairs={{0,128},{64,192},{128,0},{192,64},{256,384},{320,448},{384,256},{4... | collective-permute-start | bytes 393224 | tf_op jit(solution)/shard_map/ppermute | solution.py:278
  46.5 6.1 %collective-permute-done.3.far4 = f32[16,16,128]{2,1,0:T(8,128)S(1)} collective-permute-done((f32[16,16,128]{2,1,0:T(8,128)S(1)}, f32[16,16,128]{2,1,0:T(8,128)S(1)}, u32[]{:S(2)}, u32[]{:S(2)}) %collective-permute-start.3) | collective-permute-done | bytes 131104 | tf_op jit(solution)/shard_map/ppermute | solution.py:278
  52.6 4.8 %collective-permute-done.2.far2 = f32[16,16,128]{2,1,0:T(8,128)S(1)} collective-permute-done((f32[16,16,128]{2,1,0:T(8,128)S(1)}, f32[16,16,128]{2,1,0:T(8,128)S(1)}, u32[]{:S(2)}, u32[]{:S(2)}) %collective-permute-start.2) | collective-permute-done | bytes 131104 | tf_op jit(solution)/shard_map/ppermute | solution.py:278
  57.5 0.1 middle.1
  57.5 1.9 %collective-permute-start.5 = (f32[4,16,16,128]{3,2,1,0:T(8,128)S(1)}, f32[4,16,16,128]{3,2,1,0:T(8,128)S(1)}, u32[]{:S(2)}, u32[]{:S(2)}) collective-permute-start(f32[4,16,16,128]{3,2,1,0:T(8,128)S(1)} %get-tuple-element.32.quad), channel_id=1, source_target_pairs={{0,64},{64,0},{128,192},{192,128},{256,320},{320,256},{384,448},{4... | collective-permute-start | bytes 1572872 | tf_op jit(solution)/shard_map/ppermute | solution.py:278
  59.4 21.4 %all_to_all.21 = f32[8,7,8,128]{3,2,1,0:T(8,128)S(1)} all-to-all(f32[8,7,8,128]{3,2,1,0:T(8,128)S(1)} %get-tuple-element.31), channel_id=1, replica_groups=mesh['members'=8,'z'=8,'x'=4,'core'=2] {'z'}, dimensions={0} | all-to-all | bytes 458752 | tf_op jit(solution)/shard_map/all_to_all | solution.py:274
  80.8 12.5 %all_to_all.22.mine = f32[8,7,8,128]{3,2,1,0:T(8,128)S(1)} all-to-all(f32[8,7,8,128]{3,2,1,0:T(8,128)S(1)} %broadcast_in_dim.2), channel_id=1, replica_groups=mesh['members'=8,'z'=8,'x'=4,'core'=2] {'members'}, dimensions={0} | all-to-all | bytes 458752 | tf_op jit(solution)/shard_map/all_to_all | solution.py:274
  93.3 5.7 %collective-permute-start.6 = (f32[8,7,8,128]{3,2,1,0:T(8,128)S(1)}, f32[8,7,8,128]{3,2,1,0:T(8,128)S(1)}, u32[]{:S(2)}, u32[]{:S(2)}) collective-permute-start(f32[8,7,8,128]{3,2,1,0:T(8,128)S(1)} %all_to_all.22.mine), channel_id=1, source_target_pairs={{0,1},{1,0},{2,3},{3,2},{4,5},{5,4},{6,7},{7,6},{8,9},{9,8},{10,11... | collective-permute-start | bytes 688136 | tf_op jit(solution)/shard_map/ppermute | solution.py:336
  99.1 1.1 %collective-permute-done.6.other = f32[8,7,8,128]{3,2,1,0:T(8,128)S(1)} collective-permute-done((f32[8,7,8,128]{3,2,1,0:T(8,128)S(1)}, f32[8,7,8,128]{3,2,1,0:T(8,128)S(1)}, u32[]{:S(2)}, u32[]{:S(2)}) %collective-permute-start.6) | collective-permute-done | bytes 229408 | tf_op jit(solution)/shard_map/ppermute | solution.py:336
  100.2 5.1 %analysis.1 = f32[16,16,128]{2,1,0:T(8,128)} custom-call(f32[8,7,8,128]{3,2,1,0:T(8,128)S(1)} %all_to_all.22.mine, f32[8,7,8,128]{3,2,1,0:T(8,128)S(1)} %collective-permute-done.6.other, f32[4,16,16,128]{3,2,1,0:T(8,128)S(1)} %get-tuple-element.32.quad, f32[4,16,16,128]{3,2,1,0:T(8,128)S(1)} %collective-permute-done.5.far_quad, f32[4,128]{1,0:T(4,128)S(1)} %copy-done.3), custom_call_target="tpu_custom_call" | custom-call | tf_op jit(solution)/shard_map/analysis/pallas_call | solution.py:338
  (26 shorter events, 0.2 us)
Async XLA Ops:
  0.0 11.8 %copy-start.2 = (f32[16,16,128]{2,1,0:T(8,128)S(1)}, f32[16,16,128]{2,1,0:T(8,128)}, u32[]{:S(2)}) copy-start(f32[16,16,128]{2,1,0:T(8,128)} %ens.1) | copy-start | bytes 393220
  0.9 10.7 %copy-start.10 = (s32[16,4]{0,1:T(4,128)S(1)}, s32[16,4]{0,1:T(4,128)}, u32[]{:S(2)}) copy-start(s32[16,4]{0,1:T(4,128)} %param.12) | copy-start | bytes 772
  0.9 14.5 %collective-permute-start.1 = (f32[16,8,128]{2,1,0:T(8,128)S(1)}, f32[16,8,128]{2,1,0:T(8,128)S(1)}, u32[]{:S(2)}, u32[]{:S(2)}) collective-permute-start(f32[16,8,128]{2,1,0:T(8,128)S(1)} %get-tuple-element.35), channel_id=1, source_target_pairs={{1,0},{2,1},{3,2},{4,3},{5,4},{6,5},{7,6},{8,7},{9,8},{10,9},{11,1... | collective-permute-start | bytes 196616 | tf_op jit(solution)/shard_map/ppermute | solution.py:294
  9.7 5.7 %collective-permute-start = (f32[16,8,128]{2,1,0:T(8,128)S(1)}, f32[16,8,128]{2,1,0:T(8,128)S(1)}, u32[]{:S(2)}, u32[]{:S(2)}) collective-permute-start(f32[16,8,128]{2,1,0:T(8,128)S(1)} %get-tuple-element.36), channel_id=1, source_target_pairs={{0,1},{1,2},{2,3},{3,4},{4,5},{5,6},{6,7},{7,8},{8,9},{9,10},{10,1... | collective-permute-start | bytes 196616 | tf_op jit(solution)/shard_map/ppermute | solution.py:293
  11.8 0.7 copy-start.7
  11.8 0.7 copy-start.9
  11.8 0.7 copy-start.5
  11.8 0.7 copy-start.6
  11.8 0.7 copy-start.3
  11.8 0.7 copy-start.4
  11.8 0.7 copy-start.8
  12.5 1.0 copy-start
  13.6 1.0 copy-start.1
  29.1 28.4 %all-to-all-start.1 = ((f32[8,7,8,128]{3,2,1,0:T(8,128)}), f32[8,7,8,128]{3,2,1,0:T(8,128)S(1)}, u32[]{:S(2)}, u32[]{:S(2)}) async-start(f32[8,7,8,128]{3,2,1,0:T(8,128)} %gram.1), calls=%async_computation.1 | async-start | bytes 458752 | tf_op jit(solution)/shard_map/all_to_all | solution.py:274
  35.1 11.4 %collective-permute-start.4 = (f32[16,16,128]{2,1,0:T(8,128)S(1)}, f32[16,16,128]{2,1,0:T(8,128)S(1)}, u32[]{:S(2)}, u32[]{:S(2)}) collective-permute-start(f32[16,16,128]{2,1,0:T(8,128)S(1)} %get-tuple-element.30.own), channel_id=1, source_target_pairs={{0,384},{64,448},{128,256},{192,320},{256,128},{320,192},{384,0},{... | collective-permute-start | bytes 393224 | tf_op jit(solution)/shard_map/ppermute | solution.py:278
  37.0 15.6 %collective-permute-start.3 = (f32[16,16,128]{2,1,0:T(8,128)S(1)}, f32[16,16,128]{2,1,0:T(8,128)S(1)}, u32[]{:S(2)}, u32[]{:S(2)}) collective-permute-start(f32[16,16,128]{2,1,0:T(8,128)S(1)} %get-tuple-element.30.own), channel_id=1, source_target_pairs={{0,256},{64,320},{128,384},{192,448},{256,0},{320,64},{384,128},{4... | collective-permute-start | bytes 393224 | tf_op jit(solution)/shard_map/ppermute | solution.py:278
  42.0 15.5 %collective-permute-start.2 = (f32[16,16,128]{2,1,0:T(8,128)S(1)}, f32[16,16,128]{2,1,0:T(8,128)S(1)}, u32[]{:S(2)}, u32[]{:S(2)}) collective-permute-start(f32[16,16,128]{2,1,0:T(8,128)S(1)} %get-tuple-element.30.own), channel_id=1, source_target_pairs={{0,128},{64,192},{128,0},{192,64},{256,384},{320,448},{384,256},{4... | collective-permute-start | bytes 393224 | tf_op jit(solution)/shard_map/ppermute | solution.py:278
  57.5 23.3 %collective-permute-start.5 = (f32[4,16,16,128]{3,2,1,0:T(8,128)S(1)}, f32[4,16,16,128]{3,2,1,0:T(8,128)S(1)}, u32[]{:S(2)}, u32[]{:S(2)}) collective-permute-start(f32[4,16,16,128]{3,2,1,0:T(8,128)S(1)} %get-tuple-element.32.quad), channel_id=1, source_target_pairs={{0,64},{64,0},{128,192},{192,128},{256,320},{320,256},{384,448},{4... | collective-permute-start | bytes 1572872 | tf_op jit(solution)/shard_map/ppermute | solution.py:278
  93.3 6.8 %collective-permute-start.6 = (f32[8,7,8,128]{3,2,1,0:T(8,128)S(1)}, f32[8,7,8,128]{3,2,1,0:T(8,128)S(1)}, u32[]{:S(2)}, u32[]{:S(2)}) collective-permute-start(f32[8,7,8,128]{3,2,1,0:T(8,128)S(1)} %all_to_all.22.mine), channel_id=1, source_target_pairs={{0,1},{1,0},{2,3},{3,2},{4,5},{5,4},{6,7},{7,6},{8,9},{9,8},{10,11... | collective-permute-start | bytes 688136 | tf_op jit(solution)/shard_map/ppermute | solution.py:336

commit v5 on v2

--- a/solution.py
+++ b/solution.py
@@ -25,7 +25,6 @@
 BF = jnp.bfloat16
 F32 = jnp.float32
 VMEM_LIMIT = 40 * 1024 * 1024
-FULL_LIMIT = 53 * 1024 * 1024
 BANDS = ("z", "x", "core")
 
 
@@ -74,7 +73,7 @@
 
 def forecast_kernel(
     nb, own_columns, low, high, up, down, one_hot, which_ref, rows_in, place_in,
-    f_out, v_out, wide,
+    v_out, wide,
 ):
     band = (lax.axis_index("z") * 4 + lax.axis_index("x")) * 2 + lax.axis_index("core")
     wide[HALO:HALO + C] = own_columns[...]
@@ -103,8 +102,6 @@
         part = dot(jnp.where(which4 == e, hidden, 0.0).astype(BF), down[e])
         tendency = part if tendency is None else tendency + part
     out = flat + tendency
-    f_out[...] = out.reshape(C, MD, LEV)
-
     picked = None
     for part in split3(out):
         got = dot(part, one_hot[...])
@@ -115,12 +112,14 @@
         sampled = sampled + jnp.where(place == c, picked[c * MD:(c + 1) * MD, :], 0.0)
     sampled = sampled / rows_in[L + 1:L + 2, :]
     for g in range(GROUPS):
-        v_out[g] = sampled
+        for k in range(2):
+            v_out[g, k] = sampled[:, k * LEV:(k + 1) * LEV]
+            v_out[g, 2 + k] = out[(2 * g + k) * MD:(2 * g + k + 1) * MD]
 
 
 def gram_kernel(values, at_obs, packed, centred):
     group = lax.axis_index("members")
-    raw = values[...].reshape(M, OBS)
+    raw = jnp.concatenate([values[:, k].reshape(M, LEV) for k in range(2)], axis=1)
     mean = jnp.sum(raw, axis=0, keepdims=True) * (1.0 / M)
     pert = raw - mean
     again = jnp.sum(pert, axis=0, keepdims=True) * (1.0 / M)
@@ -155,12 +154,9 @@
 
 
 def analysis_kernel(
-    mine, other, forecasts, modes, out,
-    packed, crosses, zf, zh, fh, held, arrival,
+    mine, other, values, modes, out,
+    packed, crosses, zf, zh, fh,
 ):
-    fetch = pltpu.make_async_copy(forecasts, held, arrival)
-    fetch.start()
-    group = lax.axis_index("members")
     core = lax.axis_index("core")
     for g in range(GROUPS):
         for t in range(PACKS):
@@ -196,10 +192,7 @@
             square = part if square is None else square + part
     norm = jnp.sqrt(jnp.sum(square, axis=1, keepdims=True))
     inverse_norm = 1.0 / norm
-    own_rows = pl.ds(pl.multiple_of(group * MD, MD), MD)
-    v = jnp.concatenate(
-        [drives[a] - 0.5 * crosses[a, own_rows, :] for a in range(L)], axis=1
-    )
+    v = jnp.concatenate([drives[a] - 0.5 * crosses[a] for a in range(L)], axis=1)
     size = L * M
     z = zf[...] * inverse_norm
     for step in range(3):
@@ -208,13 +201,13 @@
         zh[0:size] = high
         zh[size:2 * size] = low
         vh, vl = split2(v)
-        zh[2 * size:2 * size + MD] = vh
-        zh[2 * size + MD:] = vl
+        zh[2 * size:2 * size + M] = vh
+        zh[2 * size + M:] = vl
         q = dot(zh[0:size], zh[0:size])
         fh[...] = (0.25 * q - 1.5 * zf[...]).astype(BF)
         new = dot(zh[...], fh[...])
         z = 2.25 * zf[...] + (new[0:size] + new[size:2 * size])
-        v = 2.25 * v + (new[2 * size:2 * size + MD] + new[2 * size + MD:])
+        v = 2.25 * v + (new[2 * size:2 * size + M] + new[2 * size + M:])
     high, low = split2(z)
     fh[...] = high
     zh[0:size] = low
@@ -222,7 +215,7 @@
         vh, vl = split2(v)
         both = jnp.concatenate([vh, vl], axis=0)
         got = dot(both, fh[...])
-        got = got[:MD] + (got[MD:] + dot(vh, zh[0:size]))
+        got = got[:M] + (got[M:] + dot(vh, zh[0:size]))
         v = 1.5 * v - 0.5 * got
     v = v * inverse_norm
     blocks = []
@@ -231,32 +224,26 @@
         blocks.append(block - jnp.mean(block, axis=1, keepdims=True))
     coeff = jnp.concatenate(blocks, axis=0)
     ch, cl = split2(coeff)
-    both = jnp.concatenate([ch, cl], axis=0)
     scaled = modes[...] * (1.0 / ROOT)
-    fetch.wait()
-    for c in range(0, C, 2):
-        block = jnp.concatenate(
-            [held[:, c + k].reshape(M, LEV) for k in range(2)], axis=1
-        )
-        bh, bl = split2(block)
-        r = dot(both, bh)
-        r = r[:L * MD] + (r[L * MD:] + dot(ch, bl))
-        for k in range(2):
-            total = held[group, c + k]
-            for a in range(L):
-                total = total + scaled[a:a + 1] * r[a * MD:(a + 1) * MD, k * LEV:(k + 1) * LEV]
-            out[:, c + k, :] = total
-
-
-def call(kernel, outs, scratch, total, smem=0, remain=None, name=None):
-    spaces = [pltpu.SMEM if n < smem else pltpu.HBM if n == remain else pltpu.VMEM for n in range(total)]
+    columns = [values[:, 2 + k].reshape(M, LEV) for k in range(2)]
+    bh, bl = split2(jnp.concatenate(columns, axis=1))
+    r = dot(ch, bh) + (dot(cl, bh) + dot(ch, bl))
+    for k in range(2):
+        total = columns[k]
+        for a in range(L):
+            total = total + scaled[a:a + 1] * r[a * M:(a + 1) * M, k * LEV:(k + 1) * LEV]
+        out[:, k] = total.reshape(GROUPS, MD, LEV)
+
+
+def call(kernel, outs, scratch, total, smem=0, name=None):
+    spaces = [pltpu.SMEM if n < smem else pltpu.VMEM for n in range(total)]
     return pl.pallas_call(
         kernel,
         out_shape=outs,
         in_specs=[pl.BlockSpec(memory_space=s) for s in spaces],
         out_specs=jax.tree.map(lambda _: pl.BlockSpec(memory_space=pltpu.VMEM), outs),
         scratch_shapes=scratch,
-        compiler_params=pltpu.CompilerParams(vmem_limit_bytes=VMEM_LIMIT if remain is None else FULL_LIMIT),
+        compiler_params=pltpu.CompilerParams(vmem_limit_bytes=VMEM_LIMIT),
         name=name,
     )
 
@@ -295,14 +282,13 @@
         regime, ensemble, up_weight, down_weight, col, lev, val, err, vertical_modes,
         norm_gain.reshape(1, LEV),
     )
-    forecast, values = call(
+    values = call(
         forecast_kernel,
-        [shape((C, MD, LEV), F32), shape((GROUPS, MD, OBS), F32)],
+        shape((GROUPS, 4, MD, LEV), F32),
         [pltpu.VMEM((C + 2 * HALO, MD, LEV), F32)],
         10, smem=1, name="forecast",
     )(neighbours, own, low, high, up, down, one_hot, which, at_obs, place)
     values = swap(values, "members")
-    gathered = lax.all_gather(forecast, "members")
     packed = call(
         gram_kernel,
         shape((8, PACKS, 8, M), F32),
@@ -314,20 +300,20 @@
     mine = swap(summed_copies(packed, GROUPS), "members")
     other = lax.ppermute(mine, "core", [(0, 1), (1, 0)])
     size = L * M
-    return call(
+    analysis = call(
         analysis_kernel,
-        shape((MD, C, LEV), F32),
+        shape((GROUPS, 2, MD, LEV), F32),
         [
             pltpu.VMEM((PACKS, M, M), F32),
             pltpu.VMEM((L, M, M), F32),
             pltpu.VMEM((size, size), F32),
-            pltpu.VMEM((2 * size + 2 * MD, size), BF),
+            pltpu.VMEM((2 * size + 2 * M, size), BF),
             pltpu.VMEM((size, size), BF),
-            pltpu.VMEM((GROUPS, C, MD, LEV), F32),
-            pltpu.SemaphoreType.DMA,
         ],
-        4, remain=2, name="analysis",
-    )(mine, other, gathered, vertical_modes)
+        4, name="analysis",
+    )(mine, other, values, vertical_modes)
+    analysis = swap(analysis, "members")
+    return analysis.transpose(2, 0, 1, 3).reshape(MD, C, LEV)
 
 
 def solution(mesh):

time: 98.5 us -> 97.8 us (level)
  between operations: 13.5 us -> 0.15 us
  blocking collectives: 54.4 us -> 66.9 us
    all_to_all x4 -> x5, blocking collectives: 54.4 us -> 66.9 us  [swap(): return lax.all_to_all(x, axes, split_axis=0, concat_axis=0, tiled=True)]
  transfers between devices with their start and end apart: 4 -> 3, of which waited for: 1 -> 1; matrix products, arithmetic and copies ran while one was open for 0% -> 0% of each run, Pallas kernels for 1% -> 1%
where the time goes in v5:
time: 97.8 us; the launch traced here: 97.4 us
  blocking collectives  66.9 us (68%)
  starting transfers between devices  16.4 us (17%)
  Pallas kernels  8.21 us (8%)
  local copies, waits for them, and re-layouts  4.55 us (5%)
  waiting for transfers between devices  1.1 us (1%)
    all_to_all x5, blocking collectives, swap(): return lax.all_to_all(x, axes, split_axis=0, concat_axis=0, tiled=True)  66.9 us
    ppermute x1, starting transfers between devices, per_device(): high = lax.ppermute(ensemble[:, :HALO, :], BANDS, backward)  8.79 us
    ppermute x1, starting transfers between devices, per_device(): other = lax.ppermute(mine, 'core', [(0, 1), (1, 0)])  5.72 us
    pallas_call x1, Pallas kernels, per_device(): call(analysis_kernel, shape((GROUPS, 2, MD, LEV), F32), [pltpu.VMEM((PACK...  5.02 us
    unnamed x23, local copies, waits for them, and re-layouts  2.9 us
    pallas_call x1, Pallas kernels, per_device(): call(forecast_kernel, shape((GROUPS, 4, MD, LEV), F32), [pltpu.VMEM((C +...  2.01 us
  transfers between devices with their start and end apart: 3, of which 1 were waited for; matrix products, arithmetic and copies ran while one was open for 0% of the time, Pallas kernels for 1%

profile of v5, /device:TPU:1, one launch (start us, length us, event | category | flops | bytes accessed | tf_op | source)
XLA Modules:
  0.0 97.4 jit_solution(2577324079066040255)
XLA Ops:
  0.0 0.9 fusion
  0.9 8.8 %collective-permute-start.1 = (f32[16,8,128]{2,1,0:T(8,128)S(1)}, f32[16,8,128]{2,1,0:T(8,128)S(1)}, u32[]{:S(2)}, u32[]{:S(2)}) collective-permute-start(f32[16,8,128]{2,1,0:T(8,128)S(1)} %get-tuple-element.19), channel_id=1, source_target_pairs={{1,0},{2,1},{3,2},{4,3},{5,4},{6,5},{7,6},{8,7},{9,8},{10,9},{11,1... | collective-permute-start | bytes 196616 | tf_op jit(solution)/shard_map/ppermute | solution.py:268
  9.7 1.9 %collective-permute-start = (f32[16,8,128]{2,1,0:T(8,128)S(1)}, f32[16,8,128]{2,1,0:T(8,128)S(1)}, u32[]{:S(2)}, u32[]{:S(2)}) collective-permute-start(f32[16,8,128]{2,1,0:T(8,128)S(1)} %get-tuple-element.20), channel_id=1, source_target_pairs={{0,1},{1,2},{2,3},{3,4},{4,5},{5,6},{6,7},{7,8},{8,9},{9,10},{10,1... | collective-permute-start | bytes 196616 | tf_op jit(solution)/shard_map/ppermute | solution.py:267
  11.7 0.1 copy.14.nb
  11.8 0.6 copy-done.7
  12.4 0.0 copy-done.5
  12.5 0.0 copy-done.6
  12.5 0.0 copy-done.3
  12.5 0.0 copy-done.4
  12.5 1.0 %copy-done = bf16[4,128,512]{2,1,0:T(8,128)(2,1)S(1)} copy-done((bf16[4,128,512]{2,1,0:T(8,128)(2,1)S(1)}, bf16[4,128,512]{2,1,0:T(8,128)(2,1)}, u32[]{:S(2)}) %copy-start) | copy-done | bytes 524312
  13.6 1.0 %copy-done.1 = bf16[4,512,128]{2,1,0:T(8,128)(2,1)S(1)} copy-done((bf16[4,512,128]{2,1,0:T(8,128)(2,1)S(1)}, bf16[4,512,128]{2,1,0:T(8,128)(2,1)}, u32[]{:S(2)}) %copy-start.1) | copy-done | bytes 524312
  14.6 0.8 prepare.1
  15.4 0.0 collective-permute-done.low
  15.4 2.0 %forecast.1 = f32[8,4,16,128]{3,2,1,0:T(8,128)S(1)} custom-call(s32[16,4]{1,0:T(8,128)S(1)} %copy.14.nb, f32[16,16,128]{2,1,0:T(8,128)S(1)} %get-tuple-element.12.own_columns, f32[16,8,128]{2,1,0:T(8,128)S(1)} %collective-permute-done.low, f32[16,8,128]{2,1,0:T(8,128)S(1)} %collective-permute-done.1.high, bf16[4,128,512]{2,1,0:T(8,128)(2,1)S(1)} %get-tuple-element.13.up, ...), custom_call_target="tpu_custom_call" | custom-call | tf_op jit(solution)/shard_map/forecast/pallas_call | solution.py:285
  17.5 14.4 %all_to_all.25.values = f32[8,4,16,128]{3,2,1,0:T(8,128)S(1)} all-to-all(f32[8,4,16,128]{3,2,1,0:T(8,128)S(1)} %forecast.1), channel_id=1, replica_groups=mesh['members'=8,'z'=8,'x'=4,'core'=2] {'members'}, dimensions={0} | all-to-all | bytes 524288 | tf_op jit(solution)/shard_map/all_to_all | solution.py:252
  31.9 0.4 gram.1
  32.2 11.0 %all_to_all.26 = f32[8,7,8,128]{3,2,1,0:T(8,128)S(1)} all-to-all(f32[8,7,8,128]{3,2,1,0:T(8,128)S(1)} %gram.1), channel_id=1, replica_groups=mesh['members'=8,'z'=8,'x'=4,'core'=2] {'x','core'}, dimensions={0} | all-to-all | bytes 458752 | tf_op jit(solution)/shard_map/all_to_all | solution.py:252
  43.3 19.2 %all_to_all.27 = f32[8,7,8,128]{3,2,1,0:T(8,128)S(1)} all-to-all(f32[8,7,8,128]{3,2,1,0:T(8,128)S(1)} %broadcast_in_dim.4), channel_id=1, replica_groups=mesh['members'=8,'z'=8,'x'=4,'core'=2] {'z'}, dimensions={0} | all-to-all | bytes 458752 | tf_op jit(solution)/shard_map/all_to_all | solution.py:252
  62.6 11.4 %all_to_all.28.mine = f32[8,7,8,128]{3,2,1,0:T(8,128)S(1)} all-to-all(f32[8,7,8,128]{3,2,1,0:T(8,128)S(1)} %broadcast_in_dim.5), channel_id=1, replica_groups=mesh['members'=8,'z'=8,'x'=4,'core'=2] {'members'}, dimensions={0} | all-to-all | bytes 458752 | tf_op jit(solution)/shard_map/all_to_all | solution.py:252
  74.0 5.7 %collective-permute-start.2 = (f32[8,7,8,128]{3,2,1,0:T(8,128)S(1)}, f32[8,7,8,128]{3,2,1,0:T(8,128)S(1)}, u32[]{:S(2)}, u32[]{:S(2)}) collective-permute-start(f32[8,7,8,128]{3,2,1,0:T(8,128)S(1)} %all_to_all.28.mine), channel_id=1, source_target_pairs={{0,1},{1,0},{2,3},{3,2},{4,5},{5,4},{6,7},{7,6},{8,9},{9,8},{10,11... | collective-permute-start | bytes 688136 | tf_op jit(solution)/shard_map/ppermute | solution.py:301
  79.7 1.1 %collective-permute-done.2.other = f32[8,7,8,128]{3,2,1,0:T(8,128)S(1)} collective-permute-done((f32[8,7,8,128]{3,2,1,0:T(8,128)S(1)}, f32[8,7,8,128]{3,2,1,0:T(8,128)S(1)}, u32[]{:S(2)}, u32[]{:S(2)}) %collective-permute-start.2) | collective-permute-done | bytes 229408 | tf_op jit(solution)/shard_map/ppermute | solution.py:301
  80.8 5.0 %analysis.1 = f32[8,2,16,128]{3,2,1,0:T(8,128)S(1)} custom-call(f32[8,7,8,128]{3,2,1,0:T(8,128)S(1)} %all_to_all.28.mine, f32[8,7,8,128]{3,2,1,0:T(8,128)S(1)} %collective-permute-done.2.other, f32[8,4,16,128]{3,2,1,0:T(8,128)S(1)} %all_to_all.25.values, f32[4,128]{1,0:T(4,128)S(1)} %copy-done.3), custom_call_target="tpu_custom_call" | custom-call | tf_op jit(solution)/shard_map/analysis/pallas_call | solution.py:303
  85.9 10.8 %all_to_all.29 = f32[8,2,16,128]{3,2,1,0:T(8,128)S(1)} all-to-all(f32[8,2,16,128]{3,2,1,0:T(8,128)S(1)} %analysis.1), channel_id=1, replica_groups=mesh['members'=8,'z'=8,'x'=4,'core'=2] {'members'}, dimensions={0} | all-to-all | bytes 262144 | tf_op jit(solution)/shard_map/all_to_all | solution.py:252
  96.7 0.7 copy.15
  (20 shorter events, 0.1 us)
Async XLA Ops:
  0.0 11.8 %copy-start.2 = (f32[16,16,128]{2,1,0:T(8,128)S(1)}, f32[16,16,128]{2,1,0:T(8,128)}, u32[]{:S(2)}) copy-start(f32[16,16,128]{2,1,0:T(8,128)} %ens.1) | copy-start | bytes 393220
  0.9 10.7 %copy-start.10 = (s32[16,4]{0,1:T(4,128)S(1)}, s32[16,4]{0,1:T(4,128)}, u32[]{:S(2)}) copy-start(s32[16,4]{0,1:T(4,128)} %param.12) | copy-start | bytes 772
  0.9 14.5 %collective-permute-start.1 = (f32[16,8,128]{2,1,0:T(8,128)S(1)}, f32[16,8,128]{2,1,0:T(8,128)S(1)}, u32[]{:S(2)}, u32[]{:S(2)}) collective-permute-start(f32[16,8,128]{2,1,0:T(8,128)S(1)} %get-tuple-element.19), channel_id=1, source_target_pairs={{1,0},{2,1},{3,2},{4,3},{5,4},{6,5},{7,6},{8,7},{9,8},{10,9},{11,1... | collective-permute-start | bytes 196616 | tf_op jit(solution)/shard_map/ppermute | solution.py:268
  9.7 5.7 %collective-permute-start = (f32[16,8,128]{2,1,0:T(8,128)S(1)}, f32[16,8,128]{2,1,0:T(8,128)S(1)}, u32[]{:S(2)}, u32[]{:S(2)}) collective-permute-start(f32[16,8,128]{2,1,0:T(8,128)S(1)} %get-tuple-element.20), channel_id=1, source_target_pairs={{0,1},{1,2},{2,3},{3,4},{4,5},{5,6},{6,7},{7,8},{8,9},{9,10},{10,1... | collective-permute-start | bytes 196616 | tf_op jit(solution)/shard_map/ppermute | solution.py:267
  11.8 0.7 copy-start.7
  11.8 0.7 copy-start.9
  11.8 0.7 copy-start.5
  11.8 0.7 copy-start.6
  11.8 0.7 copy-start.3
  11.8 0.7 copy-start.4
  11.8 0.7 copy-start.8
  12.5 1.0 %copy-start = (bf16[4,128,512]{2,1,0:T(8,128)(2,1)S(1)}, bf16[4,128,512]{2,1,0:T(8,128)(2,1)}, u32[]{:S(2)}) copy-start(bf16[4,128,512]{2,1,0:T(8,128)(2,1)} %up.1) | copy-start | bytes 1572868
  13.6 1.0 %copy-start.1 = (bf16[4,512,128]{2,1,0:T(8,128)(2,1)S(1)}, bf16[4,512,128]{2,1,0:T(8,128)(2,1)}, u32[]{:S(2)}) copy-start(bf16[4,512,128]{2,1,0:T(8,128)(2,1)} %down.1) | copy-start | bytes 1572868
  74.0 6.8 %collective-permute-start.2 = (f32[8,7,8,128]{3,2,1,0:T(8,128)S(1)}, f32[8,7,8,128]{3,2,1,0:T(8,128)S(1)}, u32[]{:S(2)}, u32[]{:S(2)}) collective-permute-start(f32[8,7,8,128]{3,2,1,0:T(8,128)S(1)} %all_to_all.28.mine), channel_id=1, source_target_pairs={{0,1},{1,0},{2,3},{3,2},{4,5},{5,4},{6,7},{7,6},{8,9},{9,8},{10,11... | collective-permute-start | bytes 688136 | tf_op jit(solution)/shard_map/ppermute | solution.py:301

commit v6 on v5

--- a/solution.py
+++ b/solution.py
@@ -72,14 +72,17 @@
 
 
 def forecast_kernel(
-    nb, own_columns, low, high, up, down, one_hot, which_ref, rows_in, place_in,
+    nb, own_columns, inner, outer, up, down, one_hot, which_ref, rows_in, place_in,
     v_out, wide,
 ):
-    band = (lax.axis_index("z") * 4 + lax.axis_index("x")) * 2 + lax.axis_index("core")
+    core = lax.axis_index("core")
+    band = (lax.axis_index("z") * 4 + lax.axis_index("x")) * 2 + core
     wide[HALO:HALO + C] = own_columns[...]
+    inner_at = (1 - core) * (HALO + C)
+    outer_at = core * (HALO + C)
     for c in range(HALO):
-        wide[c] = low[:, c, :]
-        wide[HALO + C + c] = high[:, c, :]
+        wide[inner_at + c] = inner[:, c, :]
+        wide[outer_at + c] = outer[:, c, :]
     start = band * C - HALO
     rows = []
     for c in range(C):
@@ -205,18 +208,20 @@
         zh[2 * size + M:] = vl
         q = dot(zh[0:size], zh[0:size])
         fh[...] = (0.25 * q - 1.5 * zf[...]).astype(BF)
+        if step == 2:
+            new = dot(zh[2 * size:], fh[...])
+            v = 2.25 * v + (new[:M] + new[M:])
+            break
         new = dot(zh[...], fh[...])
         z = 2.25 * zf[...] + (new[0:size] + new[size:2 * size])
         v = 2.25 * v + (new[2 * size:2 * size + M] + new[2 * size + M:])
-    high, low = split2(z)
-    fh[...] = high
-    zh[0:size] = low
     for step in range(2):
         vh, vl = split2(v)
-        both = jnp.concatenate([vh, vl], axis=0)
-        got = dot(both, fh[...])
-        got = got[:M] + (got[M:] + dot(vh, zh[0:size]))
-        v = 1.5 * v - 0.5 * got
+        got = dot(jnp.concatenate([vh, vl], axis=0), zh[0:size])
+        got = got[:M] + (got[M:] + dot(vh, zh[size:2 * size]))
+        th, tl = split2(got)
+        new = dot(jnp.concatenate([th, tl], axis=0), fh[...])
+        v = 1.5 * v - 0.5 * (2.25 * got + (new[:M] + new[M:]))
     v = v * inverse_norm
     blocks = []
     for a in range(L):
@@ -262,10 +267,12 @@
     obs_col, obs_lev, obs_val, obs_err,
 ):
     shape = jax.ShapeDtypeStruct
-    forward = [(n, n + 1) for n in range(63)]
-    backward = [(b, a) for a, b in forward]
-    low = lax.ppermute(ensemble[:, C - HALO:, :], BANDS, forward)
-    high = lax.ppermute(ensemble[:, :HALO, :], BANDS, backward)
+    first = ensemble[:, :HALO, :]
+    last = ensemble[:, C - HALO:, :]
+    even = lax.axis_index("core") == 0
+    apart = [(n, n + 1) for n in range(1, 63, 2)]
+    outer = lax.ppermute(jnp.where(even, first, last), BANDS, apart + [(b, a) for a, b in apart])
+    inner = lax.ppermute(jnp.where(even, last, first), "core", [(0, 1), (1, 0)])
     lev = obs_lev.reshape(1, OBS)
     col = obs_col.reshape(1, OBS)
     val = obs_val.reshape(1, OBS)
@@ -287,7 +294,7 @@
         shape((GROUPS, 4, MD, LEV), F32),
         [pltpu.VMEM((C + 2 * HALO, MD, LEV), F32)],
         10, smem=1, name="forecast",
-    )(neighbours, own, low, high, up, down, one_hot, which, at_obs, place)
+    )(neighbours, own, inner, outer, up, down, one_hot, which, at_obs, place)
     values = swap(values, "members")
     packed = call(
         gram_kernel,

time: 97.8 us -> 97.5 us (level)
  starting transfers between devices: 16.4 us -> 15.2 us
  blocking collectives: 66.9 us -> 67.9 us
    ppermute x2, starting transfers between devices: 10.7 us -> 9.45 us  [the longest x1 4.94 us: per_device(): inner = lax.ppermute(jnp.where(even, last, first), 'core', [(0, 1), (1, 0)])]
    all_to_all x5, blocking collectives: 66.9 us -> 67.9 us  [swap(): return lax.all_to_all(x, axes, split_axis=0, concat_axis=0, tiled=True)]
where the time goes in v6:
time: 97.5 us; the launch traced here: 97.1 us
  blocking collectives  67.9 us (70%)
  starting transfers between devices  15.2 us (16%)
  Pallas kernels  8.17 us (8%)
  local copies, waits for them, and re-layouts  3.63 us (4%)
  waiting for transfers between devices  1.1 us (1%)
    all_to_all x5, blocking collectives, swap(): return lax.all_to_all(x, axes, split_axis=0, concat_axis=0, tiled=True)  67.9 us
    ppermute x1, starting transfers between devices, per_device(): other = lax.ppermute(mine, 'core', [(0, 1), (1, 0)])  5.72 us
    pallas_call x1, Pallas kernels, per_device(): call(analysis_kernel, shape((GROUPS, 2, MD, LEV), F32), [pltpu.VMEM((PACK...  4.97 us
    ppermute x1, starting transfers between devices, per_device(): inner = lax.ppermute(jnp.where(even, last, first), 'core', [(0, 1), (1, 0)])  4.94 us
    ppermute x1, starting transfers between devices, per_device(): lax.ppermute(jnp.where(even, first, last), BANDS, apart + [(b, a) for a,...  4.51 us
    unnamed x23, local copies, waits for them, and re-layouts  2.9 us
    pallas_call x1, Pallas kernels, per_device(): call(forecast_kernel, shape((GROUPS, 4, MD, LEV), F32), [pltpu.VMEM((C +...  2.01 us
  transfers between devices with their start and end apart: 3, of which 1 were waited for; matrix products, arithmetic and copies ran while one was open for 0% of the time, Pallas kernels for 1%

profile of v6, /device:TPU:1, one launch (start us, length us, event | category | flops | bytes accessed | tf_op | source)
XLA Modules:
  0.0 97.1 jit_solution(17735843956107200378)
XLA Ops:
  0.0 0.9 slice_select_fusion
  0.9 4.5 %collective-permute-start.1 = (f32[16,8,128]{2,1,0:T(8,128)S(1)}, f32[16,8,128]{2,1,0:T(8,128)S(1)}, u32[]{:S(2)}, u32[]{:S(2)}) collective-permute-start(f32[16,8,128]{2,1,0:T(8,128)S(1)} %get-tuple-element.19), channel_id=1, source_target_pairs={{1,2},{3,4},{5,6},{7,8},{9,10},{11,12},{13,14},{15,16},{17,18},{19... | collective-permute-start | bytes 196616 | tf_op jit(solution)/shard_map/ppermute | solution.py:274
  5.5 4.9 %collective-permute-start = (f32[16,8,128]{2,1,0:T(8,128)S(1)}, f32[16,8,128]{2,1,0:T(8,128)S(1)}, u32[]{:S(2)}, u32[]{:S(2)}) collective-permute-start(f32[16,8,128]{2,1,0:T(8,128)S(1)} %get-tuple-element.20), channel_id=1, source_target_pairs={{0,1},{1,0},{2,3},{3,2},{4,5},{5,4},{6,7},{7,6},{8,9},{9,8},{10,11... | collective-permute-start | bytes 196616 | tf_op jit(solution)/shard_map/ppermute | solution.py:275
  10.4 0.1 copy.14.nb
  10.6 0.6 copy-done.7
  11.2 0.0 copy-done.5
  11.2 0.0 copy-done.6
  11.2 0.0 copy-done.3
  11.2 0.0 copy-done.4
  11.3 1.0 %copy-done = bf16[4,128,512]{2,1,0:T(8,128)(2,1)S(1)} copy-done((bf16[4,128,512]{2,1,0:T(8,128)(2,1)S(1)}, bf16[4,128,512]{2,1,0:T(8,128)(2,1)}, u32[]{:S(2)}) %copy-start) | copy-done | bytes 524312
  12.3 1.0 %copy-done.1 = bf16[4,512,128]{2,1,0:T(8,128)(2,1)S(1)} copy-done((bf16[4,512,128]{2,1,0:T(8,128)(2,1)S(1)}, bf16[4,512,128]{2,1,0:T(8,128)(2,1)}, u32[]{:S(2)}) %copy-start.1) | copy-done | bytes 524312
  13.3 0.8 prepare.1
  14.2 0.0 collective-permute-done.inner
  14.2 2.0 %forecast.1 = f32[8,4,16,128]{3,2,1,0:T(8,128)S(1)} custom-call(s32[16,4]{1,0:T(8,128)S(1)} %copy.14.nb, f32[16,16,128]{2,1,0:T(8,128)S(1)} %get-tuple-element.12.own_columns, f32[16,8,128]{2,1,0:T(8,128)S(1)} %collective-permute-done.inner, f32[16,8,128]{2,1,0:T(8,128)S(1)} %collective-permute-done.1.outer, bf16[4,128,512]{2,1,0:T(8,128)(2,1)S(1)} %get-tuple-element.13.up, ...), custom_call_target="tpu_custom_call" | custom-call | tf_op jit(solution)/shard_map/forecast/pallas_call | solution.py:292
  16.2 14.3 %all_to_all.25.values = f32[8,4,16,128]{3,2,1,0:T(8,128)S(1)} all-to-all(f32[8,4,16,128]{3,2,1,0:T(8,128)S(1)} %forecast.1), channel_id=1, replica_groups=mesh['members'=8,'z'=8,'x'=4,'core'=2] {'members'}, dimensions={0} | all-to-all | bytes 524288 | tf_op jit(solution)/shard_map/all_to_all | solution.py:257
  30.5 0.4 gram.1
  30.9 13.0 %all_to_all.26 = f32[8,7,8,128]{3,2,1,0:T(8,128)S(1)} all-to-all(f32[8,7,8,128]{3,2,1,0:T(8,128)S(1)} %gram.1), channel_id=1, replica_groups=mesh['members'=8,'z'=8,'x'=4,'core'=2] {'x','core'}, dimensions={0} | all-to-all | bytes 458752 | tf_op jit(solution)/shard_map/all_to_all | solution.py:257
  43.9 18.4 %all_to_all.27 = f32[8,7,8,128]{3,2,1,0:T(8,128)S(1)} all-to-all(f32[8,7,8,128]{3,2,1,0:T(8,128)S(1)} %broadcast_in_dim.4), channel_id=1, replica_groups=mesh['members'=8,'z'=8,'x'=4,'core'=2] {'z'}, dimensions={0} | all-to-all | bytes 458752 | tf_op jit(solution)/shard_map/all_to_all | solution.py:257
  62.3 11.4 %all_to_all.28.mine = f32[8,7,8,128]{3,2,1,0:T(8,128)S(1)} all-to-all(f32[8,7,8,128]{3,2,1,0:T(8,128)S(1)} %broadcast_in_dim.5), channel_id=1, replica_groups=mesh['members'=8,'z'=8,'x'=4,'core'=2] {'members'}, dimensions={0} | all-to-all | bytes 458752 | tf_op jit(solution)/shard_map/all_to_all | solution.py:257
  73.8 5.7 %collective-permute-start.2 = (f32[8,7,8,128]{3,2,1,0:T(8,128)S(1)}, f32[8,7,8,128]{3,2,1,0:T(8,128)S(1)}, u32[]{:S(2)}, u32[]{:S(2)}) collective-permute-start(f32[8,7,8,128]{3,2,1,0:T(8,128)S(1)} %all_to_all.28.mine), channel_id=1, source_target_pairs={{0,1},{1,0},{2,3},{3,2},{4,5},{5,4},{6,7},{7,6},{8,9},{9,8},{10,11... | collective-permute-start | bytes 688136 | tf_op jit(solution)/shard_map/ppermute | solution.py:308
  79.5 1.1 %collective-permute-done.2.other = f32[8,7,8,128]{3,2,1,0:T(8,128)S(1)} collective-permute-done((f32[8,7,8,128]{3,2,1,0:T(8,128)S(1)}, f32[8,7,8,128]{3,2,1,0:T(8,128)S(1)}, u32[]{:S(2)}, u32[]{:S(2)}) %collective-permute-start.2) | collective-permute-done | bytes 229408 | tf_op jit(solution)/shard_map/ppermute | solution.py:308
  80.6 5.0 %analysis.1 = f32[8,2,16,128]{3,2,1,0:T(8,128)S(1)} custom-call(f32[8,7,8,128]{3,2,1,0:T(8,128)S(1)} %all_to_all.28.mine, f32[8,7,8,128]{3,2,1,0:T(8,128)S(1)} %collective-permute-done.2.other, f32[8,4,16,128]{3,2,1,0:T(8,128)S(1)} %all_to_all.25.values, f32[4,128]{1,0:T(4,128)S(1)} %copy-done.3), custom_call_target="tpu_custom_call" | custom-call | tf_op jit(solution)/shard_map/analysis/pallas_call | solution.py:310
  85.6 10.8 %all_to_all.29 = f32[8,2,16,128]{3,2,1,0:T(8,128)S(1)} all-to-all(f32[8,2,16,128]{3,2,1,0:T(8,128)S(1)} %analysis.1), channel_id=1, replica_groups=mesh['members'=8,'z'=8,'x'=4,'core'=2] {'members'}, dimensions={0} | all-to-all | bytes 262144 | tf_op jit(solution)/shard_map/all_to_all | solution.py:257
  96.4 0.7 copy.15
  (20 shorter events, 0.1 us)
Async XLA Ops:
  0.0 10.6 %copy-start.2 = (f32[16,16,128]{2,1,0:T(8,128)S(1)}, f32[16,16,128]{2,1,0:T(8,128)}, u32[]{:S(2)}) copy-start(f32[16,16,128]{2,1,0:T(8,128)} %ens.1) | copy-start | bytes 393220
  0.9 9.5 %copy-start.10 = (s32[16,4]{0,1:T(4,128)S(1)}, s32[16,4]{0,1:T(4,128)}, u32[]{:S(2)}) copy-start(s32[16,4]{0,1:T(4,128)} %param.12) | copy-start | bytes 772
  0.9 13.2 %collective-permute-start.1 = (f32[16,8,128]{2,1,0:T(8,128)S(1)}, f32[16,8,128]{2,1,0:T(8,128)S(1)}, u32[]{:S(2)}, u32[]{:S(2)}) collective-permute-start(f32[16,8,128]{2,1,0:T(8,128)S(1)} %get-tuple-element.19), channel_id=1, source_target_pairs={{1,2},{3,4},{5,6},{7,8},{9,10},{11,12},{13,14},{15,16},{17,18},{19... | collective-permute-start | bytes 196616 | tf_op jit(solution)/shard_map/ppermute | solution.py:274
  5.5 8.7 %collective-permute-start = (f32[16,8,128]{2,1,0:T(8,128)S(1)}, f32[16,8,128]{2,1,0:T(8,128)S(1)}, u32[]{:S(2)}, u32[]{:S(2)}) collective-permute-start(f32[16,8,128]{2,1,0:T(8,128)S(1)} %get-tuple-element.20), channel_id=1, source_target_pairs={{0,1},{1,0},{2,3},{3,2},{4,5},{5,4},{6,7},{7,6},{8,9},{9,8},{10,11... | collective-permute-start | bytes 196616 | tf_op jit(solution)/shard_map/ppermute | solution.py:275
  10.5 0.7 copy-start.7
  10.5 0.7 copy-start.9
  10.5 0.7 copy-start.5
  10.5 0.7 copy-start.6
  10.5 0.7 copy-start.3
  10.5 0.7 copy-start.4
  10.5 0.7 copy-start.8
  11.3 1.0 %copy-start = (bf16[4,128,512]{2,1,0:T(8,128)(2,1)S(1)}, bf16[4,128,512]{2,1,0:T(8,128)(2,1)}, u32[]{:S(2)}) copy-start(bf16[4,128,512]{2,1,0:T(8,128)(2,1)} %up.1) | copy-start | bytes 1572868
  12.3 1.0 %copy-start.1 = (bf16[4,512,128]{2,1,0:T(8,128)(2,1)S(1)}, bf16[4,512,128]{2,1,0:T(8,128)(2,1)}, u32[]{:S(2)}) copy-start(bf16[4,512,128]{2,1,0:T(8,128)(2,1)} %down.1) | copy-start | bytes 1572868
  73.8 6.8 %collective-permute-start.2 = (f32[8,7,8,128]{3,2,1,0:T(8,128)S(1)}, f32[8,7,8,128]{3,2,1,0:T(8,128)S(1)}, u32[]{:S(2)}, u32[]{:S(2)}) collective-permute-start(f32[8,7,8,128]{3,2,1,0:T(8,128)S(1)} %all_to_all.28.mine), channel_id=1, source_target_pairs={{0,1},{1,0},{2,3},{3,2},{4,5},{5,4},{6,7},{7,6},{8,9},{9,8},{10,11... | collective-permute-start | bytes 688136 | tf_op jit(solution)/shard_map/ppermute | solution.py:308

commit v7 on v6

--- a/solution.py
+++ b/solution.py
@@ -49,16 +49,14 @@
 
 
 def prepare_kernel(
-    regime, ens, up, down, col, lev, val, err, modes, gain,
-    own_out, up_out, down_out, hot_out, regs_out, w_out, place_out,
+    regime, ens, col, lev, val, err, modes, gain,
+    own_out, hot_out, regs_out, w_out, place_out,
 ):
     band = (lax.axis_index("z") * 4 + lax.axis_index("x")) * 2 + lax.axis_index("core")
     place_out[...] = col[...] - band * C
     for c in range(C):
         own_out[c] = ens[:, c, :]
         regs_out[c * MD:(c + 1) * MD, :] = jnp.full((MD, LEV), regime[c], jnp.int32)
-    up_out[...] = up[...]
-    down_out[...] = down[...]
     one_hot = (lax.broadcasted_iota(jnp.int32, (LEV, OBS), 0) == lev[...]).astype(F32).astype(BF)
     hot_out[...] = one_hot
     at_obs = None
@@ -240,7 +238,7 @@
         out[:, k] = total.reshape(GROUPS, MD, LEV)
 
 
-def call(kernel, outs, scratch, total, smem=0, name=None):
+def call(kernel, outs, scratch, total, smem=0, name=None, cost=None):
     spaces = [pltpu.SMEM if n < smem else pltpu.VMEM for n in range(total)]
     return pl.pallas_call(
         kernel,
@@ -250,6 +248,7 @@
         scratch_shapes=scratch,
         compiler_params=pltpu.CompilerParams(vmem_limit_bytes=VMEM_LIMIT),
         name=name,
+        cost_estimate=cost,
     )
 
 
@@ -277,16 +276,15 @@
     col = obs_col.reshape(1, OBS)
     val = obs_val.reshape(1, OBS)
     err = obs_err.reshape(1, OBS)
-    own, up, down, one_hot, which, at_obs, place = call(
+    own, one_hot, which, at_obs, place = call(
         prepare_kernel,
         [
-            shape((C, MD, LEV), F32), shape((E, LEV, FF), BF), shape((E, FF, LEV), BF),
-            shape((LEV, OBS), BF), shape((C * MD, LEV), jnp.int32), shape((8, OBS), F32),
+            shape((C, MD, LEV), F32), shape((LEV, OBS), BF), shape((C * MD, LEV), jnp.int32), shape((8, OBS), F32),
             shape((1, OBS), jnp.int32),
         ],
-        [], 10, smem=1, name="prepare",
+        [], 8, smem=1, name="prepare", cost=pl.CostEstimate(flops=1 << 33, bytes_accessed=1 << 20, transcendentals=0),
     )(
-        regime, ensemble, up_weight, down_weight, col, lev, val, err, vertical_modes,
+        regime, ensemble, col, lev, val, err, vertical_modes,
         norm_gain.reshape(1, LEV),
     )
     values = call(
@@ -294,7 +292,7 @@
         shape((GROUPS, 4, MD, LEV), F32),
         [pltpu.VMEM((C + 2 * HALO, MD, LEV), F32)],
         10, smem=1, name="forecast",
-    )(neighbours, own, inner, outer, up, down, one_hot, which, at_obs, place)
+    )(neighbours, own, inner, outer, up_weight, down_weight, one_hot, which, at_obs, place)
     values = swap(values, "members")
     packed = call(
         gram_kernel,

time: 97.5 us -> 95.8 us (0.983)
  local copies, waits for them, and re-layouts: 3.63 us -> 1.87 us
    unnamed x23, local copies, waits for them, and re-layouts: 2.9 us -> 1.14 us
where the time goes in v7:
time: 95.8 us; the launch traced here: 95.4 us
  blocking collectives  68 us (71%)
  starting transfers between devices  15.2 us (16%)
  Pallas kernels  8.1 us (8%)
  local copies, waits for them, and re-layouts  1.87 us (2%)
  waiting for transfers between devices  1.1 us (1%)
  other arithmetic  0.96 us (1%)
    all_to_all x5, blocking collectives, swap(): return lax.all_to_all(x, axes, split_axis=0, concat_axis=0, tiled=True)  68 us
    ppermute x1, starting transfers between devices, per_device(): other = lax.ppermute(mine, 'core', [(0, 1), (1, 0)])  5.72 us
    pallas_call x1, Pallas kernels, per_device(): call(analysis_kernel, shape((GROUPS, 2, MD, LEV), F32), [pltpu.VMEM((PACK...  4.98 us
    ppermute x1, starting transfers between devices, per_device(): inner = lax.ppermute(jnp.where(even, last, first), 'core', [(0, 1), (1, 0)])  4.94 us
    ppermute x1, starting transfers between devices, per_device(): lax.ppermute(jnp.where(even, first, last), BANDS, apart + [(b, a) for a,...  4.51 us
    pallas_call x1, Pallas kernels, per_device(): call(forecast_kernel, shape((GROUPS, 4, MD, LEV), F32), [pltpu.VMEM((C +...  1.99 us
  transfers between devices with their start and end apart: 3, of which 1 were waited for; matrix products, arithmetic and copies ran while one was open for 0% of the time, Pallas kernels for 1%

profile of v7, /device:TPU:1, one launch (start us, length us, event | category | flops | bytes accessed | tf_op | source)
XLA Modules:
  0.0 95.4 jit_solution(13211043256815853521)
XLA Ops:
  0.0 0.9 slice_select_fusion
  0.9 4.5 %collective-permute-start.1 = (f32[16,8,128]{2,1,0:T(8,128)S(1)}, f32[16,8,128]{2,1,0:T(8,128)S(1)}, u32[]{:S(2)}, u32[]{:S(2)}) collective-permute-start(f32[16,8,128]{2,1,0:T(8,128)S(1)} %get-tuple-element.15), channel_id=1, source_target_pairs={{1,2},{3,4},{5,6},{7,8},{9,10},{11,12},{13,14},{15,16},{17,18},{19... | collective-permute-start | bytes 196616 | tf_op jit(solution)/shard_map/ppermute | solution.py:273
  5.4 4.9 %collective-permute-start = (f32[16,8,128]{2,1,0:T(8,128)S(1)}, f32[16,8,128]{2,1,0:T(8,128)S(1)}, u32[]{:S(2)}, u32[]{:S(2)}) collective-permute-start(f32[16,8,128]{2,1,0:T(8,128)S(1)} %get-tuple-element.16), channel_id=1, source_target_pairs={{0,1},{1,0},{2,3},{3,2},{4,5},{5,4},{6,7},{7,6},{8,9},{9,8},{10,11... | collective-permute-start | bytes 196616 | tf_op jit(solution)/shard_map/ppermute | solution.py:274
  10.4 0.0 copy-start.9
  10.5 0.6 copy-done.7
  11.1 0.0 copy-done.5
  11.1 0.0 copy-done.6
  11.1 0.0 copy-done.3
  11.1 0.0 copy-done.4
  11.2 0.8 prepare.1
  11.9 0.1 copy.14.nb
  12.0 0.2 copy-done
  12.2 0.2 copy-done.1
  12.4 2.0 %forecast.1 = f32[8,4,16,128]{3,2,1,0:T(8,128)S(1)} custom-call(s32[16,4]{1,0:T(8,128)S(1)} %copy.14.nb, f32[16,16,128]{2,1,0:T(8,128)S(1)} %get-tuple-element.10.own_columns, f32[16,8,128]{2,1,0:T(8,128)S(1)} %collective-permute-done.inner, f32[16,8,128]{2,1,0:T(8,128)S(1)} %collective-permute-done.1.outer, bf16[4,128,512]{2,1,0:T(8,128)(2,1)S(1)} %copy-done, ...), custom_call_target="tpu_custom_call" | custom-call | tf_op jit(solution)/shard_map/forecast/pallas_call | solution.py:290
  14.4 14.3 %all_to_all.25.values = f32[8,4,16,128]{3,2,1,0:T(8,128)S(1)} all-to-all(f32[8,4,16,128]{3,2,1,0:T(8,128)S(1)} %forecast.1), channel_id=1, replica_groups=mesh['members'=8,'z'=8,'x'=4,'core'=2] {'members'}, dimensions={0} | all-to-all | bytes 524288 | tf_op jit(solution)/shard_map/all_to_all | solution.py:256
  28.7 0.4 gram.1
  29.0 13.0 %all_to_all.26 = f32[8,7,8,128]{3,2,1,0:T(8,128)S(1)} all-to-all(f32[8,7,8,128]{3,2,1,0:T(8,128)S(1)} %gram.1), channel_id=1, replica_groups=mesh['members'=8,'z'=8,'x'=4,'core'=2] {'x','core'}, dimensions={0} | all-to-all | bytes 458752 | tf_op jit(solution)/shard_map/all_to_all | solution.py:256
  42.0 18.6 %all_to_all.27 = f32[8,7,8,128]{3,2,1,0:T(8,128)S(1)} all-to-all(f32[8,7,8,128]{3,2,1,0:T(8,128)S(1)} %broadcast_in_dim.4), channel_id=1, replica_groups=mesh['members'=8,'z'=8,'x'=4,'core'=2] {'z'}, dimensions={0} | all-to-all | bytes 458752 | tf_op jit(solution)/shard_map/all_to_all | solution.py:256
  60.6 11.4 %all_to_all.28.mine = f32[8,7,8,128]{3,2,1,0:T(8,128)S(1)} all-to-all(f32[8,7,8,128]{3,2,1,0:T(8,128)S(1)} %broadcast_in_dim.5), channel_id=1, replica_groups=mesh['members'=8,'z'=8,'x'=4,'core'=2] {'members'}, dimensions={0} | all-to-all | bytes 458752 | tf_op jit(solution)/shard_map/all_to_all | solution.py:256
  72.1 5.7 %collective-permute-start.2 = (f32[8,7,8,128]{3,2,1,0:T(8,128)S(1)}, f32[8,7,8,128]{3,2,1,0:T(8,128)S(1)}, u32[]{:S(2)}, u32[]{:S(2)}) collective-permute-start(f32[8,7,8,128]{3,2,1,0:T(8,128)S(1)} %all_to_all.28.mine), channel_id=1, source_target_pairs={{0,1},{1,0},{2,3},{3,2},{4,5},{5,4},{6,7},{7,6},{8,9},{9,8},{10,11... | collective-permute-start | bytes 688136 | tf_op jit(solution)/shard_map/ppermute | solution.py:306
  77.8 1.1 %collective-permute-done.2.other = f32[8,7,8,128]{3,2,1,0:T(8,128)S(1)} collective-permute-done((f32[8,7,8,128]{3,2,1,0:T(8,128)S(1)}, f32[8,7,8,128]{3,2,1,0:T(8,128)S(1)}, u32[]{:S(2)}, u32[]{:S(2)}) %collective-permute-start.2) | collective-permute-done | bytes 229408 | tf_op jit(solution)/shard_map/ppermute | solution.py:306
  78.9 5.0 %analysis.1 = f32[8,2,16,128]{3,2,1,0:T(8,128)S(1)} custom-call(f32[8,7,8,128]{3,2,1,0:T(8,128)S(1)} %all_to_all.28.mine, f32[8,7,8,128]{3,2,1,0:T(8,128)S(1)} %collective-permute-done.2.other, f32[8,4,16,128]{3,2,1,0:T(8,128)S(1)} %all_to_all.25.values, f32[4,128]{1,0:T(4,128)S(1)} %copy-done.3), custom_call_target="tpu_custom_call" | custom-call | tf_op jit(solution)/shard_map/analysis/pallas_call | solution.py:308
  83.9 10.8 %all_to_all.29 = f32[8,2,16,128]{3,2,1,0:T(8,128)S(1)} all-to-all(f32[8,2,16,128]{3,2,1,0:T(8,128)S(1)} %analysis.1), channel_id=1, replica_groups=mesh['members'=8,'z'=8,'x'=4,'core'=2] {'members'}, dimensions={0} | all-to-all | bytes 262144 | tf_op jit(solution)/shard_map/all_to_all | solution.py:256
  94.7 0.7 copy.15
  (20 shorter events, 0.1 us)
Async XLA Ops:
  0.0 10.5 %copy-start.2 = (f32[16,16,128]{2,1,0:T(8,128)S(1)}, f32[16,16,128]{2,1,0:T(8,128)}, u32[]{:S(2)}) copy-start(f32[16,16,128]{2,1,0:T(8,128)} %ens.1) | copy-start | bytes 393220
  0.9 11.1 %collective-permute-start.1 = (f32[16,8,128]{2,1,0:T(8,128)S(1)}, f32[16,8,128]{2,1,0:T(8,128)S(1)}, u32[]{:S(2)}, u32[]{:S(2)}) collective-permute-start(f32[16,8,128]{2,1,0:T(8,128)S(1)} %get-tuple-element.15), channel_id=1, source_target_pairs={{1,2},{3,4},{5,6},{7,8},{9,10},{11,12},{13,14},{15,16},{17,18},{19... | collective-permute-start | bytes 196616 | tf_op jit(solution)/shard_map/ppermute | solution.py:273
  5.4 6.6 %collective-permute-start = (f32[16,8,128]{2,1,0:T(8,128)S(1)}, f32[16,8,128]{2,1,0:T(8,128)S(1)}, u32[]{:S(2)}, u32[]{:S(2)}) collective-permute-start(f32[16,8,128]{2,1,0:T(8,128)S(1)} %get-tuple-element.16), channel_id=1, source_target_pairs={{0,1},{1,0},{2,3},{3,2},{4,5},{5,4},{6,7},{7,6},{8,9},{9,8},{10,11... | collective-permute-start | bytes 196616 | tf_op jit(solution)/shard_map/ppermute | solution.py:274
  10.4 0.7 copy-start.7
  10.4 0.7 copy-start.9
  10.4 0.7 copy-start.5
  10.4 0.7 copy-start.6
  10.4 0.7 copy-start.3
  10.5 0.7 copy-start.4
  10.5 0.7 copy-start.8
  11.2 0.8 copy-start.10
  11.2 1.1 %copy-start = (bf16[4,128,512]{2,1,0:T(8,128)(2,1)S(1)}, bf16[4,128,512]{2,1,0:T(8,128)(2,1)}, u32[]{:S(2)}) copy-start(bf16[4,128,512]{2,1,0:T(8,128)(2,1)} %up.1) | copy-start | bytes 1572868
  11.2 1.2 %copy-start.1 = (bf16[4,512,128]{2,1,0:T(8,128)(2,1)S(1)}, bf16[4,512,128]{2,1,0:T(8,128)(2,1)}, u32[]{:S(2)}) copy-start(bf16[4,512,128]{2,1,0:T(8,128)(2,1)} %down.1) | copy-start | bytes 1572868
  72.1 6.8 %collective-permute-start.2 = (f32[8,7,8,128]{3,2,1,0:T(8,128)S(1)}, f32[8,7,8,128]{3,2,1,0:T(8,128)S(1)}, u32[]{:S(2)}, u32[]{:S(2)}) collective-permute-start(f32[8,7,8,128]{3,2,1,0:T(8,128)S(1)} %all_to_all.28.mine), channel_id=1, source_target_pairs={{0,1},{1,0},{2,3},{3,2},{4,5},{5,4},{6,7},{7,6},{8,9},{9,8},{10,11... | collective-permute-start | bytes 688136 | tf_op jit(solution)/shard_map/ppermute | solution.py:306

commit v8 on v7

--- a/solution.py
+++ b/solution.py
@@ -49,13 +49,12 @@
 
 
 def prepare_kernel(
-    regime, ens, col, lev, val, err, modes, gain,
-    own_out, hot_out, regs_out, w_out, place_out,
+    regime, col, lev, val, err, modes, gain,
+    hot_out, regs_out, w_out, place_out,
 ):
     band = (lax.axis_index("z") * 4 + lax.axis_index("x")) * 2 + lax.axis_index("core")
     place_out[...] = col[...] - band * C
     for c in range(C):
-        own_out[c] = ens[:, c, :]
         regs_out[c * MD:(c + 1) * MD, :] = jnp.full((MD, LEV), regime[c], jnp.int32)
     one_hot = (lax.broadcasted_iota(jnp.int32, (LEV, OBS), 0) == lev[...]).astype(F32).astype(BF)
     hot_out[...] = one_hot
@@ -70,24 +69,27 @@
 
 
 def forecast_kernel(
-    nb, own_columns, inner, outer, up, down, one_hot, which_ref, rows_in, place_in,
-    v_out, wide,
+    nb, ens, inner, outer, up, down, one_hot, which_ref, rows_in, place_in,
+    v_out, wide, halves,
 ):
     core = lax.axis_index("core")
     band = (lax.axis_index("z") * 4 + lax.axis_index("x")) * 2 + core
-    wide[HALO:HALO + C] = own_columns[...]
+    for c in range(C):
+        wide[HALO + c] = ens[:, c, :]
     inner_at = (1 - core) * (HALO + C)
     outer_at = core * (HALO + C)
+    halves[0] = inner[:, pl.ds(pl.multiple_of(core * HALO, HALO), HALO), :]
+    halves[1] = outer[:, pl.ds(pl.multiple_of((1 - core) * HALO, HALO), HALO), :]
     for c in range(HALO):
-        wide[inner_at + c] = inner[:, c, :]
-        wide[outer_at + c] = outer[:, c, :]
+        wide[inner_at + c] = halves[0, :, c, :]
+        wide[outer_at + c] = halves[1, :, c, :]
     start = band * C - HALO
     rows = []
     for c in range(C):
         total = wide[nb[c, 0] - start]
         for k in range(1, NB):
             total = total + wide[nb[c, k] - start]
-        own = own_columns[c]
+        own = wide[HALO + c]
         rows.append(own + 0.5 * (0.25 * total - own))
     flat = jnp.concatenate(rows, axis=0)
     inv_rms = lax.rsqrt(jnp.mean(flat * flat, axis=1, keepdims=True) + 1e-05)
@@ -266,33 +268,30 @@
     obs_col, obs_lev, obs_val, obs_err,
 ):
     shape = jax.ShapeDtypeStruct
-    first = ensemble[:, :HALO, :]
-    last = ensemble[:, C - HALO:, :]
-    even = lax.axis_index("core") == 0
     apart = [(n, n + 1) for n in range(1, 63, 2)]
-    outer = lax.ppermute(jnp.where(even, first, last), BANDS, apart + [(b, a) for a, b in apart])
-    inner = lax.ppermute(jnp.where(even, last, first), "core", [(0, 1), (1, 0)])
+    outer = lax.ppermute(ensemble, BANDS, apart + [(b, a) for a, b in apart])
+    inner = lax.ppermute(ensemble, "core", [(0, 1), (1, 0)])
     lev = obs_lev.reshape(1, OBS)
     col = obs_col.reshape(1, OBS)
     val = obs_val.reshape(1, OBS)
     err = obs_err.reshape(1, OBS)
-    own, one_hot, which, at_obs, place = call(
+    one_hot, which, at_obs, place = call(
         prepare_kernel,
         [
-            shape((C, MD, LEV), F32), shape((LEV, OBS), BF), shape((C * MD, LEV), jnp.int32), shape((8, OBS), F32),
+            shape((LEV, OBS), BF), shape((C * MD, LEV), jnp.int32), shape((8, OBS), F32),
             shape((1, OBS), jnp.int32),
         ],
-        [], 8, smem=1, name="prepare", cost=pl.CostEstimate(flops=1 << 33, bytes_accessed=1 << 20, transcendentals=0),
+        [], 7, smem=1, name="prepare", cost=pl.CostEstimate(flops=1 << 33, bytes_accessed=1 << 20, transcendentals=0),
     )(
-        regime, ensemble, col, lev, val, err, vertical_modes,
+        regime, col, lev, val, err, vertical_modes,
         norm_gain.reshape(1, LEV),
     )
     values = call(
         forecast_kernel,
         shape((GROUPS, 4, MD, LEV), F32),
-        [pltpu.VMEM((C + 2 * HALO, MD, LEV), F32)],
+        [pltpu.VMEM((C + 2 * HALO, MD, LEV), F32), pltpu.VMEM((2, MD, HALO, LEV), F32)],
         10, smem=1, name="forecast",
-    )(neighbours, own, inner, outer, up_weight, down_weight, one_hot, which, at_obs, place)
+    )(neighbours, ensemble, inner, outer, up_weight, down_weight, one_hot, which, at_obs, place)
     values = swap(values, "members")
     packed = call(
         gram_kernel,

time: 95.8 us -> 96.5 us (level)
  waiting for transfers between devices: 1.1 us -> 4.11 us
  blocking collectives: 68 us -> 65.8 us
  starting transfers between devices: 15.2 us -> 16.4 us
    ppermute x2, waiting for transfers between devices: 0.01 us -> 3.01 us  [the longest x1 3.01 us: per_device(): outer = lax.ppermute(ensemble, BANDS, apart + [(b, a) for a, b in apart])]
    all_to_all x5, blocking collectives: 68 us -> 65.8 us  [swap(): return lax.all_to_all(x, axes, split_axis=0, concat_axis=0, tiled=True)]
    ppermute x2, starting transfers between devices: 9.45 us -> 10.7 us  [the longest x1 8.77 us: per_device(): inner = lax.ppermute(ensemble, 'core', [(0, 1), (1, 0)])]
  transfers between devices with their start and end apart: 3 -> 3, of which waited for: 1 -> 2; matrix products, arithmetic and copies ran while one was open for 0% -> 0% of each run, Pallas kernels for 1% -> 1%
where the time goes in v8:
time: 96.5 us; the launch traced here: 96.1 us
  blocking collectives  65.8 us (68%)
  starting transfers between devices  16.4 us (17%)
  Pallas kernels  8.08 us (8%)
  waiting for transfers between devices  4.11 us (4%)
  local copies, waits for them, and re-layouts  1.54 us (2%)
    all_to_all x5, blocking collectives, swap(): return lax.all_to_all(x, axes, split_axis=0, concat_axis=0, tiled=True)  65.8 us
    ppermute x1, starting transfers between devices, per_device(): inner = lax.ppermute(ensemble, 'core', [(0, 1), (1, 0)])  8.77 us
    ppermute x1, starting transfers between devices, per_device(): other = lax.ppermute(mine, 'core', [(0, 1), (1, 0)])  5.72 us
    pallas_call x1, Pallas kernels, per_device(): call(analysis_kernel, shape((GROUPS, 2, MD, LEV), F32), [pltpu.VMEM((PACK...  4.97 us
    ppermute x1, waiting for transfers between devices, per_device(): outer = lax.ppermute(ensemble, BANDS, apart + [(b, a) for a, b in apart])  3.01 us
    pallas_call x1, Pallas kernels, per_device(): call(forecast_kernel, shape((GROUPS, 4, MD, LEV), F32), [pltpu.VMEM((C +...  2.06 us
  transfers between devices with their start and end apart: 3, of which 2 were waited for; matrix products, arithmetic and copies ran while one was open for 0% of the time, Pallas kernels for 1%

profile of v8, /device:TPU:1, one launch (start us, length us, event | category | flops | bytes accessed | tf_op | source)
XLA Modules:
  0.0 96.1 jit_solution(5595017412677411284)
XLA Ops:
  0.0 8.8 %collective-permute-start = (f32[16,16,128]{2,1,0:T(8,128)}, f32[16,16,128]{2,1,0:T(8,128)S(1)}, u32[]{:S(2)}, u32[]{:S(2)}) collective-permute-start(f32[16,16,128]{2,1,0:T(8,128)} %ens.1), channel_id=1, source_target_pairs={{0,1},{1,0},{2,3},{3,2},{4,5},{5,4},{6,7},{7,6},{8,9},{9,8},{10,11... | collective-permute-start | bytes 393224 | tf_op jit(solution)/shard_map/ppermute | solution.py:273
  8.8 1.9 %collective-permute-start.1 = (f32[16,16,128]{2,1,0:T(8,128)}, f32[16,16,128]{2,1,0:T(8,128)S(1)}, u32[]{:S(2)}, u32[]{:S(2)}) collective-permute-start(f32[16,16,128]{2,1,0:T(8,128)} %ens.1), channel_id=1, source_target_pairs={{1,2},{3,4},{5,6},{7,8},{9,10},{11,12},{13,14},{15,16},{17,18},{19... | collective-permute-start | bytes 393224 | tf_op jit(solution)/shard_map/ppermute | solution.py:272
  10.7 0.0 copy-start.7
  10.7 0.0 copy-start.9
  10.8 0.6 copy-done.7
  11.4 0.0 copy-done.5
  11.4 0.0 copy-done.6
  11.4 0.0 copy-done.3
  11.5 0.0 copy-done.4
  11.5 0.7 prepare.1
  12.2 0.1 copy.14.nb
  12.3 0.0 collective-permute-done.inner
  12.3 3.0 %collective-permute-done.1.outer = f32[16,16,128]{2,1,0:T(8,128)S(1)} collective-permute-done((f32[16,16,128]{2,1,0:T(8,128)}, f32[16,16,128]{2,1,0:T(8,128)S(1)}, u32[]{:S(2)}, u32[]{:S(2)}) %collective-permute-start.1) | collective-permute-done | bytes 131104 | tf_op jit(solution)/shard_map/ppermute | solution.py:272
  15.3 2.1 %forecast.1 = f32[8,4,16,128]{3,2,1,0:T(8,128)S(1)} custom-call(s32[16,4]{1,0:T(8,128)S(1)} %copy.14.nb, f32[16,16,128]{2,1,0:T(8,128)S(1)} %copy-done.2, f32[16,16,128]{2,1,0:T(8,128)S(1)} %collective-permute-done.inner, f32[16,16,128]{2,1,0:T(8,128)S(1)} %collective-permute-done.1.outer, bf16[4,128,512]{2,1,0:T(8,128)(2,1)S(1)} %copy-done, ...), custom_call_target="tpu_custom_call" | custom-call | tf_op jit(solution)/shard_map/forecast/pallas_call | solution.py:289
  17.4 11.7 %all_to_all.25.values = f32[8,4,16,128]{3,2,1,0:T(8,128)S(1)} all-to-all(f32[8,4,16,128]{3,2,1,0:T(8,128)S(1)} %forecast.1), channel_id=1, replica_groups=mesh['members'=8,'z'=8,'x'=4,'core'=2] {'members'}, dimensions={0} | all-to-all | bytes 524288 | tf_op jit(solution)/shard_map/all_to_all | solution.py:258
  29.1 0.4 gram.1
  29.5 12.6 %all_to_all.26 = f32[8,7,8,128]{3,2,1,0:T(8,128)S(1)} all-to-all(f32[8,7,8,128]{3,2,1,0:T(8,128)S(1)} %gram.1), channel_id=1, replica_groups=mesh['members'=8,'z'=8,'x'=4,'core'=2] {'x','core'}, dimensions={0} | all-to-all | bytes 458752 | tf_op jit(solution)/shard_map/all_to_all | solution.py:258
  42.1 19.2 %all_to_all.27 = f32[8,7,8,128]{3,2,1,0:T(8,128)S(1)} all-to-all(f32[8,7,8,128]{3,2,1,0:T(8,128)S(1)} %broadcast_in_dim.4), channel_id=1, replica_groups=mesh['members'=8,'z'=8,'x'=4,'core'=2] {'z'}, dimensions={0} | all-to-all | bytes 458752 | tf_op jit(solution)/shard_map/all_to_all | solution.py:258
  61.4 11.4 %all_to_all.28.mine = f32[8,7,8,128]{3,2,1,0:T(8,128)S(1)} all-to-all(f32[8,7,8,128]{3,2,1,0:T(8,128)S(1)} %broadcast_in_dim.5), channel_id=1, replica_groups=mesh['members'=8,'z'=8,'x'=4,'core'=2] {'members'}, dimensions={0} | all-to-all | bytes 458752 | tf_op jit(solution)/shard_map/all_to_all | solution.py:258
  72.9 5.7 %collective-permute-start.2 = (f32[8,7,8,128]{3,2,1,0:T(8,128)S(1)}, f32[8,7,8,128]{3,2,1,0:T(8,128)S(1)}, u32[]{:S(2)}, u32[]{:S(2)}) collective-permute-start(f32[8,7,8,128]{3,2,1,0:T(8,128)S(1)} %all_to_all.28.mine), channel_id=1, source_target_pairs={{0,1},{1,0},{2,3},{3,2},{4,5},{5,4},{6,7},{7,6},{8,9},{9,8},{10,11... | collective-permute-start | bytes 688136 | tf_op jit(solution)/shard_map/ppermute | solution.py:305
  78.6 1.1 %collective-permute-done.2.other = f32[8,7,8,128]{3,2,1,0:T(8,128)S(1)} collective-permute-done((f32[8,7,8,128]{3,2,1,0:T(8,128)S(1)}, f32[8,7,8,128]{3,2,1,0:T(8,128)S(1)}, u32[]{:S(2)}, u32[]{:S(2)}) %collective-permute-start.2) | collective-permute-done | bytes 229408 | tf_op jit(solution)/shard_map/ppermute | solution.py:305
  79.7 5.0 %analysis.1 = f32[8,2,16,128]{3,2,1,0:T(8,128)S(1)} custom-call(f32[8,7,8,128]{3,2,1,0:T(8,128)S(1)} %all_to_all.28.mine, f32[8,7,8,128]{3,2,1,0:T(8,128)S(1)} %collective-permute-done.2.other, f32[8,4,16,128]{3,2,1,0:T(8,128)S(1)} %all_to_all.25.values, f32[4,128]{1,0:T(4,128)S(1)} %copy-done.3), custom_call_target="tpu_custom_call" | custom-call | tf_op jit(solution)/shard_map/analysis/pallas_call | solution.py:307
  84.7 10.8 %all_to_all.29 = f32[8,2,16,128]{3,2,1,0:T(8,128)S(1)} all-to-all(f32[8,2,16,128]{3,2,1,0:T(8,128)S(1)} %analysis.1), channel_id=1, replica_groups=mesh['members'=8,'z'=8,'x'=4,'core'=2] {'members'}, dimensions={0} | all-to-all | bytes 262144 | tf_op jit(solution)/shard_map/all_to_all | solution.py:258
  95.5 0.7 copy.15
  (19 shorter events, 0.1 us)
Async XLA Ops:
  0.0 12.3 %collective-permute-start = (f32[16,16,128]{2,1,0:T(8,128)}, f32[16,16,128]{2,1,0:T(8,128)S(1)}, u32[]{:S(2)}, u32[]{:S(2)}) collective-permute-start(f32[16,16,128]{2,1,0:T(8,128)} %ens.1), channel_id=1, source_target_pairs={{0,1},{1,0},{2,3},{3,2},{4,5},{5,4},{6,7},{7,6},{8,9},{9,8},{10,11... | collective-permute-start | bytes 393224 | tf_op jit(solution)/shard_map/ppermute | solution.py:273
  8.8 6.5 %collective-permute-start.1 = (f32[16,16,128]{2,1,0:T(8,128)}, f32[16,16,128]{2,1,0:T(8,128)S(1)}, u32[]{:S(2)}, u32[]{:S(2)}) collective-permute-start(f32[16,16,128]{2,1,0:T(8,128)} %ens.1), channel_id=1, source_target_pairs={{1,2},{3,4},{5,6},{7,8},{9,10},{11,12},{13,14},{15,16},{17,18},{19... | collective-permute-start | bytes 393224 | tf_op jit(solution)/shard_map/ppermute | solution.py:272
  10.7 0.7 copy-start.7
  10.7 0.7 copy-start.9
  10.7 0.7 copy-start.5
  10.7 0.7 copy-start.6
  10.8 0.7 copy-start.3
  10.8 0.7 copy-start.4
  10.8 0.7 copy-start.8
  11.5 0.7 copy-start.10
  11.5 3.8 %copy-start = (bf16[4,128,512]{2,1,0:T(8,128)(2,1)S(1)}, bf16[4,128,512]{2,1,0:T(8,128)(2,1)}, u32[]{:S(2)}) copy-start(bf16[4,128,512]{2,1,0:T(8,128)(2,1)} %up.1) | copy-start | bytes 1572868
  11.5 3.8 %copy-start.1 = (bf16[4,512,128]{2,1,0:T(8,128)(2,1)S(1)}, bf16[4,512,128]{2,1,0:T(8,128)(2,1)}, u32[]{:S(2)}) copy-start(bf16[4,512,128]{2,1,0:T(8,128)(2,1)} %down.1) | copy-start | bytes 1572868
  11.5 3.8 %copy-start.2 = (f32[16,16,128]{2,1,0:T(8,128)S(1)}, f32[16,16,128]{2,1,0:T(8,128)}, u32[]{:S(2)}) copy-start(f32[16,16,128]{2,1,0:T(8,128)} %ens.1) | copy-start | bytes 393220
  72.9 6.8 %collective-permute-start.2 = (f32[8,7,8,128]{3,2,1,0:T(8,128)S(1)}, f32[8,7,8,128]{3,2,1,0:T(8,128)S(1)}, u32[]{:S(2)}, u32[]{:S(2)}) collective-permute-start(f32[8,7,8,128]{3,2,1,0:T(8,128)S(1)} %all_to_all.28.mine), channel_id=1, source_target_pairs={{0,1},{1,0},{2,3},{3,2},{4,5},{5,4},{6,7},{7,6},{8,9},{9,8},{10,11... | collective-permute-start | bytes 688136 | tf_op jit(solution)/shard_map/ppermute | solution.py:305

commit v9 on v8

--- a/solution.py
+++ b/solution.py
@@ -69,7 +69,7 @@
 
 
 def forecast_kernel(
-    nb, ens, inner, outer, up, down, one_hot, which_ref, rows_in, place_in,
+    nb, ens, outer, inner, up, down, one_hot, which_ref, rows_in, place_in,
     v_out, wide, halves,
 ):
     core = lax.axis_index("core")
@@ -291,7 +291,7 @@
         shape((GROUPS, 4, MD, LEV), F32),
         [pltpu.VMEM((C + 2 * HALO, MD, LEV), F32), pltpu.VMEM((2, MD, HALO, LEV), F32)],
         10, smem=1, name="forecast",
-    )(neighbours, ensemble, inner, outer, up_weight, down_weight, one_hot, which, at_obs, place)
+    )(neighbours, ensemble, outer, inner, up_weight, down_weight, one_hot, which, at_obs, place)
     values = swap(values, "members")
     packed = call(
         gram_kernel,

time: 96.5 us -> 95.8 us (level)
  blocking collectives: 65.8 us -> 68.9 us
  waiting for transfers between devices: 4.11 us -> 1.1 us
  starting transfers between devices: 16.4 us -> 15.2 us
    ppermute x1, starting transfers between devices: 8.77 us -> 4.95 us  [per_device(): inner = lax.ppermute(ensemble, 'core', [(0, 1), (1, 0)])]
    all_to_all x5, blocking collectives: 65.8 us -> 68.9 us  [swap(): return lax.all_to_all(x, axes, split_axis=0, concat_axis=0, tiled=True)]
    ppermute x1, waiting for transfers between devices: 3.01 us -> 0.01 us  [per_device(): outer = lax.ppermute(ensemble, BANDS, apart + [(b, a) for a, b in apart])]
    ppermute x1, starting transfers between devices: 1.92 us -> 4.5 us  [per_device(): outer = lax.ppermute(ensemble, BANDS, apart + [(b, a) for a, b in apart])]
  transfers between devices with their start and end apart: 3 -> 3, of which waited for: 2 -> 1; matrix products, arithmetic and copies ran while one was open for 0% -> 0% of each run, Pallas kernels for 1% -> 1%
where the time goes in v9:
time: 95.8 us; the launch traced here: 95.4 us
  blocking collectives  68.9 us (72%)
  starting transfers between devices  15.2 us (16%)
  Pallas kernels  8.09 us (8%)
  local copies, waits for them, and re-layouts  1.97 us (2%)
  waiting for transfers between devices  1.1 us (1%)
    all_to_all x5, blocking collectives, swap(): return lax.all_to_all(x, axes, split_axis=0, concat_axis=0, tiled=True)  68.9 us
    ppermute x1, starting transfers between devices, per_device(): other = lax.ppermute(mine, 'core', [(0, 1), (1, 0)])  5.72 us
    pallas_call x1, Pallas kernels, per_device(): call(analysis_kernel, shape((GROUPS, 2, MD, LEV), F32), [pltpu.VMEM((PACK...  4.99 us
    ppermute x1, starting transfers between devices, per_device(): inner = lax.ppermute(ensemble, 'core', [(0, 1), (1, 0)])  4.95 us
    ppermute x1, starting transfers between devices, per_device(): outer = lax.ppermute(ensemble, BANDS, apart + [(b, a) for a, b in apart])  4.5 us
    pallas_call x1, Pallas kernels, per_device(): call(forecast_kernel, shape((GROUPS, 4, MD, LEV), F32), [pltpu.VMEM((C +...  2.06 us
  transfers between devices with their start and end apart: 3, of which 1 were waited for; matrix products, arithmetic and copies ran while one was open for 0% of the time, Pallas kernels for 1%

profile of v9, /device:TPU:1, one launch (start us, length us, event | category | flops | bytes accessed | tf_op | source)
XLA Modules:
  0.0 95.4 jit_solution(6277034657131552110)
XLA Ops:
  0.0 4.5 %collective-permute-start = (f32[16,16,128]{2,1,0:T(8,128)}, f32[16,16,128]{2,1,0:T(8,128)S(1)}, u32[]{:S(2)}, u32[]{:S(2)}) collective-permute-start(f32[16,16,128]{2,1,0:T(8,128)} %ens.1), channel_id=1, source_target_pairs={{1,2},{3,4},{5,6},{7,8},{9,10},{11,12},{13,14},{15,16},{17,18},{19... | collective-permute-start | bytes 393224 | tf_op jit(solution)/shard_map/ppermute | solution.py:272
  4.5 4.9 %collective-permute-start.1 = (f32[16,16,128]{2,1,0:T(8,128)}, f32[16,16,128]{2,1,0:T(8,128)S(1)}, u32[]{:S(2)}, u32[]{:S(2)}) collective-permute-start(f32[16,16,128]{2,1,0:T(8,128)} %ens.1), channel_id=1, source_target_pairs={{0,1},{1,0},{2,3},{3,2},{4,5},{5,4},{6,7},{7,6},{8,9},{9,8},{10,11... | collective-permute-start | bytes 393224 | tf_op jit(solution)/shard_map/ppermute | solution.py:273
  9.5 0.6 copy-done.7
  10.1 0.0 copy-done.5
  10.2 0.0 copy-done.6
  10.2 0.0 copy-done.3
  10.2 0.0 copy-done.4
  10.2 0.7 prepare.1
  10.9 0.1 copy.14.nb
  11.0 0.0 collective-permute-done.outer
  11.0 0.3 copy-done
  11.3 0.2 copy-done.1
  11.4 0.0 copy-done.2
  11.5 2.1 %forecast.1 = f32[8,4,16,128]{3,2,1,0:T(8,128)S(1)} custom-call(s32[16,4]{1,0:T(8,128)S(1)} %copy.14.nb, f32[16,16,128]{2,1,0:T(8,128)S(1)} %copy-done.2, f32[16,16,128]{2,1,0:T(8,128)S(1)} %collective-permute-done.outer, f32[16,16,128]{2,1,0:T(8,128)S(1)} %collective-permute-done.1.inner, bf16[4,128,512]{2,1,0:T(8,128)(2,1)S(1)} %copy-done, ...), custom_call_target="tpu_custom_call" | custom-call | tf_op jit(solution)/shard_map/forecast/pallas_call | solution.py:289
  13.5 14.3 %all_to_all.25.values = f32[8,4,16,128]{3,2,1,0:T(8,128)S(1)} all-to-all(f32[8,4,16,128]{3,2,1,0:T(8,128)S(1)} %forecast.1), channel_id=1, replica_groups=mesh['members'=8,'z'=8,'x'=4,'core'=2] {'members'}, dimensions={0} | all-to-all | bytes 524288 | tf_op jit(solution)/shard_map/all_to_all | solution.py:258
  27.8 0.4 gram.1
  28.2 13.2 %all_to_all.26 = f32[8,7,8,128]{3,2,1,0:T(8,128)S(1)} all-to-all(f32[8,7,8,128]{3,2,1,0:T(8,128)S(1)} %gram.1), channel_id=1, replica_groups=mesh['members'=8,'z'=8,'x'=4,'core'=2] {'x','core'}, dimensions={0} | all-to-all | bytes 458752 | tf_op jit(solution)/shard_map/all_to_all | solution.py:258
  41.4 19.2 %all_to_all.27 = f32[8,7,8,128]{3,2,1,0:T(8,128)S(1)} all-to-all(f32[8,7,8,128]{3,2,1,0:T(8,128)S(1)} %broadcast_in_dim.4), channel_id=1, replica_groups=mesh['members'=8,'z'=8,'x'=4,'core'=2] {'z'}, dimensions={0} | all-to-all | bytes 458752 | tf_op jit(solution)/shard_map/all_to_all | solution.py:258
  60.7 11.4 %all_to_all.28.mine = f32[8,7,8,128]{3,2,1,0:T(8,128)S(1)} all-to-all(f32[8,7,8,128]{3,2,1,0:T(8,128)S(1)} %broadcast_in_dim.5), channel_id=1, replica_groups=mesh['members'=8,'z'=8,'x'=4,'core'=2] {'members'}, dimensions={0} | all-to-all | bytes 458752 | tf_op jit(solution)/shard_map/all_to_all | solution.py:258
  72.1 5.7 %collective-permute-start.2 = (f32[8,7,8,128]{3,2,1,0:T(8,128)S(1)}, f32[8,7,8,128]{3,2,1,0:T(8,128)S(1)}, u32[]{:S(2)}, u32[]{:S(2)}) collective-permute-start(f32[8,7,8,128]{3,2,1,0:T(8,128)S(1)} %all_to_all.28.mine), channel_id=1, source_target_pairs={{0,1},{1,0},{2,3},{3,2},{4,5},{5,4},{6,7},{7,6},{8,9},{9,8},{10,11... | collective-permute-start | bytes 688136 | tf_op jit(solution)/shard_map/ppermute | solution.py:305
  77.8 1.1 %collective-permute-done.2.other = f32[8,7,8,128]{3,2,1,0:T(8,128)S(1)} collective-permute-done((f32[8,7,8,128]{3,2,1,0:T(8,128)S(1)}, f32[8,7,8,128]{3,2,1,0:T(8,128)S(1)}, u32[]{:S(2)}, u32[]{:S(2)}) %collective-permute-start.2) | collective-permute-done | bytes 229408 | tf_op jit(solution)/shard_map/ppermute | solution.py:305
  78.9 5.0 %analysis.1 = f32[8,2,16,128]{3,2,1,0:T(8,128)S(1)} custom-call(f32[8,7,8,128]{3,2,1,0:T(8,128)S(1)} %all_to_all.28.mine, f32[8,7,8,128]{3,2,1,0:T(8,128)S(1)} %collective-permute-done.2.other, f32[8,4,16,128]{3,2,1,0:T(8,128)S(1)} %all_to_all.25.values, f32[4,128]{1,0:T(4,128)S(1)} %copy-done.3), custom_call_target="tpu_custom_call" | custom-call | tf_op jit(solution)/shard_map/analysis/pallas_call | solution.py:307
  83.9 10.8 %all_to_all.29 = f32[8,2,16,128]{3,2,1,0:T(8,128)S(1)} all-to-all(f32[8,2,16,128]{3,2,1,0:T(8,128)S(1)} %analysis.1), channel_id=1, replica_groups=mesh['members'=8,'z'=8,'x'=4,'core'=2] {'members'}, dimensions={0} | all-to-all | bytes 262144 | tf_op jit(solution)/shard_map/all_to_all | solution.py:258
  94.7 0.7 copy.15
  (19 shorter events, 0.1 us)
Async XLA Ops:
  0.0 11.0 %collective-permute-start = (f32[16,16,128]{2,1,0:T(8,128)}, f32[16,16,128]{2,1,0:T(8,128)S(1)}, u32[]{:S(2)}, u32[]{:S(2)}) collective-permute-start(f32[16,16,128]{2,1,0:T(8,128)} %ens.1), channel_id=1, source_target_pairs={{1,2},{3,4},{5,6},{7,8},{9,10},{11,12},{13,14},{15,16},{17,18},{19... | collective-permute-start | bytes 393224 | tf_op jit(solution)/shard_map/ppermute | solution.py:272
  4.5 6.5 %collective-permute-start.1 = (f32[16,16,128]{2,1,0:T(8,128)}, f32[16,16,128]{2,1,0:T(8,128)S(1)}, u32[]{:S(2)}, u32[]{:S(2)}) collective-permute-start(f32[16,16,128]{2,1,0:T(8,128)} %ens.1), channel_id=1, source_target_pairs={{0,1},{1,0},{2,3},{3,2},{4,5},{5,4},{6,7},{7,6},{8,9},{9,8},{10,11... | collective-permute-start | bytes 393224 | tf_op jit(solution)/shard_map/ppermute | solution.py:273
  9.5 0.7 copy-start.7
  9.5 0.7 copy-start.9
  9.5 0.7 copy-start.5
  9.5 0.7 copy-start.6
  9.5 0.7 copy-start.3
  9.5 0.7 copy-start.4
  9.5 0.7 copy-start.8
  10.2 0.7 copy-start.10
  10.2 1.1 %copy-start = (bf16[4,128,512]{2,1,0:T(8,128)(2,1)S(1)}, bf16[4,128,512]{2,1,0:T(8,128)(2,1)}, u32[]{:S(2)}) copy-start(bf16[4,128,512]{2,1,0:T(8,128)(2,1)} %up.1) | copy-start | bytes 1572868
  10.2 1.2 %copy-start.1 = (bf16[4,512,128]{2,1,0:T(8,128)(2,1)S(1)}, bf16[4,512,128]{2,1,0:T(8,128)(2,1)}, u32[]{:S(2)}) copy-start(bf16[4,512,128]{2,1,0:T(8,128)(2,1)} %down.1) | copy-start | bytes 1572868
  10.2 1.2 %copy-start.2 = (f32[16,16,128]{2,1,0:T(8,128)S(1)}, f32[16,16,128]{2,1,0:T(8,128)}, u32[]{:S(2)}) copy-start(f32[16,16,128]{2,1,0:T(8,128)} %ens.1) | copy-start | bytes 393220
  72.1 6.8 %collective-permute-start.2 = (f32[8,7,8,128]{3,2,1,0:T(8,128)S(1)}, f32[8,7,8,128]{3,2,1,0:T(8,128)S(1)}, u32[]{:S(2)}, u32[]{:S(2)}) collective-permute-start(f32[8,7,8,128]{3,2,1,0:T(8,128)S(1)} %all_to_all.28.mine), channel_id=1, source_target_pairs={{0,1},{1,0},{2,3},{3,2},{4,5},{5,4},{6,7},{7,6},{8,9},{9,8},{10,11... | collective-permute-start | bytes 688136 | tf_op jit(solution)/shard_map/ppermute | solution.py:305

commit v10 on v9

--- a/solution.py
+++ b/solution.py
@@ -152,8 +152,9 @@
             middle = jnp.zeros((MD, M), F32)
         p = jnp.where(column > row, first, jnp.where(column < row, second, middle))
         for h in range(2):
-            for x in range(4):
-                packed[2 * x + h, t] = p[8 * h:8 * h + 8]
+            packed[2 * (t // 2) + h, t % 2] = p[8 * h:8 * h + 8]
+    for h in range(2):
+        packed[6 + h, 1] = jnp.zeros((8, M), F32)
 
 
 def analysis_kernel(
@@ -164,9 +165,9 @@
     for g in range(GROUPS):
         for t in range(PACKS):
             at = pl.multiple_of(g * MD + core * 8, 8)
-            packed[t, pl.ds(at, 8), :] = mine[g, t]
+            packed[t, pl.ds(at, 8), :] = mine[4 * g + t // 2, t % 2]
             at = pl.multiple_of(g * MD + 8 - core * 8, 8)
-            packed[t, pl.ds(at, 8), :] = other[g, t]
+            packed[t, pl.ds(at, 8), :] = other[4 * g + t // 2, t % 2]
     i = lax.broadcasted_iota(jnp.int32, (M, M), 0)
     j = lax.broadcasted_iota(jnp.int32, (M, M), 1)
     diagonal = i == j
@@ -295,13 +296,13 @@
     values = swap(values, "members")
     packed = call(
         gram_kernel,
-        shape((8, PACKS, 8, M), F32),
+        shape((8, 2, 8, M), F32),
         [pltpu.VMEM((M, OBS), F32)],
         2, name="gram",
     )(values, at_obs)
     packed = swap(packed, ("x", "core"))
     packed = swap(summed_copies(packed, 8), "z")
-    mine = swap(summed_copies(packed, GROUPS), "members")
+    mine = swap(summed_copies(packed, 4 * GROUPS), ("members", "x"))
     other = lax.ppermute(mine, "core", [(0, 1), (1, 0)])
     size = L * M
     analysis = call(

time: 95.8 us -> 94.1 us (0.982)
  blocking collectives: 68.9 us -> 67.5 us
    all_to_all x5, blocking collectives: 68.9 us -> 67.5 us  [swap(): return lax.all_to_all(x, axes, split_axis=0, concat_axis=0, tiled=True)]
where the time goes in v10:
time: 94.1 us; the launch traced here: 93.7 us
  blocking collectives  67.5 us (72%)
  starting transfers between devices  14.8 us (16%)
  Pallas kernels  8.09 us (9%)
  local copies, waits for them, and re-layouts  1.96 us (2%)
  waiting for transfers between devices  1.15 us (1%)
    all_to_all x5, blocking collectives, swap(): return lax.all_to_all(x, axes, split_axis=0, concat_axis=0, tiled=True)  67.5 us
    ppermute x1, starting transfers between devices, per_device(): other = lax.ppermute(mine, 'core', [(0, 1), (1, 0)])  5.4 us
    pallas_call x1, Pallas kernels, per_device(): call(analysis_kernel, shape((GROUPS, 2, MD, LEV), F32), [pltpu.VMEM((PACK...  4.98 us
    ppermute x1, starting transfers between devices, per_device(): inner = lax.ppermute(ensemble, 'core', [(0, 1), (1, 0)])  4.95 us
    ppermute x1, starting transfers between devices, per_device(): outer = lax.ppermute(ensemble, BANDS, apart + [(b, a) for a, b in apart])  4.5 us
    pallas_call x1, Pallas kernels, per_device(): call(forecast_kernel, shape((GROUPS, 4, MD, LEV), F32), [pltpu.VMEM((C +...  2.06 us
  transfers between devices with their start and end apart: 3, of which 1 were waited for; matrix products, arithmetic and copies ran while one was open for 0% of the time, Pallas kernels for 1%

profile of v10, /device:TPU:1, one launch (start us, length us, event | category | flops | bytes accessed | tf_op | source)
XLA Modules:
  0.0 93.7 jit_solution(4358141405722630674)
XLA Ops:
  0.0 4.5 %collective-permute-start = (f32[16,16,128]{2,1,0:T(8,128)}, f32[16,16,128]{2,1,0:T(8,128)S(1)}, u32[]{:S(2)}, u32[]{:S(2)}) collective-permute-start(f32[16,16,128]{2,1,0:T(8,128)} %ens.1), channel_id=1, source_target_pairs={{1,2},{3,4},{5,6},{7,8},{9,10},{11,12},{13,14},{15,16},{17,18},{19... | collective-permute-start | bytes 393224 | tf_op jit(solution)/shard_map/ppermute | solution.py:273
  4.5 4.9 %collective-permute-start.1 = (f32[16,16,128]{2,1,0:T(8,128)}, f32[16,16,128]{2,1,0:T(8,128)S(1)}, u32[]{:S(2)}, u32[]{:S(2)}) collective-permute-start(f32[16,16,128]{2,1,0:T(8,128)} %ens.1), channel_id=1, source_target_pairs={{0,1},{1,0},{2,3},{3,2},{4,5},{5,4},{6,7},{7,6},{8,9},{9,8},{10,11... | collective-permute-start | bytes 393224 | tf_op jit(solution)/shard_map/ppermute | solution.py:274
  9.5 0.6 copy-done.7
  10.1 0.0 copy-done.5
  10.2 0.0 copy-done.6
  10.2 0.0 copy-done.3
  10.2 0.0 copy-done.4
  10.2 0.7 prepare.1
  10.9 0.1 copy.14.nb
  11.0 0.0 collective-permute-done.outer
  11.0 0.3 copy-done
  11.3 0.2 copy-done.1
  11.4 0.0 copy-done.2
  11.5 2.1 %forecast.1 = f32[8,4,16,128]{3,2,1,0:T(8,128)S(1)} custom-call(s32[16,4]{1,0:T(8,128)S(1)} %copy.14.nb, f32[16,16,128]{2,1,0:T(8,128)S(1)} %copy-done.2, f32[16,16,128]{2,1,0:T(8,128)S(1)} %collective-permute-done.outer, f32[16,16,128]{2,1,0:T(8,128)S(1)} %collective-permute-done.1.inner, bf16[4,128,512]{2,1,0:T(8,128)(2,1)S(1)} %copy-done, ...), custom_call_target="tpu_custom_call" | custom-call | tf_op jit(solution)/shard_map/forecast/pallas_call | solution.py:290
  13.5 14.3 %all_to_all.25.values = f32[8,4,16,128]{3,2,1,0:T(8,128)S(1)} all-to-all(f32[8,4,16,128]{3,2,1,0:T(8,128)S(1)} %forecast.1), channel_id=1, replica_groups=mesh['members'=8,'z'=8,'x'=4,'core'=2] {'members'}, dimensions={0} | all-to-all | bytes 524288 | tf_op jit(solution)/shard_map/all_to_all | solution.py:259
  27.8 0.4 gram.1
  28.2 11.8 %all_to_all.26 = f32[8,2,8,128]{3,2,1,0:T(8,128)S(1)} all-to-all(f32[8,2,8,128]{3,2,1,0:T(8,128)S(1)} %gram.1), channel_id=1, replica_groups=mesh['members'=8,'z'=8,'x'=4,'core'=2] {'x','core'}, dimensions={0} | all-to-all | bytes 131072 | tf_op jit(solution)/shard_map/all_to_all | solution.py:259
  40.0 17.1 %all_to_all.27 = f32[8,2,8,128]{3,2,1,0:T(8,128)S(1)} all-to-all(f32[8,2,8,128]{3,2,1,0:T(8,128)S(1)} %broadcast_in_dim.4), channel_id=1, replica_groups=mesh['members'=8,'z'=8,'x'=4,'core'=2] {'z'}, dimensions={0} | all-to-all | bytes 131072 | tf_op jit(solution)/shard_map/all_to_all | solution.py:259
  57.1 13.6 %all_to_all.28.mine = f32[32,2,8,128]{3,2,1,0:T(8,128)S(1)} all-to-all(f32[32,2,8,128]{3,2,1,0:T(8,128)S(1)} %broadcast_in_dim.5), channel_id=1, replica_groups=mesh['members'=8,'z'=8,'x'=4,'core'=2] {'members','x'}, dimensions={0} | all-to-all | bytes 524288 | tf_op jit(solution)/shard_map/all_to_all | solution.py:259
  70.7 5.4 %collective-permute-start.2 = (f32[32,2,8,128]{3,2,1,0:T(8,128)S(1)}, f32[32,2,8,128]{3,2,1,0:T(8,128)S(1)}, u32[]{:S(2)}, u32[]{:S(2)}) collective-permute-start(f32[32,2,8,128]{3,2,1,0:T(8,128)S(1)} %all_to_all.28.mine), channel_id=1, source_target_pairs={{0,1},{1,0},{2,3},{3,2},{4,5},{5,4},{6,7},{7,6},{8,9},{9,8},{10,11... | collective-permute-start | bytes 786440 | tf_op jit(solution)/shard_map/ppermute | solution.py:306
  76.1 1.1 %collective-permute-done.2.other = f32[32,2,8,128]{3,2,1,0:T(8,128)S(1)} collective-permute-done((f32[32,2,8,128]{3,2,1,0:T(8,128)S(1)}, f32[32,2,8,128]{3,2,1,0:T(8,128)S(1)}, u32[]{:S(2)}, u32[]{:S(2)}) %collective-permute-start.2) | collective-permute-done | bytes 262176 | tf_op jit(solution)/shard_map/ppermute | solution.py:306
  77.3 5.0 %analysis.1 = f32[8,2,16,128]{3,2,1,0:T(8,128)S(1)} custom-call(f32[32,2,8,128]{3,2,1,0:T(8,128)S(1)} %all_to_all.28.mine, f32[32,2,8,128]{3,2,1,0:T(8,128)S(1)} %collective-permute-done.2.other, f32[8,4,16,128]{3,2,1,0:T(8,128)S(1)} %all_to_all.25.values, f32[4,128]{1,0:T(4,128)S(1)} %copy-done.3), custom_call_target="tpu_custom_call" | custom-call | tf_op jit(solution)/shard_map/analysis/pallas_call | solution.py:308
  82.2 10.8 %all_to_all.29 = f32[8,2,16,128]{3,2,1,0:T(8,128)S(1)} all-to-all(f32[8,2,16,128]{3,2,1,0:T(8,128)S(1)} %analysis.1), channel_id=1, replica_groups=mesh['members'=8,'z'=8,'x'=4,'core'=2] {'members'}, dimensions={0} | all-to-all | bytes 262144 | tf_op jit(solution)/shard_map/all_to_all | solution.py:259
  93.0 0.7 copy.15
  (19 shorter events, 0.1 us)
Async XLA Ops:
  0.0 11.0 %collective-permute-start = (f32[16,16,128]{2,1,0:T(8,128)}, f32[16,16,128]{2,1,0:T(8,128)S(1)}, u32[]{:S(2)}, u32[]{:S(2)}) collective-permute-start(f32[16,16,128]{2,1,0:T(8,128)} %ens.1), channel_id=1, source_target_pairs={{1,2},{3,4},{5,6},{7,8},{9,10},{11,12},{13,14},{15,16},{17,18},{19... | collective-permute-start | bytes 393224 | tf_op jit(solution)/shard_map/ppermute | solution.py:273
  4.5 6.5 %collective-permute-start.1 = (f32[16,16,128]{2,1,0:T(8,128)}, f32[16,16,128]{2,1,0:T(8,128)S(1)}, u32[]{:S(2)}, u32[]{:S(2)}) collective-permute-start(f32[16,16,128]{2,1,0:T(8,128)} %ens.1), channel_id=1, source_target_pairs={{0,1},{1,0},{2,3},{3,2},{4,5},{5,4},{6,7},{7,6},{8,9},{9,8},{10,11... | collective-permute-start | bytes 393224 | tf_op jit(solution)/shard_map/ppermute | solution.py:274
  9.5 0.7 copy-start.7
  9.5 0.7 copy-start.9
  9.5 0.7 copy-start.5
  9.5 0.7 copy-start.6
  9.5 0.7 copy-start.3
  9.5 0.7 copy-start.4
  9.5 0.7 copy-start.8
  10.2 0.7 copy-start.10
  10.2 1.1 %copy-start = (bf16[4,128,512]{2,1,0:T(8,128)(2,1)S(1)}, bf16[4,128,512]{2,1,0:T(8,128)(2,1)}, u32[]{:S(2)}) copy-start(bf16[4,128,512]{2,1,0:T(8,128)(2,1)} %up.1) | copy-start | bytes 1572868
  10.2 1.2 %copy-start.1 = (bf16[4,512,128]{2,1,0:T(8,128)(2,1)S(1)}, bf16[4,512,128]{2,1,0:T(8,128)(2,1)}, u32[]{:S(2)}) copy-start(bf16[4,512,128]{2,1,0:T(8,128)(2,1)} %down.1) | copy-start | bytes 1572868
  10.2 1.2 %copy-start.2 = (f32[16,16,128]{2,1,0:T(8,128)S(1)}, f32[16,16,128]{2,1,0:T(8,128)}, u32[]{:S(2)}) copy-start(f32[16,16,128]{2,1,0:T(8,128)} %ens.1) | copy-start | bytes 393220
  70.7 6.6 %collective-permute-start.2 = (f32[32,2,8,128]{3,2,1,0:T(8,128)S(1)}, f32[32,2,8,128]{3,2,1,0:T(8,128)S(1)}, u32[]{:S(2)}, u32[]{:S(2)}) collective-permute-start(f32[32,2,8,128]{3,2,1,0:T(8,128)S(1)} %all_to_all.28.mine), channel_id=1, source_target_pairs={{0,1},{1,0},{2,3},{3,2},{4,5},{5,4},{6,7},{7,6},{8,9},{9,8},{10,11... | collective-permute-start | bytes 786440 | tf_op jit(solution)/shard_map/ppermute | solution.py:306

commit v11 on v10

--- a/solution.py
+++ b/solution.py
@@ -165,9 +165,9 @@
     for g in range(GROUPS):
         for t in range(PACKS):
             at = pl.multiple_of(g * MD + core * 8, 8)
-            packed[t, pl.ds(at, 8), :] = mine[4 * g + t // 2, t % 2]
+            packed[t, pl.ds(at, 8), :] = mine[GROUPS * (t // 2) + g, t % 2]
             at = pl.multiple_of(g * MD + 8 - core * 8, 8)
-            packed[t, pl.ds(at, 8), :] = other[4 * g + t // 2, t % 2]
+            packed[t, pl.ds(at, 8), :] = other[GROUPS * (t // 2) + g, t % 2]
     i = lax.broadcasted_iota(jnp.int32, (M, M), 0)
     j = lax.broadcasted_iota(jnp.int32, (M, M), 1)
     diagonal = i == j
@@ -200,22 +200,33 @@
     size = L * M
     z = zf[...] * inverse_norm
     for step in range(3):
-        high, low = split2(z)
-        zf[0:size] = z
-        zh[0:size] = high
-        zh[size:2 * size] = low
+        if step == 0:
+            high, low = split2(z)
+            zf[...] = z
+            zh[0:size] = high
+            zh[size:2 * size] = low
         vh, vl = split2(v)
         zh[2 * size:2 * size + M] = vh
         zh[2 * size + M:] = vl
-        q = dot(zh[0:size], zh[0:size])
-        fh[...] = (0.25 * q - 1.5 * zf[...]).astype(BF)
+        for r in range(0, size, M):
+            to = r + M
+            q = dot(zh[r:to], zh[0:size])
+            fh[r:to] = (0.25 * q - 1.5 * zf[r:to]).astype(BF)
         if step == 2:
             new = dot(zh[2 * size:], fh[...])
             v = 2.25 * v + (new[:M] + new[M:])
             break
-        new = dot(zh[...], fh[...])
-        z = 2.25 * zf[...] + (new[0:size] + new[size:2 * size])
-        v = 2.25 * v + (new[2 * size:2 * size + M] + new[2 * size + M:])
+        for r in range(0, size, M):
+            to = r + M
+            both = jnp.concatenate([zh[r:to], zh[size + r:size + to]], axis=0)
+            new = dot(both, fh[...])
+            piece = 2.25 * zf[r:to] + (new[:M] + new[M:])
+            zf[r:to] = piece
+            high, low = split2(piece)
+            zh[r:to] = high
+            zh[size + r:size + to] = low
+        new = dot(zh[2 * size:], fh[...])
+        v = 2.25 * v + (new[:M] + new[M:])
     for step in range(2):
         vh, vl = split2(v)
         got = dot(jnp.concatenate([vh, vl], axis=0), zh[0:size])
@@ -302,7 +313,7 @@
     )(values, at_obs)
     packed = swap(packed, ("x", "core"))
     packed = swap(summed_copies(packed, 8), "z")
-    mine = swap(summed_copies(packed, 4 * GROUPS), ("members", "x"))
+    mine = swap(summed_copies(packed, 4 * GROUPS), ("x", "members"))
     other = lax.ppermute(mine, "core", [(0, 1), (1, 0)])
     size = L * M
     analysis = call(

time: 94.1 us -> 93 us (0.988)
  blocking collectives: 67.5 us -> 66.4 us
    all_to_all x5, blocking collectives: 67.5 us -> 66.4 us  [swap(): return lax.all_to_all(x, axes, split_axis=0, concat_axis=0, tiled=True)]
where the time goes in v11:
time: 93 us; the launch traced here: 92.6 us
  blocking collectives  66.4 us (71%)
  starting transfers between devices  15.1 us (16%)
  Pallas kernels  7.82 us (8%)
  local copies, waits for them, and re-layouts  1.96 us (2%)
  waiting for transfers between devices  1.15 us (1%)
    all_to_all x5, blocking collectives, swap(): return lax.all_to_all(x, axes, split_axis=0, concat_axis=0, tiled=True)  66.4 us
    ppermute x1, starting transfers between devices, per_device(): other = lax.ppermute(mine, 'core', [(0, 1), (1, 0)])  5.69 us
    ppermute x1, starting transfers between devices, per_device(): inner = lax.ppermute(ensemble, 'core', [(0, 1), (1, 0)])  4.95 us
    pallas_call x1, Pallas kernels, per_device(): call(analysis_kernel, shape((GROUPS, 2, MD, LEV), F32), [pltpu.VMEM((PACK...  4.72 us
    ppermute x1, starting transfers between devices, per_device(): outer = lax.ppermute(ensemble, BANDS, apart + [(b, a) for a, b in apart])  4.5 us
    pallas_call x1, Pallas kernels, per_device(): call(forecast_kernel, shape((GROUPS, 4, MD, LEV), F32), [pltpu.VMEM((C +...  2.06 us
  transfers between devices with their start and end apart: 3, of which 1 were waited for; matrix products, arithmetic and copies ran while one was open for 0% of the time, Pallas kernels for 1%

profile of v11, /device:TPU:1, one launch (start us, length us, event | category | flops | bytes accessed | tf_op | source)
XLA Modules:
  0.0 92.6 jit_solution(13034763081041766068)
XLA Ops:
  0.0 4.5 %collective-permute-start = (f32[16,16,128]{2,1,0:T(8,128)}, f32[16,16,128]{2,1,0:T(8,128)S(1)}, u32[]{:S(2)}, u32[]{:S(2)}) collective-permute-start(f32[16,16,128]{2,1,0:T(8,128)} %ens.1), channel_id=1, source_target_pairs={{1,2},{3,4},{5,6},{7,8},{9,10},{11,12},{13,14},{15,16},{17,18},{19... | collective-permute-start | bytes 393224 | tf_op jit(solution)/shard_map/ppermute | solution.py:284
  4.5 4.9 %collective-permute-start.1 = (f32[16,16,128]{2,1,0:T(8,128)}, f32[16,16,128]{2,1,0:T(8,128)S(1)}, u32[]{:S(2)}, u32[]{:S(2)}) collective-permute-start(f32[16,16,128]{2,1,0:T(8,128)} %ens.1), channel_id=1, source_target_pairs={{0,1},{1,0},{2,3},{3,2},{4,5},{5,4},{6,7},{7,6},{8,9},{9,8},{10,11... | collective-permute-start | bytes 393224 | tf_op jit(solution)/shard_map/ppermute | solution.py:285
  9.5 0.6 copy-done.7
  10.1 0.0 copy-done.5
  10.2 0.0 copy-done.6
  10.2 0.0 copy-done.3
  10.2 0.0 copy-done.4
  10.2 0.7 prepare.1
  10.9 0.1 copy.14.nb
  11.0 0.0 collective-permute-done.outer
  11.0 0.3 copy-done
  11.3 0.2 copy-done.1
  11.4 0.0 copy-done.2
  11.5 2.1 %forecast.1 = f32[8,4,16,128]{3,2,1,0:T(8,128)S(1)} custom-call(s32[16,4]{1,0:T(8,128)S(1)} %copy.14.nb, f32[16,16,128]{2,1,0:T(8,128)S(1)} %copy-done.2, f32[16,16,128]{2,1,0:T(8,128)S(1)} %collective-permute-done.outer, f32[16,16,128]{2,1,0:T(8,128)S(1)} %collective-permute-done.1.inner, bf16[4,128,512]{2,1,0:T(8,128)(2,1)S(1)} %copy-done, ...), custom_call_target="tpu_custom_call" | custom-call | tf_op jit(solution)/shard_map/forecast/pallas_call | solution.py:301
  13.5 14.3 %all_to_all.25.values = f32[8,4,16,128]{3,2,1,0:T(8,128)S(1)} all-to-all(f32[8,4,16,128]{3,2,1,0:T(8,128)S(1)} %forecast.1), channel_id=1, replica_groups=mesh['members'=8,'z'=8,'x'=4,'core'=2] {'members'}, dimensions={0} | all-to-all | bytes 524288 | tf_op jit(solution)/shard_map/all_to_all | solution.py:270
  27.8 0.4 gram.1
  28.2 11.8 %all_to_all.26 = f32[8,2,8,128]{3,2,1,0:T(8,128)S(1)} all-to-all(f32[8,2,8,128]{3,2,1,0:T(8,128)S(1)} %gram.1), channel_id=1, replica_groups=mesh['members'=8,'z'=8,'x'=4,'core'=2] {'x','core'}, dimensions={0} | all-to-all | bytes 131072 | tf_op jit(solution)/shard_map/all_to_all | solution.py:270
  40.0 17.1 %all_to_all.27 = f32[8,2,8,128]{3,2,1,0:T(8,128)S(1)} all-to-all(f32[8,2,8,128]{3,2,1,0:T(8,128)S(1)} %broadcast_in_dim.4), channel_id=1, replica_groups=mesh['members'=8,'z'=8,'x'=4,'core'=2] {'z'}, dimensions={0} | all-to-all | bytes 131072 | tf_op jit(solution)/shard_map/all_to_all | solution.py:270
  57.1 12.7 %all_to_all.28.mine = f32[32,2,8,128]{3,2,1,0:T(8,128)S(1)} all-to-all(f32[32,2,8,128]{3,2,1,0:T(8,128)S(1)} %broadcast_in_dim.5), channel_id=1, replica_groups=mesh['members'=8,'z'=8,'x'=4,'core'=2] {'x','members'}, dimensions={0} | all-to-all | bytes 524288 | tf_op jit(solution)/shard_map/all_to_all | solution.py:270
  69.8 5.7 %collective-permute-start.2 = (f32[32,2,8,128]{3,2,1,0:T(8,128)S(1)}, f32[32,2,8,128]{3,2,1,0:T(8,128)S(1)}, u32[]{:S(2)}, u32[]{:S(2)}) collective-permute-start(f32[32,2,8,128]{3,2,1,0:T(8,128)S(1)} %all_to_all.28.mine), channel_id=1, source_target_pairs={{0,1},{1,0},{2,3},{3,2},{4,5},{5,4},{6,7},{7,6},{8,9},{9,8},{10,11... | collective-permute-start | bytes 786440 | tf_op jit(solution)/shard_map/ppermute | solution.py:317
  75.5 1.1 %collective-permute-done.2.other = f32[32,2,8,128]{3,2,1,0:T(8,128)S(1)} collective-permute-done((f32[32,2,8,128]{3,2,1,0:T(8,128)S(1)}, f32[32,2,8,128]{3,2,1,0:T(8,128)S(1)}, u32[]{:S(2)}, u32[]{:S(2)}) %collective-permute-start.2) | collective-permute-done | bytes 262176 | tf_op jit(solution)/shard_map/ppermute | solution.py:317
  76.6 4.7 %analysis.1 = f32[8,2,16,128]{3,2,1,0:T(8,128)S(1)} custom-call(f32[32,2,8,128]{3,2,1,0:T(8,128)S(1)} %all_to_all.28.mine, f32[32,2,8,128]{3,2,1,0:T(8,128)S(1)} %collective-permute-done.2.other, f32[8,4,16,128]{3,2,1,0:T(8,128)S(1)} %all_to_all.25.values, f32[4,128]{1,0:T(4,128)S(1)} %copy-done.3), custom_call_target="tpu_custom_call" | custom-call | tf_op jit(solution)/shard_map/analysis/pallas_call | solution.py:319
  81.4 10.6 %all_to_all.29 = f32[8,2,16,128]{3,2,1,0:T(8,128)S(1)} all-to-all(f32[8,2,16,128]{3,2,1,0:T(8,128)S(1)} %analysis.1), channel_id=1, replica_groups=mesh['members'=8,'z'=8,'x'=4,'core'=2] {'members'}, dimensions={0} | all-to-all | bytes 262144 | tf_op jit(solution)/shard_map/all_to_all | solution.py:270
  91.9 0.7 copy.15
  (19 shorter events, 0.1 us)
Async XLA Ops:
  0.0 11.0 %collective-permute-start = (f32[16,16,128]{2,1,0:T(8,128)}, f32[16,16,128]{2,1,0:T(8,128)S(1)}, u32[]{:S(2)}, u32[]{:S(2)}) collective-permute-start(f32[16,16,128]{2,1,0:T(8,128)} %ens.1), channel_id=1, source_target_pairs={{1,2},{3,4},{5,6},{7,8},{9,10},{11,12},{13,14},{15,16},{17,18},{19... | collective-permute-start | bytes 393224 | tf_op jit(solution)/shard_map/ppermute | solution.py:284
  4.5 6.5 %collective-permute-start.1 = (f32[16,16,128]{2,1,0:T(8,128)}, f32[16,16,128]{2,1,0:T(8,128)S(1)}, u32[]{:S(2)}, u32[]{:S(2)}) collective-permute-start(f32[16,16,128]{2,1,0:T(8,128)} %ens.1), channel_id=1, source_target_pairs={{0,1},{1,0},{2,3},{3,2},{4,5},{5,4},{6,7},{7,6},{8,9},{9,8},{10,11... | collective-permute-start | bytes 393224 | tf_op jit(solution)/shard_map/ppermute | solution.py:285
  9.5 0.7 copy-start.7
  9.5 0.7 copy-start.9
  9.5 0.7 copy-start.5
  9.5 0.7 copy-start.6
  9.5 0.7 copy-start.3
  9.5 0.7 copy-start.4
  9.5 0.7 copy-start.8
  10.2 0.7 copy-start.10
  10.2 1.1 %copy-start = (bf16[4,128,512]{2,1,0:T(8,128)(2,1)S(1)}, bf16[4,128,512]{2,1,0:T(8,128)(2,1)}, u32[]{:S(2)}) copy-start(bf16[4,128,512]{2,1,0:T(8,128)(2,1)} %up.1) | copy-start | bytes 1572868
  10.2 1.2 %copy-start.1 = (bf16[4,512,128]{2,1,0:T(8,128)(2,1)S(1)}, bf16[4,512,128]{2,1,0:T(8,128)(2,1)}, u32[]{:S(2)}) copy-start(bf16[4,512,128]{2,1,0:T(8,128)(2,1)} %down.1) | copy-start | bytes 1572868
  10.2 1.2 %copy-start.2 = (f32[16,16,128]{2,1,0:T(8,128)S(1)}, f32[16,16,128]{2,1,0:T(8,128)}, u32[]{:S(2)}) copy-start(f32[16,16,128]{2,1,0:T(8,128)} %ens.1) | copy-start | bytes 393220
  69.8 6.8 %collective-permute-start.2 = (f32[32,2,8,128]{3,2,1,0:T(8,128)S(1)}, f32[32,2,8,128]{3,2,1,0:T(8,128)S(1)}, u32[]{:S(2)}, u32[]{:S(2)}) collective-permute-start(f32[32,2,8,128]{3,2,1,0:T(8,128)S(1)} %all_to_all.28.mine), channel_id=1, source_target_pairs={{0,1},{1,0},{2,3},{3,2},{4,5},{5,4},{6,7},{7,6},{8,9},{9,8},{10,11... | collective-permute-start | bytes 786440 | tf_op jit(solution)/shard_map/ppermute | solution.py:317

commit v12 on v11

--- a/solution.py
+++ b/solution.py
@@ -152,9 +152,9 @@
             middle = jnp.zeros((MD, M), F32)
         p = jnp.where(column > row, first, jnp.where(column < row, second, middle))
         for h in range(2):
-            packed[2 * (t // 2) + h, t % 2] = p[8 * h:8 * h + 8]
+            packed[4 * h + t // 2, t % 2] = p[8 * h:8 * h + 8]
     for h in range(2):
-        packed[6 + h, 1] = jnp.zeros((8, M), F32)
+        packed[4 * h + 3, 1] = jnp.zeros((8, M), F32)
 
 
 def analysis_kernel(
@@ -311,7 +311,7 @@
         [pltpu.VMEM((M, OBS), F32)],
         2, name="gram",
     )(values, at_obs)
-    packed = swap(packed, ("x", "core"))
+    packed = swap(packed, ("core", "x"))
     packed = swap(summed_copies(packed, 8), "z")
     mine = swap(summed_copies(packed, 4 * GROUPS), ("x", "members"))
     other = lax.ppermute(mine, "core", [(0, 1), (1, 0)])

time: 93 us -> 93.2 us (level)
  no operation moved by 1% of the time
where the time goes in v12:
time: 93.2 us; the launch traced here: 92.8 us
  blocking collectives  66.7 us (72%)
  starting transfers between devices  14.9 us (16%)
  Pallas kernels  7.83 us (8%)
  local copies, waits for them, and re-layouts  1.96 us (2%)
  waiting for transfers between devices  1.15 us (1%)
    all_to_all x5, blocking collectives, swap(): return lax.all_to_all(x, axes, split_axis=0, concat_axis=0, tiled=True)  66.7 us
    ppermute x1, starting transfers between devices, per_device(): other = lax.ppermute(mine, 'core', [(0, 1), (1, 0)])  5.5 us
    ppermute x1, starting transfers between devices, per_device(): inner = lax.ppermute(ensemble, 'core', [(0, 1), (1, 0)])  4.95 us
    pallas_call x1, Pallas kernels, per_device(): call(analysis_kernel, shape((GROUPS, 2, MD, LEV), F32), [pltpu.VMEM((PACK...  4.73 us
    ppermute x1, starting transfers between devices, per_device(): outer = lax.ppermute(ensemble, BANDS, apart + [(b, a) for a, b in apart])  4.5 us
    pallas_call x1, Pallas kernels, per_device(): call(forecast_kernel, shape((GROUPS, 4, MD, LEV), F32), [pltpu.VMEM((C +...  2.06 us
  transfers between devices with their start and end apart: 3, of which 1 were waited for; matrix products, arithmetic and copies ran while one was open for 0% of the time, Pallas kernels for 1%

profile of v12, /device:TPU:1, one launch (start us, length us, event | category | flops | bytes accessed | tf_op | source)
XLA Modules:
  0.0 92.8 jit_solution(14019678890375013632)
XLA Ops:
  0.0 4.5 %collective-permute-start = (f32[16,16,128]{2,1,0:T(8,128)}, f32[16,16,128]{2,1,0:T(8,128)S(1)}, u32[]{:S(2)}, u32[]{:S(2)}) collective-permute-start(f32[16,16,128]{2,1,0:T(8,128)} %ens.1), channel_id=1, source_target_pairs={{1,2},{3,4},{5,6},{7,8},{9,10},{11,12},{13,14},{15,16},{17,18},{19... | collective-permute-start | bytes 393224 | tf_op jit(solution)/shard_map/ppermute | solution.py:284
  4.5 4.9 %collective-permute-start.1 = (f32[16,16,128]{2,1,0:T(8,128)}, f32[16,16,128]{2,1,0:T(8,128)S(1)}, u32[]{:S(2)}, u32[]{:S(2)}) collective-permute-start(f32[16,16,128]{2,1,0:T(8,128)} %ens.1), channel_id=1, source_target_pairs={{0,1},{1,0},{2,3},{3,2},{4,5},{5,4},{6,7},{7,6},{8,9},{9,8},{10,11... | collective-permute-start | bytes 393224 | tf_op jit(solution)/shard_map/ppermute | solution.py:285
  9.5 0.6 copy-done.7
  10.1 0.0 copy-done.5
  10.2 0.0 copy-done.6
  10.2 0.0 copy-done.3
  10.2 0.0 copy-done.4
  10.2 0.7 prepare.1
  10.9 0.1 copy.14.nb
  11.0 0.0 collective-permute-done.outer
  11.0 0.3 copy-done
  11.3 0.2 copy-done.1
  11.4 0.0 copy-done.2
  11.5 2.1 %forecast.1 = f32[8,4,16,128]{3,2,1,0:T(8,128)S(1)} custom-call(s32[16,4]{1,0:T(8,128)S(1)} %copy.14.nb, f32[16,16,128]{2,1,0:T(8,128)S(1)} %copy-done.2, f32[16,16,128]{2,1,0:T(8,128)S(1)} %collective-permute-done.outer, f32[16,16,128]{2,1,0:T(8,128)S(1)} %collective-permute-done.1.inner, bf16[4,128,512]{2,1,0:T(8,128)(2,1)S(1)} %copy-done, ...), custom_call_target="tpu_custom_call" | custom-call | tf_op jit(solution)/shard_map/forecast/pallas_call | solution.py:301
  13.5 14.3 %all_to_all.25.values = f32[8,4,16,128]{3,2,1,0:T(8,128)S(1)} all-to-all(f32[8,4,16,128]{3,2,1,0:T(8,128)S(1)} %forecast.1), channel_id=1, replica_groups=mesh['members'=8,'z'=8,'x'=4,'core'=2] {'members'}, dimensions={0} | all-to-all | bytes 524288 | tf_op jit(solution)/shard_map/all_to_all | solution.py:270
  27.8 0.4 gram.1
  28.2 12.0 %all_to_all.26 = f32[8,2,8,128]{3,2,1,0:T(8,128)S(1)} all-to-all(f32[8,2,8,128]{3,2,1,0:T(8,128)S(1)} %gram.1), channel_id=1, replica_groups=mesh['members'=8,'z'=8,'x'=4,'core'=2] {'core','x'}, dimensions={0} | all-to-all | bytes 131072 | tf_op jit(solution)/shard_map/all_to_all | solution.py:270
  40.2 17.1 %all_to_all.27 = f32[8,2,8,128]{3,2,1,0:T(8,128)S(1)} all-to-all(f32[8,2,8,128]{3,2,1,0:T(8,128)S(1)} %broadcast_in_dim.4), channel_id=1, replica_groups=mesh['members'=8,'z'=8,'x'=4,'core'=2] {'z'}, dimensions={0} | all-to-all | bytes 131072 | tf_op jit(solution)/shard_map/all_to_all | solution.py:270
  57.3 12.6 %all_to_all.28.mine = f32[32,2,8,128]{3,2,1,0:T(8,128)S(1)} all-to-all(f32[32,2,8,128]{3,2,1,0:T(8,128)S(1)} %broadcast_in_dim.5), channel_id=1, replica_groups=mesh['members'=8,'z'=8,'x'=4,'core'=2] {'x','members'}, dimensions={0} | all-to-all | bytes 524288 | tf_op jit(solution)/shard_map/all_to_all | solution.py:270
  69.9 5.5 %collective-permute-start.2 = (f32[32,2,8,128]{3,2,1,0:T(8,128)S(1)}, f32[32,2,8,128]{3,2,1,0:T(8,128)S(1)}, u32[]{:S(2)}, u32[]{:S(2)}) collective-permute-start(f32[32,2,8,128]{3,2,1,0:T(8,128)S(1)} %all_to_all.28.mine), channel_id=1, source_target_pairs={{0,1},{1,0},{2,3},{3,2},{4,5},{5,4},{6,7},{7,6},{8,9},{9,8},{10,11... | collective-permute-start | bytes 786440 | tf_op jit(solution)/shard_map/ppermute | solution.py:317
  75.4 1.1 %collective-permute-done.2.other = f32[32,2,8,128]{3,2,1,0:T(8,128)S(1)} collective-permute-done((f32[32,2,8,128]{3,2,1,0:T(8,128)S(1)}, f32[32,2,8,128]{3,2,1,0:T(8,128)S(1)}, u32[]{:S(2)}, u32[]{:S(2)}) %collective-permute-start.2) | collective-permute-done | bytes 262176 | tf_op jit(solution)/shard_map/ppermute | solution.py:317
  76.6 4.7 %analysis.1 = f32[8,2,16,128]{3,2,1,0:T(8,128)S(1)} custom-call(f32[32,2,8,128]{3,2,1,0:T(8,128)S(1)} %all_to_all.28.mine, f32[32,2,8,128]{3,2,1,0:T(8,128)S(1)} %collective-permute-done.2.other, f32[8,4,16,128]{3,2,1,0:T(8,128)S(1)} %all_to_all.25.values, f32[4,128]{1,0:T(4,128)S(1)} %copy-done.3), custom_call_target="tpu_custom_call" | custom-call | tf_op jit(solution)/shard_map/analysis/pallas_call | solution.py:319
  81.3 10.8 %all_to_all.29 = f32[8,2,16,128]{3,2,1,0:T(8,128)S(1)} all-to-all(f32[8,2,16,128]{3,2,1,0:T(8,128)S(1)} %analysis.1), channel_id=1, replica_groups=mesh['members'=8,'z'=8,'x'=4,'core'=2] {'members'}, dimensions={0} | all-to-all | bytes 262144 | tf_op jit(solution)/shard_map/all_to_all | solution.py:270
  92.1 0.7 copy.15
  (19 shorter events, 0.1 us)
Async XLA Ops:
  0.0 11.0 %collective-permute-start = (f32[16,16,128]{2,1,0:T(8,128)}, f32[16,16,128]{2,1,0:T(8,128)S(1)}, u32[]{:S(2)}, u32[]{:S(2)}) collective-permute-start(f32[16,16,128]{2,1,0:T(8,128)} %ens.1), channel_id=1, source_target_pairs={{1,2},{3,4},{5,6},{7,8},{9,10},{11,12},{13,14},{15,16},{17,18},{19... | collective-permute-start | bytes 393224 | tf_op jit(solution)/shard_map/ppermute | solution.py:284
  4.5 6.5 %collective-permute-start.1 = (f32[16,16,128]{2,1,0:T(8,128)}, f32[16,16,128]{2,1,0:T(8,128)S(1)}, u32[]{:S(2)}, u32[]{:S(2)}) collective-permute-start(f32[16,16,128]{2,1,0:T(8,128)} %ens.1), channel_id=1, source_target_pairs={{0,1},{1,0},{2,3},{3,2},{4,5},{5,4},{6,7},{7,6},{8,9},{9,8},{10,11... | collective-permute-start | bytes 393224 | tf_op jit(solution)/shard_map/ppermute | solution.py:285
  9.5 0.7 copy-start.7
  9.5 0.7 copy-start.9
  9.5 0.7 copy-start.5
  9.5 0.7 copy-start.6
  9.5 0.7 copy-start.3
  9.5 0.7 copy-start.4
  9.5 0.7 copy-start.8
  10.2 0.7 copy-start.10
  10.2 1.1 %copy-start = (bf16[4,128,512]{2,1,0:T(8,128)(2,1)S(1)}, bf16[4,128,512]{2,1,0:T(8,128)(2,1)}, u32[]{:S(2)}) copy-start(bf16[4,128,512]{2,1,0:T(8,128)(2,1)} %up.1) | copy-start | bytes 1572868
  10.2 1.2 %copy-start.1 = (bf16[4,512,128]{2,1,0:T(8,128)(2,1)S(1)}, bf16[4,512,128]{2,1,0:T(8,128)(2,1)}, u32[]{:S(2)}) copy-start(bf16[4,512,128]{2,1,0:T(8,128)(2,1)} %down.1) | copy-start | bytes 1572868
  10.2 1.2 %copy-start.2 = (f32[16,16,128]{2,1,0:T(8,128)S(1)}, f32[16,16,128]{2,1,0:T(8,128)}, u32[]{:S(2)}) copy-start(f32[16,16,128]{2,1,0:T(8,128)} %ens.1) | copy-start | bytes 393220
  69.9 6.7 %collective-permute-start.2 = (f32[32,2,8,128]{3,2,1,0:T(8,128)S(1)}, f32[32,2,8,128]{3,2,1,0:T(8,128)S(1)}, u32[]{:S(2)}, u32[]{:S(2)}) collective-permute-start(f32[32,2,8,128]{3,2,1,0:T(8,128)S(1)} %all_to_all.28.mine), channel_id=1, source_target_pairs={{0,1},{1,0},{2,3},{3,2},{4,5},{5,4},{6,7},{7,6},{8,9},{9,8},{10,11... | collective-permute-start | bytes 786440 | tf_op jit(solution)/shard_map/ppermute | solution.py:317

commit v13 on v11

--- a/solution.py
+++ b/solution.py
@@ -94,16 +94,20 @@
     flat = jnp.concatenate(rows, axis=0)
     inv_rms = lax.rsqrt(jnp.mean(flat * flat, axis=1, keepdims=True) + 1e-05)
     normed = (flat * inv_rms * rows_in[L + 2:L + 3, 0:LEV]).astype(BF)
-    which = which_ref[...]
-    which4 = jnp.concatenate([which] * (FF // LEV), axis=1)
-    pre = dot(normed, up[0])
-    for e in range(1, E):
-        pre = jnp.where(which4 == e, dot(normed, up[e]), pre)
-    hidden = pre / (1.0 + jnp.exp(-pre))
-    tendency = None
-    for e in range(E):
-        part = dot(jnp.where(which4 == e, hidden, 0.0).astype(BF), down[e])
-        tendency = part if tendency is None else tendency + part
+    pieces = []
+    for r in range(0, C * MD, M):
+        rows_here = normed[r:r + M]
+        which4 = jnp.concatenate([which_ref[r:r + M]] * (FF // LEV), axis=1)
+        pre = dot(rows_here, up[0])
+        for e in range(1, E):
+            pre = jnp.where(which4 == e, dot(rows_here, up[e]), pre)
+        hidden = pre / (1.0 + jnp.exp(-pre))
+        piece = None
+        for e in range(E):
+            part = dot(jnp.where(which4 == e, hidden, 0.0).astype(BF), down[e])
+            piece = part if piece is None else piece + part
+        pieces.append(piece)
+    tendency = jnp.concatenate(pieces, axis=0)
     out = flat + tendency
     picked = None
     for part in split3(out):

time: 93 us -> 93 us (level)
  no operation moved by 1% of the time
where the time goes in v13:
time: 93 us; the launch traced here: 92.7 us
  blocking collectives  66.4 us (71%)
  starting transfers between devices  15.1 us (16%)
  Pallas kernels  7.83 us (8%)
  local copies, waits for them, and re-layouts  1.96 us (2%)
  waiting for transfers between devices  1.15 us (1%)
    all_to_all x5, blocking collectives, swap(): return lax.all_to_all(x, axes, split_axis=0, concat_axis=0, tiled=True)  66.4 us
    ppermute x1, starting transfers between devices, per_device(): other = lax.ppermute(mine, 'core', [(0, 1), (1, 0)])  5.69 us
    ppermute x1, starting transfers between devices, per_device(): inner = lax.ppermute(ensemble, 'core', [(0, 1), (1, 0)])  4.95 us
    pallas_call x1, Pallas kernels, per_device(): call(analysis_kernel, shape((GROUPS, 2, MD, LEV), F32), [pltpu.VMEM((PACK...  4.73 us
    ppermute x1, starting transfers between devices, per_device(): outer = lax.ppermute(ensemble, BANDS, apart + [(b, a) for a, b in apart])  4.5 us
    pallas_call x1, Pallas kernels, per_device(): call(forecast_kernel, shape((GROUPS, 4, MD, LEV), F32), [pltpu.VMEM((C +...  2.06 us
  transfers between devices with their start and end apart: 3, of which 1 were waited for; matrix products, arithmetic and copies ran while one was open for 0% of the time, Pallas kernels for 1%

profile of v13, /device:TPU:1, one launch (start us, length us, event | category | flops | bytes accessed | tf_op | source)
XLA Modules:
  0.0 92.7 jit_solution(17449364031242306430)
XLA Ops:
  0.0 4.5 %collective-permute-start = (f32[16,16,128]{2,1,0:T(8,128)}, f32[16,16,128]{2,1,0:T(8,128)S(1)}, u32[]{:S(2)}, u32[]{:S(2)}) collective-permute-start(f32[16,16,128]{2,1,0:T(8,128)} %ens.1), channel_id=1, source_target_pairs={{1,2},{3,4},{5,6},{7,8},{9,10},{11,12},{13,14},{15,16},{17,18},{19... | collective-permute-start | bytes 393224 | tf_op jit(solution)/shard_map/ppermute | solution.py:288
  4.5 4.9 %collective-permute-start.1 = (f32[16,16,128]{2,1,0:T(8,128)}, f32[16,16,128]{2,1,0:T(8,128)S(1)}, u32[]{:S(2)}, u32[]{:S(2)}) collective-permute-start(f32[16,16,128]{2,1,0:T(8,128)} %ens.1), channel_id=1, source_target_pairs={{0,1},{1,0},{2,3},{3,2},{4,5},{5,4},{6,7},{7,6},{8,9},{9,8},{10,11... | collective-permute-start | bytes 393224 | tf_op jit(solution)/shard_map/ppermute | solution.py:289
  9.5 0.6 copy-done.7
  10.1 0.0 copy-done.5
  10.2 0.0 copy-done.6
  10.2 0.0 copy-done.3
  10.2 0.0 copy-done.4
  10.2 0.7 prepare.1
  10.9 0.1 copy.14.nb
  11.0 0.0 collective-permute-done.outer
  11.0 0.3 copy-done
  11.3 0.2 copy-done.1
  11.4 0.0 copy-done.2
  11.5 2.1 %forecast.1 = f32[8,4,16,128]{3,2,1,0:T(8,128)S(1)} custom-call(s32[16,4]{1,0:T(8,128)S(1)} %copy.14.nb, f32[16,16,128]{2,1,0:T(8,128)S(1)} %copy-done.2, f32[16,16,128]{2,1,0:T(8,128)S(1)} %collective-permute-done.outer, f32[16,16,128]{2,1,0:T(8,128)S(1)} %collective-permute-done.1.inner, bf16[4,128,512]{2,1,0:T(8,128)(2,1)S(1)} %copy-done, ...), custom_call_target="tpu_custom_call" | custom-call | tf_op jit(solution)/shard_map/forecast/pallas_call | solution.py:305
  13.5 14.3 %all_to_all.25.values = f32[8,4,16,128]{3,2,1,0:T(8,128)S(1)} all-to-all(f32[8,4,16,128]{3,2,1,0:T(8,128)S(1)} %forecast.1), channel_id=1, replica_groups=mesh['members'=8,'z'=8,'x'=4,'core'=2] {'members'}, dimensions={0} | all-to-all | bytes 524288 | tf_op jit(solution)/shard_map/all_to_all | solution.py:274
  27.8 0.4 gram.1
  28.2 11.8 %all_to_all.26 = f32[8,2,8,128]{3,2,1,0:T(8,128)S(1)} all-to-all(f32[8,2,8,128]{3,2,1,0:T(8,128)S(1)} %gram.1), channel_id=1, replica_groups=mesh['members'=8,'z'=8,'x'=4,'core'=2] {'x','core'}, dimensions={0} | all-to-all | bytes 131072 | tf_op jit(solution)/shard_map/all_to_all | solution.py:274
  40.0 17.1 %all_to_all.27 = f32[8,2,8,128]{3,2,1,0:T(8,128)S(1)} all-to-all(f32[8,2,8,128]{3,2,1,0:T(8,128)S(1)} %broadcast_in_dim.4), channel_id=1, replica_groups=mesh['members'=8,'z'=8,'x'=4,'core'=2] {'z'}, dimensions={0} | all-to-all | bytes 131072 | tf_op jit(solution)/shard_map/all_to_all | solution.py:274
  57.1 12.7 %all_to_all.28.mine = f32[32,2,8,128]{3,2,1,0:T(8,128)S(1)} all-to-all(f32[32,2,8,128]{3,2,1,0:T(8,128)S(1)} %broadcast_in_dim.5), channel_id=1, replica_groups=mesh['members'=8,'z'=8,'x'=4,'core'=2] {'x','members'}, dimensions={0} | all-to-all | bytes 524288 | tf_op jit(solution)/shard_map/all_to_all | solution.py:274
  69.8 5.7 %collective-permute-start.2 = (f32[32,2,8,128]{3,2,1,0:T(8,128)S(1)}, f32[32,2,8,128]{3,2,1,0:T(8,128)S(1)}, u32[]{:S(2)}, u32[]{:S(2)}) collective-permute-start(f32[32,2,8,128]{3,2,1,0:T(8,128)S(1)} %all_to_all.28.mine), channel_id=1, source_target_pairs={{0,1},{1,0},{2,3},{3,2},{4,5},{5,4},{6,7},{7,6},{8,9},{9,8},{10,11... | collective-permute-start | bytes 786440 | tf_op jit(solution)/shard_map/ppermute | solution.py:321
  75.5 1.1 %collective-permute-done.2.other = f32[32,2,8,128]{3,2,1,0:T(8,128)S(1)} collective-permute-done((f32[32,2,8,128]{3,2,1,0:T(8,128)S(1)}, f32[32,2,8,128]{3,2,1,0:T(8,128)S(1)}, u32[]{:S(2)}, u32[]{:S(2)}) %collective-permute-start.2) | collective-permute-done | bytes 262176 | tf_op jit(solution)/shard_map/ppermute | solution.py:321
  76.6 4.7 %analysis.1 = f32[8,2,16,128]{3,2,1,0:T(8,128)S(1)} custom-call(f32[32,2,8,128]{3,2,1,0:T(8,128)S(1)} %all_to_all.28.mine, f32[32,2,8,128]{3,2,1,0:T(8,128)S(1)} %collective-permute-done.2.other, f32[8,4,16,128]{3,2,1,0:T(8,128)S(1)} %all_to_all.25.values, f32[4,128]{1,0:T(4,128)S(1)} %copy-done.3), custom_call_target="tpu_custom_call" | custom-call | tf_op jit(solution)/shard_map/analysis/pallas_call | solution.py:323
  81.4 10.6 %all_to_all.29 = f32[8,2,16,128]{3,2,1,0:T(8,128)S(1)} all-to-all(f32[8,2,16,128]{3,2,1,0:T(8,128)S(1)} %analysis.1), channel_id=1, replica_groups=mesh['members'=8,'z'=8,'x'=4,'core'=2] {'members'}, dimensions={0} | all-to-all | bytes 262144 | tf_op jit(solution)/shard_map/all_to_all | solution.py:274
  92.0 0.7 copy.15
  (19 shorter events, 0.1 us)
Async XLA Ops:
  0.0 11.0 %collective-permute-start = (f32[16,16,128]{2,1,0:T(8,128)}, f32[16,16,128]{2,1,0:T(8,128)S(1)}, u32[]{:S(2)}, u32[]{:S(2)}) collective-permute-start(f32[16,16,128]{2,1,0:T(8,128)} %ens.1), channel_id=1, source_target_pairs={{1,2},{3,4},{5,6},{7,8},{9,10},{11,12},{13,14},{15,16},{17,18},{19... | collective-permute-start | bytes 393224 | tf_op jit(solution)/shard_map/ppermute | solution.py:288
  4.5 6.5 %collective-permute-start.1 = (f32[16,16,128]{2,1,0:T(8,128)}, f32[16,16,128]{2,1,0:T(8,128)S(1)}, u32[]{:S(2)}, u32[]{:S(2)}) collective-permute-start(f32[16,16,128]{2,1,0:T(8,128)} %ens.1), channel_id=1, source_target_pairs={{0,1},{1,0},{2,3},{3,2},{4,5},{5,4},{6,7},{7,6},{8,9},{9,8},{10,11... | collective-permute-start | bytes 393224 | tf_op jit(solution)/shard_map/ppermute | solution.py:289
  9.5 0.7 copy-start.7
  9.5 0.7 copy-start.9
  9.5 0.7 copy-start.5
  9.5 0.7 copy-start.6
  9.5 0.7 copy-start.3
  9.5 0.7 copy-start.4
  9.5 0.7 copy-start.8
  10.2 0.7 copy-start.10
  10.2 1.1 %copy-start = (bf16[4,128,512]{2,1,0:T(8,128)(2,1)S(1)}, bf16[4,128,512]{2,1,0:T(8,128)(2,1)}, u32[]{:S(2)}) copy-start(bf16[4,128,512]{2,1,0:T(8,128)(2,1)} %up.1) | copy-start | bytes 1572868
  10.2 1.2 %copy-start.1 = (bf16[4,512,128]{2,1,0:T(8,128)(2,1)S(1)}, bf16[4,512,128]{2,1,0:T(8,128)(2,1)}, u32[]{:S(2)}) copy-start(bf16[4,512,128]{2,1,0:T(8,128)(2,1)} %down.1) | copy-start | bytes 1572868
  10.2 1.2 %copy-start.2 = (f32[16,16,128]{2,1,0:T(8,128)S(1)}, f32[16,16,128]{2,1,0:T(8,128)}, u32[]{:S(2)}) copy-start(f32[16,16,128]{2,1,0:T(8,128)} %ens.1) | copy-start | bytes 393220
  69.8 6.8 %collective-permute-start.2 = (f32[32,2,8,128]{3,2,1,0:T(8,128)S(1)}, f32[32,2,8,128]{3,2,1,0:T(8,128)S(1)}, u32[]{:S(2)}, u32[]{:S(2)}) collective-permute-start(f32[32,2,8,128]{3,2,1,0:T(8,128)S(1)} %all_to_all.28.mine), channel_id=1, source_target_pairs={{0,1},{1,0},{2,3},{3,2},{4,5},{5,4},{6,7},{7,6},{8,9},{9,8},{10,11... | collective-permute-start | bytes 786440 | tf_op jit(solution)/shard_map/ppermute | solution.py:321
